TPU v7x, 32 devices: a whole 2x2x4 slice. The times are simulated.
32 devices in a mesh: groups: 2 (over y), rec: 4 (over z), lig: 2 (over x), fft: 2 (over core).
Axes of the slice: x: 2, y: 2, z: 4, core: 2. Of those that a mesh axis runs over, the one named last changes fastest.
Arguments:
- receptor_occupancy: int32 [16, 4, 64, 4096], P(('groups', 'rec', 'lig'), None, 'fft'), parts along dimension 0, may hold values from 0 to 3
- ligand_occupancy: int32 [16, 4, 64, 4096], P(('groups', 'rec', 'lig'), None, 'fft'), parts along dimension 0, may hold values from 0 to 3
- rot_index: int32 [16], P(('groups', 'rec', 'lig')), parts along dimension 0, may hold values from 0 to 3
- receptor_extent: int32 [16], P(('groups', 'rec', 'lig')), parts along dimension 0, may hold values from 16 to 64, as said below
- channel_weight: float32 [4], replicated, may hold values from -1 to 2
Outputs:
- plane_top: float32 [16, 3, 2, 64], P(('groups', 'rec', 'lig'), None, None, 'fft'), parts along dimension 0
There are 2 independent parts, one for each index of `groups`. A program takes and returns all parts, laid end to end along the dimension named above; an argument that names none is the same for every part. Nothing has to cross between parts.
Inputs may be any that keep to these rules, and one draw needn't show every extreme that they name: `rot_index`: quarter turns. `receptor_extent`: some receptor has extent 64.
All inputs are finite; a program needn't handle non-finite values.
Results may differ from a plain program's by a relative error of at most 0.0062.
Values may be sent and summed in bfloat16 or wider, within the bound.
No kernel may reach another device: no remote copies, remote signals or barrier semaphores. Data moves between devices by JAX's collectives and lax.ppermute only.
A program may use at most 128 MiB of HBM per device.

v0:
```python
from functools import partial
import math

import jax
import jax.numpy as jnp
import ml_dtypes
import numpy as np
from jax import lax
from jax.experimental import pallas as pl
from jax.experimental.pallas import tpu as pltpu
from jax.sharding import PartitionSpec as P

REC_STEPS = 3
LIG_STEPS = 2
MIB = 1024 * 1024
F32 = jnp.float32
BF16 = jnp.bfloat16


def trig(cells):
    phases = np.arange(cells)[:, None] * np.arange(cells)[None, :] % cells
    angles = phases * (2.0 * math.pi / cells)
    pair = []
    for table in (np.cos(angles), np.sin(angles)):
        table = np.where(np.abs(table) < 1e-9, 0.0, table)
        pair.append(table.astype(np.float32).astype(ml_dtypes.bfloat16).astype(np.float32))
    return pair


def complex_rows(real, imag):
    return np.block([[real, -imag], [imag, real]])


def build_tables(cells, channels, slab, cores):
    cosine, sine = trig(cells)
    half = cells // 2
    own = half // cores
    sign = np.where(np.arange(cells) % 2 == 0, 1.0, -1.0).astype(np.float32)
    tables = {}

    def half_rows(core):
        order = [(core + turn) % cores * own + j for turn in range(cores) for j in range(own)]
        real = cosine[order].copy()
        imag = -sine[order]
        imag[order.index(0)] = sign
        return np.concatenate([real, imag], axis=0)

    def half_mix(core):
        order = [(core + turn) % cores * own + j for turn in range(cores) for j in range(own)]
        top = np.concatenate([cosine[order], sine[order]], axis=1)
        low = np.concatenate([-sine[order], cosine[order]], axis=1)
        at = order.index(0)
        one = np.ones(cells, np.float32)
        top[at] = np.concatenate([one, -sign])
        low[at] = np.concatenate([sign, one])
        return np.concatenate([top, low], axis=0)

    def flips(table, width):
        blocks = table.reshape(table.shape[0], -1, width)
        return np.stack([table, blocks[:, :, ::-1].reshape(table.shape)])

    two = np.eye(2, dtype=np.float32)
    full_rows = np.concatenate([cosine, -sine], axis=0)
    forward = complex_rows(cosine, -sine)
    inverse = complex_rows(cosine, sine)
    tables["z_even"] = np.stack([flips(np.kron(two, half_rows(core)), cells) for core in range(cores)], axis=1)
    tables["y_even"] = flips(forward, cells)
    tables["y_odd"] = flips(np.kron(two, full_rows), cells)
    tables["z_odd"] = np.stack([flips(half_mix(core), cells) for core in range(cores)], axis=1)

    spread = []
    for core in range(cores):
        blocks = []
        for turn in range(cores):
            start = (core + turn) % cores * slab
            mix = forward.reshape(2, cells, 2, cells)[:, :, :, start:start + slab]
            for part in range(2):
                block = np.zeros((channels, slab, channels, 2, cells), np.float32)
                for channel in range(channels):
                    block[channel, :, channel] = mix[:, :, part].transpose(2, 0, 1)
                blocks.append(block.reshape(channels * slab, channels * 2 * cells))
        spread.append(np.concatenate(blocks, axis=0))
    tables["x_forward"] = np.stack(spread)

    mirror = np.zeros((cells, cells), np.float32)
    mirror[np.arange(cells), -np.arange(cells) % cells] = 1.0
    eye = np.eye(cells, dtype=np.float32)
    none = np.zeros((cells, cells), np.float32)
    low = 0.5 * np.block([[eye + mirror, none], [none, eye - mirror]])
    high = 0.5 * np.block([[none, eye + mirror], [mirror - eye, none]])
    plain = np.eye(2 * cells, dtype=np.float32)
    tables["unpack"] = np.stack(
        [np.concatenate([low, high] if core == 0 else [plain, 0.0 * plain], axis=0) for core in range(cores)]
    )

    back = []
    for core in range(cores):
        block = np.zeros((LIG_STEPS, 2, cells, 2, cores, LIG_STEPS, slab), np.float32)
        parts = inverse.reshape(2, cells, 2, cells)
        for turn in range(cores):
            start = (core + turn) % cores * slab
            for pose in range(LIG_STEPS):
                block[pose, :, :, :, turn, pose] = parts[:, start:start + slab].transpose(2, 3, 0, 1)
        back.append(block.reshape(LIG_STEPS * 2 * cells, 2 * cores * LIG_STEPS * slab))
    tables["x_inverse"] = np.stack(back)
    tables["y_inverse"] = inverse

    last = []
    for core in range(cores):
        order = [(core + turn) % cores * own + j for turn in range(cores) for j in range(own)]
        real = 2.0 * cosine[order]
        imag = -2.0 * sine[order]
        at = order.index(0)
        real[at] = 1.0
        imag[at] = sign
        last.append(np.stack([real, imag], axis=1).reshape(2 * half, cells).T)
    tables["z_inverse"] = np.stack(last)
    return {name: jnp.asarray(table.astype(ml_dtypes.bfloat16)) for name, table in tables.items()}


def params(limit=48):
    return pltpu.CompilerParams(vmem_limit_bytes=limit * MIB)


def cost(flops, moved):
    return pl.CostEstimate(flops=int(flops), bytes_accessed=int(moved), transcendentals=0)


def lines(value):
    return value.astype(F32).astype(BF16)


def dot(left, right):
    return jnp.dot(left, right, preferred_element_type=F32)


def dot_lanes(left, right):
    return lax.dot_general(left, right, (((1,), (1,)), ((), ())), preferred_element_type=F32)


class Sizes:
    def __init__(self, channels, slab, plane, cores):
        self.channels, self.slab, self.cores = channels, slab, cores
        self.cells = slab * cores
        self.lanes = channels * slab
        self.fold = self.lanes // self.cells
        self.tiles = plane // self.lanes
        self.own = self.cells // 2 // cores
        self.chunks = 2
        self.chunk = self.own // self.chunks
        self.body = self.chunk * 2 * self.cells
        self.extra = 16


def section_kernel(s, steps, rotated, meta, occ, *refs):
    per = s.tiles // steps
    cells, lanes = s.cells, s.lanes
    if rotated:
        z_even, y_even, y_odd, z_odd = refs[:4]
        outs, (held, turned) = refs[4:-2], refs[-2:]
    else:
        z_even, y_even = refs[:2]
        outs, (held,) = refs[2:-1], refs[-1:]
    step = pl.program_id(0)

    def first(table, height):
        for pair in range(0, per, 2):
            rows = [
                lines(occ[0, :, :, (pair + k) * lanes:(pair + k + 1) * lanes].reshape(lanes, lanes)) for k in range(2)
            ]
            done = dot_lanes(table, jnp.concatenate(rows, axis=0))
            for k in range(2):
                for fold in range(s.fold):
                    at = (step * per + pair + k) * s.fold + fold
                    held[pl.ds(pl.multiple_of(at * height, 8), height), :] = done[
                        fold * height:(fold + 1) * height, k * lanes:(k + 1) * lanes
                    ]

    def column(ref, at, height):
        return ref[pl.ds(at, cells, stride=height), :]

    def put(index, value):
        group, plane = divmod(index, s.own)
        chunk, plane = divmod(plane, s.chunk)
        outs[group * s.chunks + chunk][plane * 2 * cells:(plane + 1) * 2 * cells, :] = value

    half = cells // 2

    def even():
        table = y_even[0]
        for pair in range(0, half, 2):
            rows = [
                jnp.concatenate([column(held, q * half + pair + k, cells) for q in range(2)], axis=0) for k in range(2)
            ]
            done = dot(table, jnp.concatenate(rows, axis=1).astype(BF16)).astype(BF16)
            for k in range(2):
                put(pair + k, done[:, k * lanes:(k + 1) * lanes])

    def odd():
        table = z_odd[0, 0]
        for pair in range(0, cells, 2):
            rows = [
                jnp.concatenate([column(held, q * cells + pair + k, 2 * cells) for q in range(2)], axis=0)
                for k in range(2)
            ]
            done = dot(table, jnp.concatenate(rows, axis=1).astype(BF16))
            for k in range(2):
                turned[(pair + k) * cells:(pair + k + 1) * cells, :] = done[:, k * lanes:(k + 1) * lanes]
        for plane in range(half):
            both = [column(turned, q * half + plane, cells) for q in range(2)]
            put(plane, jnp.concatenate(both, axis=0).astype(BF16))

    if rotated:
        is_odd = meta[2] % 2 == 1
        pl.when(jnp.logical_not(is_odd))(lambda: first(z_even[0, 0], cells))
        pl.when(is_odd)(lambda: first(y_odd[0], 2 * cells))
        pl.when(jnp.logical_and(step == steps - 1, jnp.logical_not(is_odd)))(even)
        pl.when(jnp.logical_and(step == steps - 1, is_odd))(odd)
    else:
        first(z_even[0, 0], cells)
        pl.when(step == steps - 1)(even)
        for chunk in range(s.chunks):
            outs[chunk][s.body:, :] = jnp.full((s.extra, lanes), meta[1].astype(F32)).astype(BF16)


def sections(s, t, meta, occ, rotated, steps=4):
    cells, lanes = s.cells, s.lanes
    extra = 0 if rotated else s.extra
    in_specs = [
        pl.BlockSpec((1, s.channels, s.slab, occ.shape[3] // steps), lambda i, m: (0, 0, 0, i)),
        pl.BlockSpec((1, 1) + t["z_even"].shape[2:], lambda i, m: (m[2] >> 1 if rotated else 0, m[0], 0, 0)),
        pl.BlockSpec((1,) + t["y_even"].shape[1:], lambda i, m: (m[2] >> 1 if rotated else 0, 0, 0)),
    ]
    operands = [occ, t["z_even"], t["y_even"]]
    scratch = [pltpu.VMEM((cells * (2 * cells if rotated else cells), lanes), F32)]
    if rotated:
        in_specs += [
            pl.BlockSpec((1,) + t["y_odd"].shape[1:], lambda i, m: (jnp.where(m[2] == 1, 1, 0), 0, 0)),
            pl.BlockSpec((1, 1) + t["z_odd"].shape[2:], lambda i, m: (jnp.where(m[2] == 3, 1, 0), m[0], 0, 0)),
        ]
        operands += [t["y_odd"], t["z_odd"]]
        scratch.append(pltpu.VMEM((cells * cells, lanes), F32))
    shapes = [jax.ShapeDtypeStruct((s.body + extra, lanes), BF16)] * s.chunks
    shapes += [jax.ShapeDtypeStruct((s.body, lanes), BF16)] * s.chunks
    out = pl.pallas_call(
        partial(section_kernel, s, steps, rotated),
        grid_spec=pltpu.PrefetchScalarGridSpec(
            num_scalar_prefetch=1,
            grid=(steps,),
            in_specs=in_specs,
            out_specs=[pl.BlockSpec(shape.shape, lambda i, m: (0, 0)) for shape in shapes],
            scratch_shapes=scratch,
        ),
        out_shape=shapes,
        compiler_params=params(),
        cost_estimate=cost(1.5e9, 4 * MIB),
    )(meta, *operands)
    return out[:s.chunks], out[s.chunks:]


def x_rows(s, own, other, base, planes, first_rows=None):
    stack = []
    for plane in planes:
        at = base + plane * 2 * s.cells
        parts = []
        for ref in (own, other):
            for p in range(2):
                parts.append(ref[at + p * s.cells:at + (p + 1) * s.cells, :])
        stack.append(jnp.concatenate(parts, axis=1))
    return stack


def unpacked_rows(s, own, other, unpack):
    cells = s.cells
    done = [dot(unpack, ref[:2 * cells, :]).astype(BF16) for ref in (own, other)]
    return [
        jnp.concatenate(
            [value[(2 * k + p) * cells:(2 * k + p + 1) * cells] for value in done for p in range(2)], axis=1
        )
        for k in range(2)
    ]


def spectrum_kernel(s, per, packed, meta, weight, own, other, table, unpack, main, *last):
    volume = 1.0 / float(s.cells) ** 3
    width = 2 * s.cells

    def put(ref, value):
        for channel in range(s.channels):
            lanes = slice(channel * width, (channel + 1) * width)
            ref[:, lanes] = (value[:, lanes] * (weight[channel] * volume)).astype(BF16)

    step = pl.program_id(0)
    rows = x_rows(s, own, other, 0, range(per))

    def first():
        low, high = unpacked_rows(s, own, other, unpack[0])
        done = dot(jnp.concatenate([low] + rows[1:] + [high], axis=0), table[0])
        put(main, done[:per * s.cells])
        put(last[0], done[per * s.cells:])

    def rest():
        put(main, dot(jnp.concatenate(rows, axis=0), table[0]))

    if packed:
        pl.when(step == 0)(first)
        pl.when(step > 0)(rest)
    else:
        rest()


def spectrum(s, t, meta, weight, own, other, chunk, per=4):
    rows, width = s.chunk * s.cells, s.channels * 2 * s.cells
    steps = s.chunk // per
    block = pl.BlockSpec((per * 2 * s.cells, s.lanes), lambda i, m, w: (i, 0))
    packed = chunk == 0
    out_specs = [
        pl.BlockSpec((per * s.cells, width), lambda i, m, w: (i, 0)),
        pl.BlockSpec((s.cells, width), lambda i, m, w: (0, 0)),
    ]
    shapes = [jax.ShapeDtypeStruct((rows, width), BF16), jax.ShapeDtypeStruct((s.cells, width), BF16)]
    return pl.pallas_call(
        partial(spectrum_kernel, s, per, packed),
        grid_spec=pltpu.PrefetchScalarGridSpec(
            num_scalar_prefetch=2,
            grid=(steps,),
            in_specs=[
                block,
                block,
                pl.BlockSpec((1,) + t["x_forward"].shape[1:], lambda i, m, w: (m[0], 0, 0)),
                pl.BlockSpec((1,) + t["unpack"].shape[1:], lambda i, m, w: (m[0], 0, 0)),
            ],
            out_specs=out_specs if packed else out_specs[:1],
        ),
        out_shape=shapes if packed else shapes[:1],
        compiler_params=params(),
        cost_estimate=cost(1.2e9, 2 * MIB),
    )(meta, weight, own, other, t["x_forward"], t["unpack"])


def cross_kernel(s, per, packed, meta, own, other, table, unpack, x_inverse, y_inverse, *refs):
    poses = refs[:LIG_STEPS]
    tops = refs[LIG_STEPS:2 * LIG_STEPS] if packed else ()
    keep, send = refs[-2:]
    cells = s.cells
    width = 2 * cells
    step = pl.program_id(0)
    lane = lax.broadcasted_iota(jnp.int32, (cells, width), 1)
    is_real = lane < cells

    def correlate(receptor, pose):
        straight = None
        for channel in range(s.channels):
            lanes = slice(channel * width, (channel + 1) * width)
            one = receptor[:, lanes]
            two = pose[:, lanes].astype(F32)
            here = (one * two, pltpu.roll(one, cells, 1) * two)
            straight = here if straight is None else (straight[0] + here[0], straight[1] + here[1])
        same, turned = straight
        return jnp.where(is_real, same + pltpu.roll(same, cells, 1), pltpu.roll(turned, cells, 1) - turned)

    def run(rows, first):
        done = dot(jnp.concatenate(rows, axis=0), table[0])
        cross = []
        for plane in range(per):
            here = slice(plane * cells, (plane + 1) * cells)
            both = []
            for pose in range(LIG_STEPS):
                value = correlate(done[here], poses[pose][here, :])
                if first and plane == 0:
                    row = lax.broadcasted_iota(jnp.int32, (cells, width), 0)
                    at_zero = (row == 0) & ((lane == 0) | (lane == cells)) & (meta[0] == 0)
                    value = jnp.where(at_zero, 0.0, value)
                    top = pltpu.roll(correlate(done[per * cells:], tops[pose][...]), cells, 1)
                    value = value + jnp.where(is_real, -top, top)
                both.append(value.astype(BF16))
            cross.append(jnp.concatenate(both, axis=1))
        back = dot(jnp.concatenate(cross, axis=0), x_inverse[0]).astype(BF16)
        lanes = s.cores * LIG_STEPS * s.slab
        kept = lax.broadcasted_iota(jnp.int32, (cells // 2, lanes), 1) < lanes // 2
        for pair in range(0, per, 2):
            planes = []
            for k in range(2):
                here = back[(pair + k) * cells:(pair + k + 1) * cells]
                planes.append(jnp.concatenate([here[:, :lanes], here[:, lanes:]], axis=0))
            out = dot(y_inverse[...], jnp.concatenate(planes, axis=1))
            for k in range(2):
                for q in range(2):
                    value = out[q * cells:(q + 1) * cells, k * lanes:(k + 1) * lanes]
                    low, high = value[:cells // 2], value[cells // 2:]
                    at = slice((pair + k) * cells + q * cells // 2, (pair + k) * cells + (q + 1) * cells // 2)
                    keep[at, :] = jnp.where(kept, low, pltpu.roll(high, lanes // 2, 1)).astype(BF16)
                    send[at, :] = jnp.where(kept, pltpu.roll(low, lanes // 2, 1), high).astype(BF16)

    rows = x_rows(s, own, other, 0, range(per))
    if packed:

        def opening():
            low, high = unpacked_rows(s, own, other, unpack[0])
            run([low] + rows[1:] + [high], True)

        pl.when(step == 0)(opening)
        pl.when(step > 0)(lambda: run(rows, False))
    else:
        run(rows, False)


def cross_back(s, t, meta, own, other, poses, tops, chunk, per=4):
    rows = s.chunk * s.cells
    steps = s.chunk // per
    packed = chunk == 0
    width = s.channels * 2 * s.cells
    block = pl.BlockSpec((per * 2 * s.cells, s.lanes), lambda i, m: (i, 0))
    in_specs = [
        block,
        block,
        pl.BlockSpec((1,) + t["x_forward"].shape[1:], lambda i, m: (m[0], 0, 0)),
        pl.BlockSpec((1,) + t["unpack"].shape[1:], lambda i, m: (m[0], 0, 0)),
        pl.BlockSpec((1,) + t["x_inverse"].shape[1:], lambda i, m: (m[0], 0, 0)),
        pl.BlockSpec(t["y_inverse"].shape, lambda i, m: (0, 0)),
    ]
    in_specs += [pl.BlockSpec((per * s.cells, width), lambda i, m: (i, 0))] * LIG_STEPS
    operands = [own, other, t["x_forward"], t["unpack"], t["x_inverse"], t["y_inverse"]]
    operands += [pose[chunk] for pose in poses]
    if packed:
        in_specs += [pl.BlockSpec((s.cells, width), lambda i, m: (0, 0))] * LIG_STEPS
        operands += tops
    lanes = s.cores * LIG_STEPS * s.slab
    out_block = pl.BlockSpec((per * s.cells, lanes), lambda i, m: (i, 0))
    return pl.pallas_call(
        partial(cross_kernel, s, per, packed),
        grid_spec=pltpu.PrefetchScalarGridSpec(
            num_scalar_prefetch=1, grid=(steps,), in_specs=in_specs, out_specs=[out_block] * 2
        ),
        out_shape=[jax.ShapeDtypeStruct((rows, lanes), BF16)] * 2,
        compiler_params=params(),
        cost_estimate=cost(1.5e9, 4 * MIB),
    )(meta, *operands)


def peak_kernel(s, last, meta, load, table, *refs):
    count = s.chunks * s.cores
    parts = refs[:count]
    earlier, out, held = refs[count:-2], refs[-2], refs[-1]
    cells = s.cells
    rows = s.chunk * cells
    for index, part in enumerate(parts):
        held[index * rows:(index + 1) * rows, :] = part[...].astype(F32)
    best = None
    low = cells // 2
    for pair in range(0, low, 2):
        columns = [held[pl.ds(pair + k, cells, stride=low), :] for k in range(2)]
        scores = dot(table[0], jnp.concatenate(columns, axis=1).astype(BF16))
        lanes = scores.shape[1] // 2
        here = jnp.maximum(scores[:, :lanes], scores[:, lanes:])
        best = here if best is None else jnp.maximum(best, here)
    row = jnp.max(best, axis=0, keepdims=True)
    row = jnp.maximum(row, pltpu.roll(row, row.shape[1] // 2, 1)) * (1.0 / (cells * math.sqrt(cells)))
    plane = lax.broadcasted_iota(jnp.int32, row.shape, 1) % s.slab + meta[0] * s.slab
    row = jnp.where(plane.astype(F32) < load[0:1, :].astype(F32), row, 0.0)
    if not last:
        out[...] = row
        return
    for index, value in enumerate([ref[...] for ref in earlier] + [row]):
        for pose in range(LIG_STEPS):
            out[0, index, pose:pose + 1, :] = value[:, pose * s.slab:(pose + 1) * s.slab]


def peaks(s, t, meta, load, kept, received, earlier, last):
    parts = [part for pair in (kept, received) for part in pair]
    lanes = parts[0].shape[1]
    in_specs = [
        pl.BlockSpec((s.extra, s.lanes), lambda i, m: (s.body // s.extra, 0)),
        pl.BlockSpec((1,) + t["z_inverse"].shape[1:], lambda i, m: (m[0], 0, 0)),
    ]
    in_specs += [pl.BlockSpec(part.shape, lambda i, m: (0, 0)) for part in parts]
    in_specs += [pl.BlockSpec((1, lanes), lambda i, m: (0, 0)) for _ in earlier]
    if last:
        shape = (1, REC_STEPS, LIG_STEPS, s.slab)
        out_spec = pl.BlockSpec(shape, lambda i, m: (0, 0, 0, 0))
    else:
        shape = (1, lanes)
        out_spec = pl.BlockSpec(shape, lambda i, m: (0, 0))
    return pl.pallas_call(
        partial(peak_kernel, s, last),
        grid_spec=pltpu.PrefetchScalarGridSpec(
            num_scalar_prefetch=1,
            grid=(1,),
            in_specs=in_specs,
            out_specs=out_spec,
            scratch_shapes=[pltpu.VMEM((len(parts) * parts[0].shape[0], lanes), F32)],
        ),
        out_shape=jax.ShapeDtypeStruct(shape, F32),
        compiler_params=params(),
        cost_estimate=cost(1e9, 2 * MIB),
    )(meta, load, t["z_inverse"], *parts, *earlier)


def passed_along(value, axis, steps=1):
    count = lax.axis_size(axis)
    return lax.ppermute(value, axis, [(source, (source + steps) % count) for source in range(count)])


def shards(tables, receptor_occupancy, ligand_occupancy, rot_index, receptor_extent, channel_weight):
    _, channels, slab, plane = receptor_occupancy.shape
    s = Sizes(channels, slab, plane, lax.axis_size("fft"))
    t = tables(s)
    core = lax.axis_index("fft").astype(jnp.int32)
    meta = jnp.concatenate([core[None], receptor_extent, rot_index])
    swapped = lambda parts: [passed_along(part, "fft") for part in parts]

    own, away = sections(s, t, meta, receptor_occupancy, False)
    other = swapped(away)
    receptors = [(own, other)]
    for _ in range(REC_STEPS - 1):
        own = [passed_along(part, "rec") for part in own]
        other = [passed_along(part, "rec") for part in other]
        receptors.append((own, other))

    pose_own, pose_away = sections(s, t, meta, ligand_occupancy, True)
    pose_other = swapped(pose_away)
    poses, tops = [], []
    for step in range(LIG_STEPS):
        if step:
            pose_own = [passed_along(part, "lig") for part in pose_own]
            pose_other = [passed_along(part, "lig") for part in pose_other]
        done = [
            spectrum(s, t, meta, channel_weight, a, b, chunk) for chunk, (a, b) in enumerate(zip(pose_own, pose_other))
        ]
        poses.append([out[0] for out in done])
        tops.append(done[0][1])

    rows = []
    for step, (own, other) in enumerate(receptors):
        kept, received = [], []
        for chunk in range(s.chunks):
            keep, send = cross_back(s, t, meta, own[chunk], other[chunk], poses, tops, chunk)
            kept.append(keep)
            received += swapped([send])
        last = step + 1 == REC_STEPS
        rows.append(peaks(s, t, meta, own[0], kept, received, rows if last else [], last))
    return rows[-1]


def solution(mesh):
    placed = (
        P(("groups", "rec", "lig"), None, "fft", None),
        P(("groups", "rec", "lig"), None, "fft", None),
        P(("groups", "rec", "lig")),
        P(("groups", "rec", "lig")),
        P(),
    )
    tables = lambda s: build_tables(s.cells, s.channels, s.slab, s.cores)
    return jax.shard_map(
        partial(shards, tables),
        mesh=mesh,
        in_specs=placed,
        out_specs=P(("groups", "rec", "lig"), None, None, "fft"),
        check_vma=False,
    )
```

profile of v0, /device:TPU:0, one launch (start us, length us, event | category | flops | bytes accessed | tf_op | source)
XLA Modules:
  0.0 83.9 jit_solution(376789446206640842)
XLA Ops:
  1.4 1.6 %copy-done = s32[1,4,32,4096]{3,2,1,0:T(8,128)S(1)} copy-done((s32[1,4,32,4096]{3,2,1,0:T(8,128)S(1)}, s32[1,4,32,4096]{3,2,1,0:T(8,128)}, u32[]{:S(2)}) %copy-start) | copy-done | bytes 2097176
  6.5 3.2 %shard_map.137 = (bf16[1024,128]{1,0:T(8,128)(2,1)S(1)}, bf16[1024,128]{1,0:T(8,128)(2,1)S(1)}, bf16[1024,128]{1,0:T(8,128)(2,1)S(1)}, bf16[1024,128]{1,0:T(8,128)(2,1)S(1)}) custom-call(s32[3]{0:T(128)S(1)} %pad_add_fusion.meta, s32[1,4,32,4096]{3,2,1,0:T(8,128)S(1)} %copy-done, bf16[2,2,128,128]{3,2,1,0:T(8,128)(2,1)S(1)} %copy-done.6, ...), custom_call_target="tpu_custom_call" | custom-call | flops 1500000000 | bytes 4194304 | tf_op jit(solution)/shard_map/pallas_call | solution.py:245
  10.3 5.4 %collective-permute-start.6 = (bf16[1024,128]{1,0:T(8,128)(2,1)S(1)}, bf16[1024,128]{1,0:T(8,128)(2,1)S(1)}, u32[]{:S(2)}, u32[]{:S(2)}) collective-permute-start(bf16[1024,128]{1,0:T(8,128)(2,1)S(1)} %get-tuple-element.31.own), channel_id=1, source_target_pairs={{0,2},{2,0},{1,3},{3,1},{4,6},{6,4},{5,7},{7,5},{8,10},{10,8},{9,1... | collective-permute-start | bytes 786440 | tf_op jit(solution)/shard_map/ppermute | solution.py:501
  15.7 3.1 %shard_map.136 = (bf16[1040,128]{1,0:T(8,128)(2,1)S(1)}, bf16[1040,128]{1,0:T(8,128)(2,1)S(1)}, bf16[1024,128]{1,0:T(8,128)(2,1)S(1)}, bf16[1024,128]{1,0:T(8,128)(2,1)S(1)}) custom-call(s32[3]{0:T(128)S(1)} %pad_add_fusion.meta, s32[1,4,32,4096]{3,2,1,0:T(8,128)S(1)} %copy-done.1, bf16[2,2,128,128]{3,2,1,0:T(8,128)(2,1)S(1)} %copy-done.7, ...), custom_call_target="tpu_custom_call" | custom-call | flops 1500000000 | bytes 4194304 | tf_op jit(solution)/shard_map/pallas_call | solution.py:245
  19.4 2.0 %collective-permute-start.7 = (bf16[1024,128]{1,0:T(8,128)(2,1)S(1)}, bf16[1024,128]{1,0:T(8,128)(2,1)S(1)}, u32[]{:S(2)}, u32[]{:S(2)}) collective-permute-start(bf16[1024,128]{1,0:T(8,128)(2,1)S(1)} %collective-permute-done.5.other), channel_id=1, source_target_pairs={{0,2},{2,0},{1,3},{3,1},{4,6},{6,4},{5,7},{7,5},{8,10},{10,8},{9,1... | collective-permute-start | bytes 786440 | tf_op jit(solution)/shard_map/ppermute | solution.py:501
  22.8 1.6 %collective-permute-start.8 = (bf16[1040,128]{1,0:T(8,128)(2,1)S(1)}, bf16[1040,128]{1,0:T(8,128)(2,1)S(1)}, u32[]{:S(2)}, u32[]{:S(2)}) collective-permute-start(bf16[1040,128]{1,0:T(8,128)(2,1)S(1)} %get-tuple-element.38.own), channel_id=1, source_target_pairs={{0,4},{4,8},{8,12},{12,0},{1,5},{5,9},{9,13},{13,1},{2,6},{6,10},{... | collective-permute-start | bytes 798728 | tf_op jit(solution)/shard_map/ppermute | solution.py:501
  24.3 4.0 %collective-permute-done.14.own = bf16[1024,128]{1,0:T(8,128)(2,1)S(1)} collective-permute-done((bf16[1024,128]{1,0:T(8,128)(2,1)S(1)}, bf16[1024,128]{1,0:T(8,128)(2,1)S(1)}, u32[]{:S(2)}, u32[]{:S(2)}) %collective-permute-start.14) | collective-permute-done | bytes 262176 | tf_op jit(solution)/shard_map/ppermute | solution.py:501
  28.4 1.6 %collective-permute-start = (bf16[1040,128]{1,0:T(8,128)(2,1)S(1)}, bf16[1040,128]{1,0:T(8,128)(2,1)S(1)}, u32[]{:S(2)}, u32[]{:S(2)}) collective-permute-start(bf16[1040,128]{1,0:T(8,128)(2,1)S(1)} %get-tuple-element.29.own.load), channel_id=1, source_target_pairs={{0,4},{4,8},{8,12},{12,0},{1,5},{5,9},{9,13},{13,1},{2,6},{6,10},{... | collective-permute-start | bytes 798728 | tf_op jit(solution)/shard_map/ppermute | solution.py:501
  30.0 2.1 %collective-permute-start.15 = (bf16[1024,128]{1,0:T(8,128)(2,1)S(1)}, bf16[1024,128]{1,0:T(8,128)(2,1)S(1)}, u32[]{:S(2)}, u32[]{:S(2)}) collective-permute-start(bf16[1024,128]{1,0:T(8,128)(2,1)S(1)} %collective-permute-done.13.other), channel_id=1, source_target_pairs={{0,2},{2,0},{1,3},{3,1},{4,6},{6,4},{5,7},{7,5},{8,10},{10,8},{9,1... | collective-permute-start | bytes 786440 | tf_op jit(solution)/shard_map/ppermute | solution.py:501
  32.2 1.8 %collective-permute-done.7.other = bf16[1024,128]{1,0:T(8,128)(2,1)S(1)} collective-permute-done((bf16[1024,128]{1,0:T(8,128)(2,1)S(1)}, bf16[1024,128]{1,0:T(8,128)(2,1)S(1)}, u32[]{:S(2)}, u32[]{:S(2)}) %collective-permute-start.7) | collective-permute-done | bytes 262176 | tf_op jit(solution)/shard_map/ppermute | solution.py:501
  34.0 1.6 %collective-permute-start.11 = (bf16[1024,128]{1,0:T(8,128)(2,1)S(1)}, bf16[1024,128]{1,0:T(8,128)(2,1)S(1)}, u32[]{:S(2)}, u32[]{:S(2)}) collective-permute-start(bf16[1024,128]{1,0:T(8,128)(2,1)S(1)} %collective-permute-done.10.other), channel_id=1, source_target_pairs={{0,4},{4,8},{8,12},{12,0},{1,5},{5,9},{9,13},{13,1},{2,6},{6,10},{... | collective-permute-start | bytes 786440 | tf_op jit(solution)/shard_map/ppermute | solution.py:501
  38.4 2.9 %shard_map.144 = (bf16[512,128]{1,0:T(8,128)(2,1)S(1)}, bf16[512,128]{1,0:T(8,128)(2,1)S(1)}) custom-call(s32[3]{0:T(128)S(1)} %pad_add_fusion.meta, bf16[1040,128]{1,0:T(8,128)(2,1)S(1)} %get-tuple-element.29.own.load, bf16[1024,128]{1,0:T(8,128)(2,1)S(1)} %collective-permute-done.2.other, bf16[2,512,512]{2,1,0:T(8,128)(2,1)S(1)} %copy-done.3, ...), custom_call_target="tpu_custom_call" | custom-call | flops 1500000000 | bytes 4194304 | tf_op jit(solution)/shard_map/pallas_call | solution.py:430
  41.3 2.2 %collective-permute-start.9 = (bf16[1040,128]{1,0:T(8,128)(2,1)S(1)}, bf16[1040,128]{1,0:T(8,128)(2,1)S(1)}, u32[]{:S(2)}, u32[]{:S(2)}) collective-permute-start(bf16[1040,128]{1,0:T(8,128)(2,1)S(1)} %collective-permute-done.8.own), channel_id=1, source_target_pairs={{0,4},{4,8},{8,12},{12,0},{1,5},{5,9},{9,13},{13,1},{2,6},{6,10},{... | collective-permute-start | bytes 798728 | tf_op jit(solution)/shard_map/ppermute | solution.py:501
  43.6 1.6 %collective-permute-done.3.other = bf16[1024,128]{1,0:T(8,128)(2,1)S(1)} collective-permute-done((bf16[1024,128]{1,0:T(8,128)(2,1)S(1)}, bf16[1024,128]{1,0:T(8,128)(2,1)S(1)}, u32[]{:S(2)}, u32[]{:S(2)}) %collective-permute-start.3) | collective-permute-done | bytes 262176 | tf_op jit(solution)/shard_map/ppermute | solution.py:501
  45.1 5.6 %collective-permute-done.11.other = bf16[1024,128]{1,0:T(8,128)(2,1)S(1)} collective-permute-done((bf16[1024,128]{1,0:T(8,128)(2,1)S(1)}, bf16[1024,128]{1,0:T(8,128)(2,1)S(1)}, u32[]{:S(2)}, u32[]{:S(2)}) %collective-permute-start.11) | collective-permute-done | bytes 262176 | tf_op jit(solution)/shard_map/ppermute | solution.py:501
  51.9 2.5 %shard_map.145 = (bf16[512,128]{1,0:T(8,128)(2,1)S(1)}, bf16[512,128]{1,0:T(8,128)(2,1)S(1)}) custom-call(s32[3]{0:T(128)S(1)} %pad_add_fusion.meta, bf16[1040,128]{1,0:T(8,128)(2,1)S(1)} %get-tuple-element.38.own, bf16[1024,128]{1,0:T(8,128)(2,1)S(1)} %collective-permute-done.10.other, bf16[2,512,512]{2,1,0:T(8,128)(2,1)S(1)} %copy-done.3, ...), custom_call_target="tpu_custom_call" | custom-call | flops 1500000000 | bytes 4194304 | tf_op jit(solution)/shard_map/pallas_call | solution.py:430
  54.5 2.5 %shard_map.148 = (bf16[512,128]{1,0:T(8,128)(2,1)S(1)}, bf16[512,128]{1,0:T(8,128)(2,1)S(1)}) custom-call(s32[3]{0:T(128)S(1)} %pad_add_fusion.meta, bf16[1040,128]{1,0:T(8,128)(2,1)S(1)} %collective-permute-done.8.own, bf16[1024,128]{1,0:T(8,128)(2,1)S(1)} %collective-permute-done.11.other, bf16[2,512,512]{2,1,0:T(8,128)(2,1)S(1)} %copy-done.3, ...), custom_call_target="tpu_custom_call" | custom-call | flops 1500000000 | bytes 4194304 | tf_op jit(solution)/shard_map/pallas_call | solution.py:430
  57.1 2.9 %shard_map.147 = (bf16[512,128]{1,0:T(8,128)(2,1)S(1)}, bf16[512,128]{1,0:T(8,128)(2,1)S(1)}) custom-call(s32[3]{0:T(128)S(1)} %pad_add_fusion.meta, bf16[1040,128]{1,0:T(8,128)(2,1)S(1)} %collective-permute-done.own.load, bf16[1024,128]{1,0:T(8,128)(2,1)S(1)} %collective-permute-done.3.other, bf16[2,512,512]{2,1,0:T(8,128)(2,1)S(1)} %copy-done.3, ...), custom_call_target="tpu_custom_call" | custom-call | flops 1500000000 | bytes 4194304 | tf_op jit(solution)/shard_map/pallas_call | solution.py:430
  60.0 12.1 %collective-permute-done.12.other = bf16[1024,128]{1,0:T(8,128)(2,1)S(1)} collective-permute-done((bf16[1024,128]{1,0:T(8,128)(2,1)S(1)}, bf16[1024,128]{1,0:T(8,128)(2,1)S(1)}, u32[]{:S(2)}, u32[]{:S(2)}) %collective-permute-start.12) | collective-permute-done | bytes 262176 | tf_op jit(solution)/shard_map/ppermute | solution.py:501
  72.2 2.6 %shard_map.143 = (bf16[512,128]{1,0:T(8,128)(2,1)S(1)}, bf16[512,128]{1,0:T(8,128)(2,1)S(1)}) custom-call(s32[3]{0:T(128)S(1)} %pad_add_fusion.meta, bf16[1040,128]{1,0:T(8,128)(2,1)S(1)} %collective-permute-done.9.own, bf16[1024,128]{1,0:T(8,128)(2,1)S(1)} %collective-permute-done.12.other, bf16[2,512,512]{2,1,0:T(8,128)(2,1)S(1)} %copy-done.3, ...), custom_call_target="tpu_custom_call" | custom-call | flops 1500000000 | bytes 4194304 | tf_op jit(solution)/shard_map/pallas_call | solution.py:430
  75.4 2.9 %shard_map.140 = (bf16[512,128]{1,0:T(8,128)(2,1)S(1)}, bf16[512,128]{1,0:T(8,128)(2,1)S(1)}) custom-call(s32[3]{0:T(128)S(1)} %pad_add_fusion.meta, bf16[1040,128]{1,0:T(8,128)(2,1)S(1)} %collective-permute-done.1.own.load, bf16[1024,128]{1,0:T(8,128)(2,1)S(1)} %collective-permute-done.4.other, bf16[2,512,512]{2,1,0:T(8,128)(2,1)S(1)} %copy-done.3, ...), custom_call_target="tpu_custom_call" | custom-call | flops 1500000000 | bytes 4194304 | tf_op jit(solution)/shard_map/pallas_call | solution.py:430
  78.8 1.5 %shard_map.146.refs_4_ = f32[1,128]{1,0:T(1,128)S(1)} custom-call(s32[3]{0:T(128)S(1)} %pad_add_fusion.meta, bf16[1040,128]{1,0:T(8,128)(2,1)S(1)} %get-tuple-element.29.own.load, bf16[2,64,64]{2,1,0:T(8,128)(2,1)S(1)} %copy-done.12, bf16[512,128]{1,0:T(8,128)(2,1)S(1)} %get-tuple-element.45.refs_0_, bf16[512,128]{1,0:T(8,128)(2,1)S(1)} %get-tuple-element.46.refs_1_, ...), custom_call_target="tpu_custom_call" | custom-call | flops 1000000000 | bytes 2097152 | tf_op jit(solution)/shard_map/pallas_call | solution.py:484
  80.3 1.5 %shard_map.149.refs_5_ = f32[1,128]{1,0:T(1,128)S(1)} custom-call(s32[3]{0:T(128)S(1)} %pad_add_fusion.meta, bf16[1040,128]{1,0:T(8,128)(2,1)S(1)} %collective-permute-done.own.load, bf16[2,64,64]{2,1,0:T(8,128)(2,1)S(1)} %copy-done.12, bf16[512,128]{1,0:T(8,128)(2,1)S(1)} %get-tuple-element.49.refs_0_, bf16[512,128]{1,0:T(8,128)(2,1)S(1)} %get-tuple-element.50.refs_1_, ...), custom_call_target="tpu_custom_call" | custom-call | flops 1000000000 | bytes 2097152 | tf_op jit(solution)/shard_map/pallas_call | solution.py:484
  81.8 2.2 %shard_map.150 = f32[1,3,2,32]{3,2,1,0:T(2,128)} custom-call(s32[3]{0:T(128)S(1)} %pad_add_fusion.meta, bf16[1040,128]{1,0:T(8,128)(2,1)S(1)} %collective-permute-done.1.own.load, bf16[2,64,64]{2,1,0:T(8,128)(2,1)S(1)} %copy-done.12, bf16[512,128]{1,0:T(8,128)(2,1)S(1)} %get-tuple-element.37.refs_0_, bf16[512,128]{1,0:T(8,128)(2,1)S(1)} %get-tuple-element.42.refs_1_, ...), custom_call_target="tpu_custom_call" | custom-call | flops 1000000000 | bytes 2097152 | tf_op jit(solution)/shard_map/pallas_call | solution.py:484
  (64 shorter events, 11.6 us)
Async XLA Ops:
  6.5 9.3 %copy-start.7 = (bf16[2,2,128,128]{3,2,1,0:T(8,128)(2,1)S(1)}, bf16[2,2,128,128]{3,2,1,0:T(8,128)(2,1)}, u32[]{:S(2)}) copy-start(bf16[2,2,128,128]{3,2,1,0:T(8,128)(2,1)} %constant.22.clone.refs_0_) | copy-start | bytes 393220
  6.5 9.3 %copy-start.10 = (bf16[2,128,128]{2,1,0:T(8,128)(2,1)S(1)}, bf16[2,128,128]{2,1,0:T(8,128)(2,1)}, u32[]{:S(2)}) copy-start(bf16[2,128,128]{2,1,0:T(8,128)(2,1)} %constant.23.clone.refs_1_) | copy-start | bytes 196612
  9.7 9.3 %collective-permute-start.5 = (bf16[1024,128]{1,0:T(8,128)(2,1)S(1)}, bf16[1024,128]{1,0:T(8,128)(2,1)S(1)}, u32[]{:S(2)}, u32[]{:S(2)}) collective-permute-start(bf16[1024,128]{1,0:T(8,128)(2,1)S(1)} %get-tuple-element.32), channel_id=1, source_target_pairs={{0,1},{1,0},{2,3},{3,2},{4,5},{5,4},{6,7},{7,6},{8,9},{9,8},{10,11... | collective-permute-start | bytes 786440 | tf_op jit(solution)/shard_map/ppermute | solution.py:501
  10.2 9.3 %collective-permute-start.13 = (bf16[1024,128]{1,0:T(8,128)(2,1)S(1)}, bf16[1024,128]{1,0:T(8,128)(2,1)S(1)}, u32[]{:S(2)}, u32[]{:S(2)}) collective-permute-start(bf16[1024,128]{1,0:T(8,128)(2,1)S(1)} %get-tuple-element.41), channel_id=1, source_target_pairs={{0,1},{1,0},{2,3},{3,2},{4,5},{5,4},{6,7},{7,6},{8,9},{9,8},{10,11... | collective-permute-start | bytes 786440 | tf_op jit(solution)/shard_map/ppermute | solution.py:501
  10.3 12.5 %collective-permute-start.6 = (bf16[1024,128]{1,0:T(8,128)(2,1)S(1)}, bf16[1024,128]{1,0:T(8,128)(2,1)S(1)}, u32[]{:S(2)}, u32[]{:S(2)}) collective-permute-start(bf16[1024,128]{1,0:T(8,128)(2,1)S(1)} %get-tuple-element.31.own), channel_id=1, source_target_pairs={{0,2},{2,0},{1,3},{3,1},{4,6},{6,4},{5,7},{7,5},{8,10},{10,8},{9,1... | collective-permute-start | bytes 786440 | tf_op jit(solution)/shard_map/ppermute | solution.py:501
  15.7 12.7 %collective-permute-start.14 = (bf16[1024,128]{1,0:T(8,128)(2,1)S(1)}, bf16[1024,128]{1,0:T(8,128)(2,1)S(1)}, u32[]{:S(2)}, u32[]{:S(2)}) collective-permute-start(bf16[1024,128]{1,0:T(8,128)(2,1)S(1)} %get-tuple-element.40.own), channel_id=1, source_target_pairs={{0,2},{2,0},{1,3},{3,1},{4,6},{6,4},{5,7},{7,5},{8,10},{10,8},{9,1... | collective-permute-start | bytes 786440 | tf_op jit(solution)/shard_map/ppermute | solution.py:501
  18.9 11.1 %collective-permute-start.2 = (bf16[1024,128]{1,0:T(8,128)(2,1)S(1)}, bf16[1024,128]{1,0:T(8,128)(2,1)S(1)}, u32[]{:S(2)}, u32[]{:S(2)}) collective-permute-start(bf16[1024,128]{1,0:T(8,128)(2,1)S(1)} %get-tuple-element.30), channel_id=1, source_target_pairs={{0,1},{1,0},{2,3},{3,2},{4,5},{5,4},{6,7},{7,6},{8,9},{9,8},{10,11... | collective-permute-start | bytes 786440 | tf_op jit(solution)/shard_map/ppermute | solution.py:501
  19.0 13.1 %collective-permute-start.10 = (bf16[1024,128]{1,0:T(8,128)(2,1)S(1)}, bf16[1024,128]{1,0:T(8,128)(2,1)S(1)}, u32[]{:S(2)}, u32[]{:S(2)}) collective-permute-start(bf16[1024,128]{1,0:T(8,128)(2,1)S(1)} %get-tuple-element.39), channel_id=1, source_target_pairs={{0,1},{1,0},{2,3},{3,2},{4,5},{5,4},{6,7},{7,6},{8,9},{9,8},{10,11... | collective-permute-start | bytes 786440 | tf_op jit(solution)/shard_map/ppermute | solution.py:501
  19.4 14.5 %collective-permute-start.7 = (bf16[1024,128]{1,0:T(8,128)(2,1)S(1)}, bf16[1024,128]{1,0:T(8,128)(2,1)S(1)}, u32[]{:S(2)}, u32[]{:S(2)}) collective-permute-start(bf16[1024,128]{1,0:T(8,128)(2,1)S(1)} %collective-permute-done.5.other), channel_id=1, source_target_pairs={{0,2},{2,0},{1,3},{3,1},{4,6},{6,4},{5,7},{7,5},{8,10},{10,8},{9,1... | collective-permute-start | bytes 786440 | tf_op jit(solution)/shard_map/ppermute | solution.py:501
  22.8 18.5 %collective-permute-start.8 = (bf16[1040,128]{1,0:T(8,128)(2,1)S(1)}, bf16[1040,128]{1,0:T(8,128)(2,1)S(1)}, u32[]{:S(2)}, u32[]{:S(2)}) collective-permute-start(bf16[1040,128]{1,0:T(8,128)(2,1)S(1)} %get-tuple-element.38.own), channel_id=1, source_target_pairs={{0,4},{4,8},{8,12},{12,0},{1,5},{5,9},{9,13},{13,1},{2,6},{6,10},{... | collective-permute-start | bytes 798728 | tf_op jit(solution)/shard_map/ppermute | solution.py:501
  28.4 15.1 %collective-permute-start = (bf16[1040,128]{1,0:T(8,128)(2,1)S(1)}, bf16[1040,128]{1,0:T(8,128)(2,1)S(1)}, u32[]{:S(2)}, u32[]{:S(2)}) collective-permute-start(bf16[1040,128]{1,0:T(8,128)(2,1)S(1)} %get-tuple-element.29.own.load), channel_id=1, source_target_pairs={{0,4},{4,8},{8,12},{12,0},{1,5},{5,9},{9,13},{13,1},{2,6},{6,10},{... | collective-permute-start | bytes 798728 | tf_op jit(solution)/shard_map/ppermute | solution.py:501
  30.0 13.6 %collective-permute-start.15 = (bf16[1024,128]{1,0:T(8,128)(2,1)S(1)}, bf16[1024,128]{1,0:T(8,128)(2,1)S(1)}, u32[]{:S(2)}, u32[]{:S(2)}) collective-permute-start(bf16[1024,128]{1,0:T(8,128)(2,1)S(1)} %collective-permute-done.13.other), channel_id=1, source_target_pairs={{0,2},{2,0},{1,3},{3,1},{4,6},{6,4},{5,7},{7,5},{8,10},{10,8},{9,1... | collective-permute-start | bytes 786440 | tf_op jit(solution)/shard_map/ppermute | solution.py:501
  32.0 13.1 %collective-permute-start.3 = (bf16[1024,128]{1,0:T(8,128)(2,1)S(1)}, bf16[1024,128]{1,0:T(8,128)(2,1)S(1)}, u32[]{:S(2)}, u32[]{:S(2)}) collective-permute-start(bf16[1024,128]{1,0:T(8,128)(2,1)S(1)} %collective-permute-done.2.other), channel_id=1, source_target_pairs={{0,4},{4,8},{8,12},{12,0},{1,5},{5,9},{9,13},{13,1},{2,6},{6,10},{... | collective-permute-start | bytes 786440 | tf_op jit(solution)/shard_map/ppermute | solution.py:501
  34.0 16.7 %collective-permute-start.11 = (bf16[1024,128]{1,0:T(8,128)(2,1)S(1)}, bf16[1024,128]{1,0:T(8,128)(2,1)S(1)}, u32[]{:S(2)}, u32[]{:S(2)}) collective-permute-start(bf16[1024,128]{1,0:T(8,128)(2,1)S(1)} %collective-permute-done.10.other), channel_id=1, source_target_pairs={{0,4},{4,8},{8,12},{12,0},{1,5},{5,9},{9,13},{13,1},{2,6},{6,10},{... | collective-permute-start | bytes 786440 | tf_op jit(solution)/shard_map/ppermute | solution.py:501
  41.3 18.7 %collective-permute-start.9 = (bf16[1040,128]{1,0:T(8,128)(2,1)S(1)}, bf16[1040,128]{1,0:T(8,128)(2,1)S(1)}, u32[]{:S(2)}, u32[]{:S(2)}) collective-permute-start(bf16[1040,128]{1,0:T(8,128)(2,1)S(1)} %collective-permute-done.8.own), channel_id=1, source_target_pairs={{0,4},{4,8},{8,12},{12,0},{1,5},{5,9},{9,13},{13,1},{2,6},{6,10},{... | collective-permute-start | bytes 798728 | tf_op jit(solution)/shard_map/ppermute | solution.py:501
  43.5 31.3 %collective-permute-start.1 = (bf16[1040,128]{1,0:T(8,128)(2,1)S(1)}, bf16[1040,128]{1,0:T(8,128)(2,1)S(1)}, u32[]{:S(2)}, u32[]{:S(2)}) collective-permute-start(bf16[1040,128]{1,0:T(8,128)(2,1)S(1)} %collective-permute-done.own.load), channel_id=1, source_target_pairs={{0,4},{4,8},{8,12},{12,0},{1,5},{5,9},{9,13},{13,1},{2,6},{6,10},{... | collective-permute-start | bytes 798728 | tf_op jit(solution)/shard_map/ppermute | solution.py:501
  43.5 34.7 %collective-permute-start.18 = (bf16[512,128]{1,0:T(8,128)(2,1)S(1)}, bf16[512,128]{1,0:T(8,128)(2,1)S(1)}, u32[]{:S(2)}, u32[]{:S(2)}) collective-permute-start(bf16[512,128]{1,0:T(8,128)(2,1)S(1)} %get-tuple-element.47), channel_id=1, source_target_pairs={{0,1},{1,0},{2,3},{3,2},{4,5},{5,4},{6,7},{7,6},{8,9},{9,8},{10,11... | collective-permute-start | bytes 393224 | tf_op jit(solution)/shard_map/ppermute | solution.py:501
  45.1 30.2 %collective-permute-start.4 = (bf16[1024,128]{1,0:T(8,128)(2,1)S(1)}, bf16[1024,128]{1,0:T(8,128)(2,1)S(1)}, u32[]{:S(2)}, u32[]{:S(2)}) collective-permute-start(bf16[1024,128]{1,0:T(8,128)(2,1)S(1)} %collective-permute-done.3.other), channel_id=1, source_target_pairs={{0,4},{4,8},{8,12},{12,0},{1,5},{5,9},{9,13},{13,1},{2,6},{6,10},{... | collective-permute-start | bytes 786440 | tf_op jit(solution)/shard_map/ppermute | solution.py:501
  50.7 21.4 %collective-permute-start.12 = (bf16[1024,128]{1,0:T(8,128)(2,1)S(1)}, bf16[1024,128]{1,0:T(8,128)(2,1)S(1)}, u32[]{:S(2)}, u32[]{:S(2)}) collective-permute-start(bf16[1024,128]{1,0:T(8,128)(2,1)S(1)} %collective-permute-done.11.other), channel_id=1, source_target_pairs={{0,4},{4,8},{8,12},{12,0},{1,5},{5,9},{9,13},{13,1},{2,6},{6,10},{... | collective-permute-start | bytes 786440 | tf_op jit(solution)/shard_map/ppermute | solution.py:501
  59.9 18.8 %collective-permute-start.19 = (bf16[512,128]{1,0:T(8,128)(2,1)S(1)}, bf16[512,128]{1,0:T(8,128)(2,1)S(1)}, u32[]{:S(2)}, u32[]{:S(2)}) collective-permute-start(bf16[512,128]{1,0:T(8,128)(2,1)S(1)} %get-tuple-element.48), channel_id=1, source_target_pairs={{0,1},{1,0},{2,3},{3,2},{4,5},{5,4},{6,7},{7,6},{8,9},{9,8},{10,11... | collective-permute-start | bytes 393224 | tf_op jit(solution)/shard_map/ppermute | solution.py:501
  72.2 8.1 %collective-permute-start.21 = (bf16[512,128]{1,0:T(8,128)(2,1)S(1)}, bf16[512,128]{1,0:T(8,128)(2,1)S(1)}, u32[]{:S(2)}, u32[]{:S(2)}) collective-permute-start(bf16[512,128]{1,0:T(8,128)(2,1)S(1)} %get-tuple-element.52), channel_id=1, source_target_pairs={{0,1},{1,0},{2,3},{3,2},{4,5},{5,4},{6,7},{7,6},{8,9},{9,8},{10,11... | collective-permute-start | bytes 393224 | tf_op jit(solution)/shard_map/ppermute | solution.py:501
  74.7 5.5 %collective-permute-start.20 = (bf16[512,128]{1,0:T(8,128)(2,1)S(1)}, bf16[512,128]{1,0:T(8,128)(2,1)S(1)}, u32[]{:S(2)}, u32[]{:S(2)}) collective-permute-start(bf16[512,128]{1,0:T(8,128)(2,1)S(1)} %get-tuple-element.51), channel_id=1, source_target_pairs={{0,1},{1,0},{2,3},{3,2},{4,5},{5,4},{6,7},{7,6},{8,9},{9,8},{10,11... | collective-permute-start | bytes 393224 | tf_op jit(solution)/shard_map/ppermute | solution.py:501
  75.3 6.4 %collective-permute-start.17 = (bf16[512,128]{1,0:T(8,128)(2,1)S(1)}, bf16[512,128]{1,0:T(8,128)(2,1)S(1)}, u32[]{:S(2)}, u32[]{:S(2)}) collective-permute-start(bf16[512,128]{1,0:T(8,128)(2,1)S(1)} %get-tuple-element.44), channel_id=1, source_target_pairs={{0,1},{1,0},{2,3},{3,2},{4,5},{5,4},{6,7},{7,6},{8,9},{9,8},{10,11... | collective-permute-start | bytes 393224 | tf_op jit(solution)/shard_map/ppermute | solution.py:501
  78.3 3.5 %collective-permute-start.16 = (bf16[512,128]{1,0:T(8,128)(2,1)S(1)}, bf16[512,128]{1,0:T(8,128)(2,1)S(1)}, u32[]{:S(2)}, u32[]{:S(2)}) collective-permute-start(bf16[512,128]{1,0:T(8,128)(2,1)S(1)} %get-tuple-element.43), channel_id=1, source_target_pairs={{0,1},{1,0},{2,3},{3,2},{4,5},{5,4},{6,7},{7,6},{8,9},{9,8},{10,11... | collective-permute-start | bytes 393224 | tf_op jit(solution)/shard_map/ppermute | solution.py:501
  (12 other events, 37.9 us)
where the time goes:
time: 84.2 us; the launch traced here: 83.9 us
  Pallas kernels  32.8 us (39%)
  waiting for transfers between devices  25.4 us (30%)
  starting transfers between devices  19 us (23%)
  local copies, waits for them, and re-layouts  5.12 us (6%)
  between operations  1.52 us (2%)
    ppermute x22, waiting for transfers between devices, passed_along(): lax.ppermute(value, axis, [(source, (source + steps) % count) for source...  25.4 us
    ppermute x22, starting transfers between devices, passed_along(): lax.ppermute(value, axis, [(source, (source + steps) % count) for source...  19 us
    pallas_call x6, Pallas kernels, cross_back(): pl.pallas_call(partial(cross_kernel, s, per, packed), grid_spec=pltpu.Pre...  16.2 us
    pallas_call x2, Pallas kernels, sections(): pl.pallas_call(partial(section_kernel, s, steps, rotated), grid_spec=pltp...  6.3 us
    pallas_call x4, Pallas kernels, spectrum(): pl.pallas_call(partial(spectrum_kernel, s, per, packed), grid_spec=pltpu....  5.14 us
    pallas_call x3, Pallas kernels, peaks(): pl.pallas_call(partial(peak_kernel, s, last), grid_spec=pltpu.PrefetchSca...  5.13 us
    unnamed x28, local copies, waits for them, and re-layouts  5.12 us
  transfers between devices with their start and end apart: 22, of which 6 were waited for; matrix products, arithmetic and copies ran while one was open for 0% of the time, Pallas kernels for 33%

commit v1 on v0

v1 whole, which is shorter than its diff:
```python
from functools import partial
import math

import jax
import jax.numpy as jnp
import ml_dtypes
import numpy as np
from jax import lax
from jax.experimental import pallas as pl
from jax.experimental.pallas import tpu as pltpu
from jax.sharding import PartitionSpec as P

REC_STEPS = 3
LIG_STEPS = 2
MIB = 1024 * 1024
F32 = jnp.float32
BF16 = jnp.bfloat16


def trig(cells):
    phases = np.arange(cells)[:, None] * np.arange(cells)[None, :] % cells
    angles = phases * (2.0 * math.pi / cells)
    pair = []
    for table in (np.cos(angles), np.sin(angles)):
        table = np.where(np.abs(table) < 1e-9, 0.0, table)
        pair.append(table.astype(np.float32).astype(ml_dtypes.bfloat16).astype(np.float32))
    return pair


def complex_rows(real, imag):
    return np.block([[real, -imag], [imag, real]])


def build_tables(cells, channels, slab, cores):
    cosine, sine = trig(cells)
    half = cells // 2
    own = half // cores
    sign = np.where(np.arange(cells) % 2 == 0, 1.0, -1.0).astype(np.float32)
    tables = {}

    def half_rows(core):
        order = [(core + turn) % cores * own + j for turn in range(cores) for j in range(own)]
        real = cosine[order].copy()
        imag = -sine[order]
        imag[order.index(0)] = sign
        return np.concatenate([real, imag], axis=0)

    def half_mix(core):
        order = [(core + turn) % cores * own + j for turn in range(cores) for j in range(own)]
        top = np.concatenate([cosine[order], sine[order]], axis=1)
        low = np.concatenate([-sine[order], cosine[order]], axis=1)
        at = order.index(0)
        one = np.ones(cells, np.float32)
        top[at] = np.concatenate([one, -sign])
        low[at] = np.concatenate([sign, one])
        return np.concatenate([top, low], axis=0)

    def flips(table, width):
        blocks = table.reshape(table.shape[0], -1, width)
        return np.stack([table, blocks[:, :, ::-1].reshape(table.shape)])

    two = np.eye(2, dtype=np.float32)
    full_rows = np.concatenate([cosine, -sine], axis=0)
    forward = complex_rows(cosine, -sine)
    inverse = complex_rows(cosine, sine)
    tables["z_even"] = np.stack([flips(np.kron(two, half_rows(core)), cells) for core in range(cores)], axis=1)
    tables["y_even"] = flips(forward, cells)
    tables["y_odd"] = flips(np.kron(two, full_rows), cells)
    tables["z_odd"] = np.stack([flips(half_mix(core), cells) for core in range(cores)], axis=1)

    spread = []
    for core in range(cores):
        blocks = []
        for turn in range(cores):
            start = (core + turn) % cores * slab
            mix = forward.reshape(2, cells, 2, cells)[:, :, :, start:start + slab]
            for part in range(2):
                block = np.zeros((channels, slab, channels, 2, cells), np.float32)
                for channel in range(channels):
                    block[channel, :, channel] = mix[:, :, part].transpose(2, 0, 1)
                blocks.append(block.reshape(channels * slab, channels * 2 * cells))
        spread.append(np.concatenate(blocks, axis=0))
    tables["x_forward"] = np.stack(spread)

    mirror = np.zeros((cells, cells), np.float32)
    mirror[np.arange(cells), -np.arange(cells) % cells] = 1.0
    eye = np.eye(cells, dtype=np.float32)
    none = np.zeros((cells, cells), np.float32)
    low = 0.5 * np.block([[eye + mirror, none], [none, eye - mirror]])
    high = 0.5 * np.block([[none, eye + mirror], [mirror - eye, none]])
    plain = np.eye(2 * cells, dtype=np.float32)
    tables["unpack"] = np.stack(
        [np.concatenate([low, high] if core == 0 else [plain, 0.0 * plain], axis=0) for core in range(cores)]
    )

    back = []
    for core in range(cores):
        block = np.zeros((LIG_STEPS, 2, cells, 2, cores, LIG_STEPS, slab), np.float32)
        parts = inverse.reshape(2, cells, 2, cells)
        for turn in range(cores):
            start = (core + turn) % cores * slab
            for pose in range(LIG_STEPS):
                block[pose, :, :, :, turn, pose] = parts[:, start:start + slab].transpose(2, 3, 0, 1)
        back.append(block.reshape(LIG_STEPS * 2 * cells, 2 * cores * LIG_STEPS * slab))
    tables["x_inverse"] = np.stack(back)
    tables["y_inverse"] = inverse

    last = []
    for core in range(cores):
        order = [(core + turn) % cores * own + j for turn in range(cores) for j in range(own)]
        real = 2.0 * cosine[order]
        imag = -2.0 * sine[order]
        at = order.index(0)
        real[at] = 1.0
        imag[at] = sign
        last.append(np.stack([real, imag], axis=1).reshape(2 * half, cells).T)
    tables["z_inverse"] = np.stack(last)
    return {name: jnp.asarray(table.astype(ml_dtypes.bfloat16)) for name, table in tables.items()}


COST = pl.CostEstimate(flops=1000, bytes_accessed=1000, transcendentals=0)


def params(limit=24):
    return pltpu.CompilerParams(vmem_limit_bytes=limit * MIB)


def lines(value):
    return value.astype(F32).astype(BF16)


def dot(left, right):
    return jnp.dot(left, right, preferred_element_type=F32)


def dot_lanes(left, right):
    return lax.dot_general(left, right, (((1,), (1,)), ((), ())), preferred_element_type=F32)


def place(cuts, plane):
    return max(k for k in range(len(cuts) - 1) if cuts[k] <= plane)


class Sizes:
    def __init__(self, channels, slab, plane, cores):
        self.channels, self.slab, self.cores = channels, slab, cores
        self.cells = slab * cores
        self.lanes = channels * slab
        self.fold = self.lanes // self.cells
        self.tiles = plane // self.lanes
        self.own = self.cells // 2 // cores
        self.halves = (0, self.own)
        self.whole = (0, self.own)
        self.size = 2 * self.cells
        self.extra = 16
        self.back = cores * LIG_STEPS * slab


def section_kernel(s, pieces, rotated, cuts, occ, scalar, *refs):
    cells, lanes = s.cells, s.lanes
    half, size = cells // 2, s.size
    count = 4 if rotated else 2
    hbm, refs = refs[:count], refs[count:]
    outs, refs = refs[:len(cuts)], refs[len(cuts):]
    small, buffer, held = refs[:3]
    tables = refs[3:3 + count]
    turned = refs[-2] if rotated else None
    sems = refs[-1]
    core = lax.axis_index("fft")

    first = pltpu.make_async_copy(scalar, small, sems.at[0])
    first.start()
    if rotated:
        first.wait()
        turns = small[0]
        is_odd = turns % 2 == 1
        picks = (
            hbm[0].at[turns // 2, core],
            hbm[1].at[turns // 2],
            hbm[2].at[jnp.where(turns == 1, 1, 0)],
            hbm[3].at[jnp.where(turns == 3, 1, 0), core],
        )
    else:
        picks = (hbm[0].at[0, core], hbm[1].at[0])
    loads = [pltpu.make_async_copy(pick, table, sems.at[1 + k]) for k, (pick, table) in enumerate(zip(picks, tables))]
    width = s.tiles // pieces * lanes
    for k in range(pieces):
        here = slice(k * width, (k + 1) * width)
        loads.append(pltpu.make_async_copy(occ.at[0, :, :, here], buffer.at[:, :, here], sems.at[1 + count + k]))
    for load in loads:
        load.start()
    for load in loads[:count]:
        load.wait()

    def lay(table, height, step):
        for tile in range(0, s.tiles, 2):
            rows = [
                lines(buffer[:, :, (tile + k) * lanes:(tile + k + 1) * lanes].reshape(lanes, lanes)) for k in range(2)
            ]
            done = dot_lanes(table[...], jnp.concatenate(rows, axis=0))
            for k in range(2):
                for fold in range(s.fold):
                    at = ((tile + k) * s.fold + fold) * step
                    held[at:at + height, :] = done[fold * height:(fold + 1) * height, k * lanes:(k + 1) * lanes]

    def column(ref, at, step):
        return ref[pl.ds(at, cells, stride=step), :]

    def put(index, value):
        group, plane = divmod(index, s.own)
        if group == 0:
            outs[0][plane * size:(plane + 1) * size, :] = value
            return
        cut = place(cuts, plane)
        plane -= cuts[cut]
        outs[1 + cut][plane * size:(plane + 1) * size, :] = value

    def even():
        step = cells + 8
        for load in loads[count:]:
            load.wait()
        lay(tables[0], cells, step)
        for pair in range(0, half, 2):
            rows = [
                jnp.concatenate([column(held, q * half + pair + k, step) for q in range(2)], axis=0) for k in range(2)
            ]
            done = dot(tables[1][...], jnp.concatenate(rows, axis=1).astype(BF16)).astype(BF16)
            for k in range(2):
                put(pair + k, done[:, k * lanes:(k + 1) * lanes])

    def odd():
        step, short = size + 8, cells + 8
        for load in loads[count:]:
            load.wait()
        lay(tables[2], size, step)
        for pair in range(0, cells, 2):
            rows = [
                jnp.concatenate([column(held, q * cells + pair + k, step) for q in range(2)], axis=0) for k in range(2)
            ]
            done = dot(tables[3][...], jnp.concatenate(rows, axis=1).astype(BF16))
            for k in range(2):
                turned[(pair + k) * short:(pair + k) * short + cells, :] = done[:, k * lanes:(k + 1) * lanes]
        for plane in range(half):
            both = [column(turned, q * half + plane, short) for q in range(2)]
            put(plane, jnp.concatenate(both, axis=0).astype(BF16))

    if rotated:
        pl.when(jnp.logical_not(is_odd))(even)
        pl.when(is_odd)(odd)
    else:
        even()
        first.wait()
        outs[0][s.own * size:, :] = jnp.full((s.extra, lanes), small[0].astype(F32)).astype(BF16)


def sections(s, t, occ, scalar, rotated, cuts, pieces=2):
    cells, lanes = s.cells, s.lanes
    names = ["z_even", "y_even"] + (["y_odd", "z_odd"] if rotated else [])
    hbm = pl.BlockSpec(memory_space=pltpu.HBM)
    pin = lambda value: pltpu.with_memory_space_constraint(value, pltpu.HBM)
    scratch = [
        pltpu.SMEM(scalar.shape, jnp.int32),
        pltpu.VMEM(occ.shape[1:], jnp.int32),
        pltpu.VMEM((cells * ((s.size if rotated else cells) + 8), lanes), F32),
    ]
    scratch += [pltpu.VMEM(t[name].shape[-2:], BF16) for name in names]
    if rotated:
        scratch.append(pltpu.VMEM((cells * (cells + 8), lanes), F32))
    scratch.append(pltpu.SemaphoreType.DMA((1 + len(names) + pieces,)))
    rows = [s.own * s.size + (0 if rotated else s.extra)]
    rows += [(high - low) * s.size for low, high in zip(cuts, cuts[1:])]
    return pl.pallas_call(
        partial(section_kernel, s, pieces, rotated, cuts),
        in_specs=[hbm, pl.BlockSpec(memory_space=pl.ANY)] + [hbm] * len(names),
        out_specs=[pl.BlockSpec(memory_space=pltpu.VMEM)] * len(rows),
        out_shape=[jax.ShapeDtypeStruct((count, lanes), BF16) for count in rows],
        scratch_shapes=scratch,
        compiler_params=params(),
        cost_estimate=COST,
    )(pin(occ), scalar, *[pin(t[name]) for name in names])


def x_rows(s, cuts, own, others, plane):
    cut = place(cuts, plane)
    parts = []
    for ref, at in ((own, plane * s.size), (others[cut], (plane - cuts[cut]) * s.size)):
        for p in range(2):
            parts.append(ref[at + p * s.cells:at + (p + 1) * s.cells, :])
    return jnp.concatenate(parts, axis=1)


def unpacked_rows(s, own, others, unpack):
    cells = s.cells
    done = [dot(unpack, ref[:s.size, :]).astype(BF16) for ref in (own, others[0])]
    return [
        jnp.concatenate(
            [value[(2 * k + p) * cells:(2 * k + p + 1) * cells] for value in done for p in range(2)], axis=1
        )
        for k in range(2)
    ]


def spectrum_kernel(s, cuts, per, weight, table, unpack, own, *refs):
    others, (main, last) = refs[:-2], refs[-2:]
    volume = 1.0 / float(s.cells) ** 3
    core = lax.axis_index("fft")

    def put(ref, at, value):
        for channel in range(s.channels):
            lanes = slice(channel * s.size, (channel + 1) * s.size)
            ref[at:at + value.shape[0], lanes] = (value[:, lanes] * (weight[channel] * volume)).astype(BF16)

    for start in range(0, s.own, per):
        rows = [x_rows(s, cuts, own, others, plane) for plane in range(start, start + per)]
        if start == 0:
            rows[0], high = unpacked_rows(s, own, others, unpack[core])
            rows.append(high)
        done = dot(jnp.concatenate(rows, axis=0), table[core])
        put(main, start * s.cells, done[:per * s.cells])
        if start == 0:
            put(last, 0, done[per * s.cells:])


def spectrum(s, t, weight, own, others, cuts, per=4):
    width = s.channels * s.size
    vmem = pl.BlockSpec(memory_space=pltpu.VMEM)
    return pl.pallas_call(
        partial(spectrum_kernel, s, cuts, per),
        in_specs=[pl.BlockSpec(memory_space=pltpu.SMEM)] + [vmem] * (3 + len(others)),
        out_specs=[vmem] * 2,
        out_shape=[jax.ShapeDtypeStruct((s.own * s.cells, width), BF16), jax.ShapeDtypeStruct((s.cells, width), BF16)],
        compiler_params=params(),
        cost_estimate=COST,
    )(weight, t["x_forward"], t["unpack"], own, *others)


def cross_kernel(s, cuts, planes, per, table, unpack, x_inverse, y_inverse, *refs):
    poses, tops = refs[:LIG_STEPS], refs[LIG_STEPS:2 * LIG_STEPS]
    own, others = refs[2 * LIG_STEPS], refs[2 * LIG_STEPS + 1:-2]
    keep, send = refs[-2:]
    cells, width, lanes = s.cells, s.size, s.back
    core = lax.axis_index("fft")
    lane = lax.broadcasted_iota(jnp.int32, (cells, width), 1)
    is_real = lane < cells
    kept = lax.broadcasted_iota(jnp.int32, (cells // 2, lanes), 1) < lanes // 2

    def correlate(receptor, pose):
        straight = None
        for channel in range(s.channels):
            here = slice(channel * width, (channel + 1) * width)
            one = receptor[:, here]
            two = pose[:, here].astype(F32)
            terms = (one * two, pltpu.roll(one, cells, 1) * two)
            straight = terms if straight is None else (straight[0] + terms[0], straight[1] + terms[1])
        same, turned = straight
        return jnp.where(is_real, same + pltpu.roll(same, cells, 1), pltpu.roll(turned, cells, 1) - turned)

    for start in range(planes[0], planes[1], per):
        rows = [x_rows(s, cuts, own, others, plane) for plane in range(start, start + per)]
        if start == 0:
            rows[0], high = unpacked_rows(s, own, others, unpack[core])
            rows.append(high)
        done = dot(jnp.concatenate(rows, axis=0), table[core])
        cross = []
        for k in range(per):
            both = []
            for pose in range(LIG_STEPS):
                at = (start + k) * cells
                value = correlate(done[k * cells:(k + 1) * cells], poses[pose][at:at + cells, :])
                if start + k == 0:
                    row = lax.broadcasted_iota(jnp.int32, (cells, width), 0)
                    at_zero = (row == 0) & ((lane == 0) | (lane == cells)) & (core == 0)
                    value = jnp.where(at_zero, 0.0, value)
                    top = pltpu.roll(correlate(done[per * cells:], tops[pose][...]), cells, 1)
                    value = value + jnp.where(is_real, -top, top)
                both.append(value.astype(BF16))
            cross.append(jnp.concatenate(both, axis=1))
        back = dot(jnp.concatenate(cross, axis=0), x_inverse[core]).astype(BF16)
        for pair in range(0, per, 2):
            sides = []
            for k in range(2):
                here = back[(pair + k) * cells:(pair + k + 1) * cells]
                sides.append(jnp.concatenate([here[:, :lanes], here[:, lanes:]], axis=0))
            out = dot(y_inverse[...], jnp.concatenate(sides, axis=1))
            for k in range(2):
                for q in range(2):
                    value = out[q * cells:(q + 1) * cells, k * lanes:(k + 1) * lanes]
                    low, high = value[:cells // 2], value[cells // 2:]
                    at = (start - planes[0] + pair + k) * cells + q * cells // 2
                    at = slice(at, at + cells // 2)
                    keep[at, :] = jnp.where(kept, low, pltpu.roll(high, lanes // 2, 1)).astype(BF16)
                    send[at, :] = jnp.where(kept, pltpu.roll(low, lanes // 2, 1), high).astype(BF16)


def cross_back(s, t, own, others, poses, tops, cuts, planes, per=4):
    vmem = pl.BlockSpec(memory_space=pltpu.VMEM)
    shape = jax.ShapeDtypeStruct(((planes[1] - planes[0]) * s.cells, s.back), BF16)
    operands = [t["x_forward"], t["unpack"], t["x_inverse"], t["y_inverse"], *poses, *tops, own, *others]
    return pl.pallas_call(
        partial(cross_kernel, s, cuts, planes, per),
        in_specs=[vmem] * len(operands),
        out_specs=[vmem] * 2,
        out_shape=[shape] * 2,
        compiler_params=params(),
        cost_estimate=COST,
    )(*operands)


def peak_kernel(s, count, last, load, table, *refs):
    parts = refs[:count]
    earlier, out, held = refs[count:-2], refs[-2], refs[-1]
    cells = s.cells
    low = cells // 2
    core = lax.axis_index("fft")
    at = 0
    for part in parts:
        held[at:at + part.shape[0], :] = part[...].astype(F32)
        at += part.shape[0]
    best = None
    for pair in range(0, low, 2):
        columns = [held[pl.ds(pair + k, cells, stride=low), :] for k in range(2)]
        scores = dot(table[core], jnp.concatenate(columns, axis=1).astype(BF16))
        here = jnp.maximum(scores[:, :s.back], scores[:, s.back:])
        best = here if best is None else jnp.maximum(best, here)
    row = jnp.max(best, axis=0, keepdims=True)
    row = jnp.maximum(row, pltpu.roll(row, s.back // 2, 1)) * (1.0 / (cells * math.sqrt(cells)))
    plane = lax.broadcasted_iota(jnp.int32, row.shape, 1) % s.slab + core * s.slab
    extent = load[s.own * s.size:s.own * s.size + 1, :].astype(F32)
    row = jnp.where(plane.astype(F32) < extent, row, 0.0)
    if not last:
        out[...] = row
        return
    for index, value in enumerate([ref[...] for ref in earlier] + [row]):
        for pose in range(LIG_STEPS):
            out[0, index, pose:pose + 1, :] = value[:, pose * s.slab:(pose + 1) * s.slab]


def peaks(s, t, load, parts, earlier, last):
    vmem = pl.BlockSpec(memory_space=pltpu.VMEM)
    shape = (1, REC_STEPS, LIG_STEPS, s.slab) if last else (1, s.back)
    return pl.pallas_call(
        partial(peak_kernel, s, len(parts), last),
        in_specs=[vmem] * (2 + len(parts) + len(earlier)),
        out_specs=vmem,
        out_shape=jax.ShapeDtypeStruct(shape, F32),
        scratch_shapes=[pltpu.VMEM((s.cells * s.cells // 2, s.back), F32)],
        compiler_params=params(),
        cost_estimate=COST,
    )(load, t["z_inverse"], *parts, *earlier)


def passed_along(value, axis, steps=1):
    count = lax.axis_size(axis)
    return lax.ppermute(value, axis, [(source, (source + steps) % count) for source in range(count)])


def passed_across(value, axis):
    count, cores = lax.axis_size(axis), lax.axis_size("fft")
    pairs = [
        (place * cores + core, (place + 1) % count * cores + (core + 1) % cores)
        for place in range(count)
        for core in range(cores)
    ]
    return lax.ppermute(value, (axis, "fft"), pairs)


def after(value, *others):
    return lax.optimization_barrier((value, *others))[0]


def shards(tables, receptor_occupancy, ligand_occupancy, rot_index, receptor_extent, channel_weight):
    _, channels, slab, plane = receptor_occupancy.shape
    s = Sizes(channels, slab, plane, lax.axis_size("fft"))
    t = tables(s)
    swapped = lambda parts: [passed_along(part, "fft") for part in parts]

    own, *away = sections(s, t, receptor_occupancy, receptor_extent, False, s.halves)
    others = swapped(away)
    receptors = [(own, others)]
    receptors.append((passed_along(own, "rec"), [passed_across(part, "rec") for part in away]))

    ligand_occupancy = after(ligand_occupancy, *others)
    pose, *pose_away = sections(s, t, ligand_occupancy, rot_index, True, s.whole)
    pose_others = swapped(pose_away)
    next_pose, next_others = passed_along(pose, "lig"), [passed_across(part, "lig") for part in pose_away]
    spectra = [spectrum(s, t, channel_weight, pose, pose_others, s.whole)]

    own, others = receptors[1]
    own = after(own, spectra[0][0])
    receptors[1] = (own, others)
    receptors.append((passed_along(own, "rec"), [passed_along(part, "rec") for part in others]))

    spectra.append(spectrum(s, t, channel_weight, next_pose, next_others, s.whole))
    poses, tops = [main for main, _ in spectra], [top for _, top in spectra]

    rows = []
    for step, (own, others) in enumerate(receptors):
        last = step + 1 == REC_STEPS
        ranges = list(zip(s.halves, s.halves[1:])) if last else [s.whole]
        if last:
            own = after(own, *rows)
        sides = [cross_back(s, t, own, others, poses, tops, s.halves, planes) for planes in ranges]
        parts = [keep for keep, _ in sides] + swapped([send for _, send in sides])
        rows.append(peaks(s, t, own, parts, rows if last else [], last))
    return rows[-1]


def solution(mesh):
    placed = (
        P(("groups", "rec", "lig"), None, "fft", None),
        P(("groups", "rec", "lig"), None, "fft", None),
        P(("groups", "rec", "lig")),
        P(("groups", "rec", "lig")),
        P(),
    )
    tables = lambda s: build_tables(s.cells, s.channels, s.slab, s.cores)
    return jax.shard_map(
        partial(shards, tables),
        mesh=mesh,
        in_specs=placed,
        out_specs=P(("groups", "rec", "lig"), None, None, "fft"),
        check_vma=False,
    )
```

time: 84.2 us -> 61.6 us (0.73)
  starting transfers between devices: 19 us -> 7.56 us
  Pallas kernels: 32.8 us -> 22.7 us
  local copies, waits for them, and re-layouts: 5.12 us -> 0.03 us
  waiting for transfers between devices: 25.4 us -> 29.7 us
    ppermute x0 -> x2, waiting for transfers between devices: none -> 16 us  [passed_across(): return lax.ppermute(value, (axis, 'fft'), pairs)]
    ppermute x22 -> x9, starting transfers between devices: 19 us -> 6 us  [passed_along(): lax.ppermute(value, axis, [(source, (source + steps) % count) for source...]
    ppermute x22 -> x9, waiting for transfers between devices: 25.4 us -> 13.6 us  [passed_along(): lax.ppermute(value, axis, [(source, (source + steps) % count) for source...]
    pallas_call x15 -> x10, Pallas kernels: 32.8 us -> 22.7 us  [the longest x3 9.65 us: cross_back(): pl.pallas_call(partial(cross_kernel, s, cuts, planes, per), in_specs=[vme...]
    unnamed x28 -> x12, local copies, waits for them, and re-layouts: 5.12 us -> 0.03 us
    ppermute x0 -> x2, starting transfers between devices: none -> 1.57 us  [passed_across(): return lax.ppermute(value, (axis, 'fft'), pairs)]
  transfers between devices with their start and end apart: 22 -> 11, of which waited for: 6 -> 6; matrix products, arithmetic and copies ran while one was open for 0% -> 0% of each run, Pallas kernels for 33% -> 25%
where the time goes in v1:
time: 61.6 us; the launch traced here: 61.4 us
  waiting for transfers between devices  29.7 us (48%)
  Pallas kernels  22.7 us (37%)
  starting transfers between devices  7.56 us (12%)
  between operations  1.45 us (2%)
    ppermute x2, waiting for transfers between devices, passed_across(): return lax.ppermute(value, (axis, 'fft'), pairs)  16 us
    ppermute x9, waiting for transfers between devices, passed_along(): lax.ppermute(value, axis, [(source, (source + steps) % count) for source...  13.6 us
    pallas_call x3, Pallas kernels, cross_back(): pl.pallas_call(partial(cross_kernel, s, cuts, planes, per), in_specs=[vme...  9.65 us
    pallas_call x2, Pallas kernels, sections(): pl.pallas_call(partial(section_kernel, s, pieces, rotated, cuts), in_spec...  6.73 us
    ppermute x9, starting transfers between devices, passed_along(): lax.ppermute(value, axis, [(source, (source + steps) % count) for source...  6 us
    pallas_call x3, Pallas kernels, peaks(): pl.pallas_call(partial(peak_kernel, s, len(parts), last), in_specs=[vmem]...  3.51 us
    pallas_call x2, Pallas kernels, spectrum(): pl.pallas_call(partial(spectrum_kernel, s, cuts, per), in_specs=[pl.Block...  2.8 us
    ppermute x2, starting transfers between devices, passed_across(): return lax.ppermute(value, (axis, 'fft'), pairs)  1.57 us
  transfers between devices with their start and end apart: 11, of which 6 were waited for; matrix products, arithmetic and copies ran while one was open for 0% of the time, Pallas kernels for 25%

profile of v1, /device:TPU:0, one launch (start us, length us, event | category | flops | bytes accessed | tf_op | source)
XLA Modules:
  0.0 61.4 jit_solution(555952524578724045)
XLA Ops:
  0.7 2.7 %shard_map.136 = (bf16[2064,128]{1,0:T(8,128)(2,1)S(1)}, bf16[2048,128]{1,0:T(8,128)(2,1)S(1)}) custom-call(s32[1,4,32,4096]{3,2,1,0:T(8,128)} %occ.1, s32[1]{0:T(128)S(6)} %copy.16.scalar, bf16[2,2,128,128]{3,2,1,0:T(8,128)(2,1)} %constant.18.clone.refs_0_, bf16[2,128,128]{2,1,0:T(8,128)(2,1)} %constant.19.clone.refs_1_), custom_call_target="tpu_custom_call" | custom-call | flops 1000 | bytes 1000 | tf_op jit(solution)/shard_map/pallas_call | solution.py:272
  3.4 0.5 collective-permute-start.1
  3.9 2.6 %collective-permute-start = (bf16[2064,128]{1,0:T(8,128)(2,1)S(1)}, bf16[2064,128]{1,0:T(8,128)(2,1)S(1)}, u32[]{:S(2)}, u32[]{:S(2)}) collective-permute-start(bf16[2064,128]{1,0:T(8,128)(2,1)S(1)} %get-tuple-element.22.refs_4_.load), channel_id=1, source_target_pairs={{0,4},{4,8},{8,12},{12,0},{1,5},{5,9},{9,13},{13,1},{2,6},{6,10},{... | collective-permute-start | bytes 1585160 | tf_op jit(solution)/shard_map/ppermute | solution.py:454
  7.2 4.0 %shard_map.137 = (bf16[2048,128]{1,0:T(8,128)(2,1)S(1)}, bf16[2048,128]{1,0:T(8,128)(2,1)S(1)}) custom-call(s32[1,4,32,4096]{3,2,1,0:T(8,128)} %occ.2, s32[1]{0:T(128)S(6)} %copy.15.scalar, bf16[2,2,128,128]{3,2,1,0:T(8,128)(2,1)} %constant.18.clone.refs_0_, bf16[2,128,128]{2,1,0:T(8,128)(2,1)} %constant.19.clone.refs_1_, ...), custom_call_target="tpu_custom_call" | custom-call | flops 1000 | bytes 1000 | tf_op jit(solution)/shard_map/pallas_call | solution.py:272
  11.3 0.2 collective-permute-start.2
  11.5 1.5 %collective-permute-start.7 = (bf16[2048,128]{1,0:T(8,128)(2,1)S(1)}, bf16[2048,128]{1,0:T(8,128)(2,1)S(1)}, u32[]{:S(2)}, u32[]{:S(2)}) collective-permute-start(bf16[2048,128]{1,0:T(8,128)(2,1)S(1)} %get-tuple-element.23), channel_id=1, source_target_pairs={{0,5},{1,4},{4,9},{5,8},{8,13},{9,12},{12,1},{13,0},{2,7},{3,6},{6... | collective-permute-start | bytes 1572872 | tf_op jit(solution)/shard_map/ppermute | solution.py:464
  13.0 1.5 %collective-permute-start.4 = (bf16[2048,128]{1,0:T(8,128)(2,1)S(1)}, bf16[2048,128]{1,0:T(8,128)(2,1)S(1)}, u32[]{:S(2)}, u32[]{:S(2)}) collective-permute-start(bf16[2048,128]{1,0:T(8,128)(2,1)S(1)} %get-tuple-element.25.own), channel_id=1, source_target_pairs={{0,2},{2,0},{1,3},{3,1},{4,6},{6,4},{5,7},{7,5},{8,10},{10,8},{9,1... | collective-permute-start | bytes 1572872 | tf_op jit(solution)/shard_map/ppermute | solution.py:454
  14.6 1.4 %shard_map.138 = (bf16[1024,512]{1,0:T(8,128)(2,1)S(1)}, bf16[64,512]{1,0:T(8,128)(2,1)S(1)}) custom-call(f32[4]{0:T(128)S(1)} %copy-done.5, bf16[2,512,512]{2,1,0:T(8,128)(2,1)S(1)} %copy-done, bf16[2,256,128]{2,1,0:T(8,128)(2,1)S(1)} %copy-done.1, bf16[2048,128]{1,0:T(8,128)(2,1)S(1)} %get-tuple-element.25.own, ...), custom_call_target="tpu_custom_call" | custom-call | flops 1000 | bytes 1000 | tf_op jit(solution)/shard_map/pallas_call | solution.py:327
  16.0 5.5 %collective-permute-done.refs_4_.load = bf16[2064,128]{1,0:T(8,128)(2,1)S(1)} collective-permute-done((bf16[2064,128]{1,0:T(8,128)(2,1)S(1)}, bf16[2064,128]{1,0:T(8,128)(2,1)S(1)}, u32[]{:S(2)}, u32[]{:S(2)}) %collective-permute-start) | collective-permute-done | bytes 528416 | tf_op jit(solution)/shard_map/ppermute | solution.py:454
  21.4 10.7 %collective-permute-done.7.refs_5_ = bf16[2048,128]{1,0:T(8,128)(2,1)S(1)} collective-permute-done((bf16[2048,128]{1,0:T(8,128)(2,1)S(1)}, bf16[2048,128]{1,0:T(8,128)(2,1)S(1)}, u32[]{:S(2)}, u32[]{:S(2)}) %collective-permute-start.7) | collective-permute-done | bytes 524320 | tf_op jit(solution)/shard_map/ppermute | solution.py:464
  32.2 5.3 %collective-permute-done.5.refs_0_ = bf16[2048,128]{1,0:T(8,128)(2,1)S(1)} collective-permute-done((bf16[2048,128]{1,0:T(8,128)(2,1)S(1)}, bf16[2048,128]{1,0:T(8,128)(2,1)S(1)}, u32[]{:S(2)}, u32[]{:S(2)}) %collective-permute-start.5) | collective-permute-done | bytes 524320 | tf_op jit(solution)/shard_map/ppermute | solution.py:464
  37.5 1.4 %shard_map.139 = (bf16[1024,512]{1,0:T(8,128)(2,1)S(1)}, bf16[64,512]{1,0:T(8,128)(2,1)S(1)}) custom-call(f32[4]{0:T(128)S(1)} %copy-done.5, bf16[2,512,512]{2,1,0:T(8,128)(2,1)S(1)} %copy-done, bf16[2,256,128]{2,1,0:T(8,128)(2,1)S(1)} %copy-done.1, bf16[2048,128]{1,0:T(8,128)(2,1)S(1)} %collective-permute-done.4.own, ...), custom_call_target="tpu_custom_call" | custom-call | flops 1000 | bytes 1000 | tf_op jit(solution)/shard_map/pallas_call | solution.py:327
  38.9 3.2 %shard_map.142 = (bf16[1024,128]{1,0:T(8,128)(2,1)S(1)}, bf16[1024,128]{1,0:T(8,128)(2,1)S(1)}) custom-call(bf16[2,512,512]{2,1,0:T(8,128)(2,1)S(1)} %copy-done, bf16[2,256,128]{2,1,0:T(8,128)(2,1)S(1)} %copy-done.1, bf16[2,256,256]{2,1,0:T(8,128)(2,1)S(1)} %copy-done.2, bf16[128,128]{1,0:T(8,128)(2,1)S(1)} %copy-done.3, ...), custom_call_target="tpu_custom_call" | custom-call | flops 1000 | bytes 1000 | tf_op jit(solution)/shard_map/pallas_call | solution.py:399
  42.1 1.0 %collective-permute-start.8 = (bf16[1024,128]{1,0:T(8,128)(2,1)S(1)}, bf16[1024,128]{1,0:T(8,128)(2,1)S(1)}, u32[]{:S(2)}, u32[]{:S(2)}) collective-permute-start(bf16[1024,128]{1,0:T(8,128)(2,1)S(1)} %get-tuple-element.35), channel_id=1, source_target_pairs={{0,1},{1,0},{2,3},{3,2},{4,5},{5,4},{6,7},{7,6},{8,9},{9,8},{10,11... | collective-permute-start | bytes 786440 | tf_op jit(solution)/shard_map/ppermute | solution.py:454
  43.1 3.2 %shard_map.140 = (bf16[1024,128]{1,0:T(8,128)(2,1)S(1)}, bf16[1024,128]{1,0:T(8,128)(2,1)S(1)}) custom-call(bf16[2,512,512]{2,1,0:T(8,128)(2,1)S(1)} %copy-done, bf16[2,256,128]{2,1,0:T(8,128)(2,1)S(1)} %copy-done.1, bf16[2,256,256]{2,1,0:T(8,128)(2,1)S(1)} %copy-done.2, bf16[128,128]{1,0:T(8,128)(2,1)S(1)} %copy-done.3, ...), custom_call_target="tpu_custom_call" | custom-call | flops 1000 | bytes 1000 | tf_op jit(solution)/shard_map/pallas_call | solution.py:399
  46.3 0.1 collective-permute-start.6
  46.4 1.0 %shard_map.143.refs_3_ = f32[1,128]{1,0:T(1,128)S(1)} custom-call(bf16[2064,128]{1,0:T(8,128)(2,1)S(1)} %collective-permute-done.refs_4_.load, bf16[2,64,64]{2,1,0:T(8,128)(2,1)S(1)} %copy-done.4, bf16[1024,128]{1,0:T(8,128)(2,1)S(1)} %get-tuple-element.34.refs_0_, bf16[1024,128]{1,0:T(8,128)(2,1)S(1)} %collective-permute-done.8.refs_1_), custom_call_target="tpu_custom_call" | custom-call | flops 1000 | bytes 1000 | tf_op jit(solution)/shard_map/pallas_call | solution.py:441
  47.4 0.5 collective-permute-done.6.refs_1_
  47.9 0.9 %shard_map.141.refs_2_ = f32[1,128]{1,0:T(1,128)S(1)} custom-call(bf16[2064,128]{1,0:T(8,128)(2,1)S(1)} %get-tuple-element.22.refs_4_.load, bf16[2,64,64]{2,1,0:T(8,128)(2,1)S(1)} %copy-done.4, bf16[1024,128]{1,0:T(8,128)(2,1)S(1)} %get-tuple-element.32.refs_0_, bf16[1024,128]{1,0:T(8,128)(2,1)S(1)} %collective-permute-done.6.refs_1_), custom_call_target="tpu_custom_call" | custom-call | flops 1000 | bytes 1000 | tf_op jit(solution)/shard_map/pallas_call | solution.py:441
  48.9 6.1 %collective-permute-done.9.refs_5_ = bf16[2048,128]{1,0:T(8,128)(2,1)S(1)} collective-permute-done((bf16[2048,128]{1,0:T(8,128)(2,1)S(1)}, bf16[2048,128]{1,0:T(8,128)(2,1)S(1)}, u32[]{:S(2)}, u32[]{:S(2)}) %collective-permute-start.9) | collective-permute-done | bytes 524320 | tf_op jit(solution)/shard_map/ppermute | solution.py:454
  55.0 3.2 %shard_map.144 = (bf16[1024,128]{1,0:T(8,128)(2,1)S(1)}, bf16[1024,128]{1,0:T(8,128)(2,1)S(1)}) custom-call(bf16[2,512,512]{2,1,0:T(8,128)(2,1)S(1)} %copy-done, bf16[2,256,128]{2,1,0:T(8,128)(2,1)S(1)} %copy-done.1, bf16[2,256,256]{2,1,0:T(8,128)(2,1)S(1)} %copy-done.2, bf16[128,128]{1,0:T(8,128)(2,1)S(1)} %copy-done.3, ...), custom_call_target="tpu_custom_call" | custom-call | flops 1000 | bytes 1000 | tf_op jit(solution)/shard_map/pallas_call | solution.py:399
  58.2 0.1 collective-permute-start.10
  58.3 1.5 %collective-permute-done.10.refs_1_ = bf16[1024,128]{1,0:T(8,128)(2,1)S(1)} collective-permute-done((bf16[1024,128]{1,0:T(8,128)(2,1)S(1)}, bf16[1024,128]{1,0:T(8,128)(2,1)S(1)}, u32[]{:S(2)}, u32[]{:S(2)}) %collective-permute-start.10) | collective-permute-done | bytes 262176 | tf_op jit(solution)/shard_map/ppermute | solution.py:454
  59.8 1.6 %shard_map.145 = f32[1,3,2,32]{3,2,1,0:T(2,128)} custom-call(bf16[2064,128]{1,0:T(8,128)(2,1)S(1)} %collective-permute-done.3.refs_4_.load, bf16[2,64,64]{2,1,0:T(8,128)(2,1)S(1)} %copy-done.4, bf16[1024,128]{1,0:T(8,128)(2,1)S(1)} %get-tuple-element.37.refs_0_, bf16[1024,128]{1,0:T(8,128)(2,1)S(1)} %collective-permute-done.10.refs_1_, ...), custom_call_target="tpu_custom_call" | custom-call | flops 1000 | bytes 1000 | tf_op jit(solution)/shard_map/pallas_call | solution.py:441
  (20 shorter events, 0.1 us)
Async XLA Ops:
  0.7 13.9 %copy-start = (bf16[2,512,512]{2,1,0:T(8,128)(2,1)S(1)}, bf16[2,512,512]{2,1,0:T(8,128)(2,1)}, u32[]{:S(2)}) copy-start(bf16[2,512,512]{2,1,0:T(8,128)(2,1)} %constant.22.clone.table) | copy-start | bytes 3145732
  0.7 13.9 %copy-start.1 = (bf16[2,256,128]{2,1,0:T(8,128)(2,1)S(1)}, bf16[2,256,128]{2,1,0:T(8,128)(2,1)}, u32[]{:S(2)}) copy-start(bf16[2,256,128]{2,1,0:T(8,128)(2,1)} %constant.23.clone.unpack) | copy-start | bytes 393220
  0.7 13.9 %copy-start.5 = (f32[4]{0:T(128)S(1)}, f32[4]{0:T(128)}, u32[]{:S(2)}) copy-start(f32[4]{0:T(128)} %weight.3) | copy-start | bytes 52
  3.4 3.8 %collective-permute-start.1 = (bf16[2048,128]{1,0:T(8,128)(2,1)S(1)}, bf16[2048,128]{1,0:T(8,128)(2,1)S(1)}, u32[]{:S(2)}, u32[]{:S(2)}) collective-permute-start(bf16[2048,128]{1,0:T(8,128)(2,1)S(1)} %get-tuple-element.23), channel_id=1, source_target_pairs={{0,1},{1,0},{2,3},{3,2},{4,5},{5,4},{6,7},{7,6},{8,9},{9,8},{10,11... | collective-permute-start | bytes 1572872 | tf_op jit(solution)/shard_map/ppermute | solution.py:454
  3.9 17.5 %collective-permute-start = (bf16[2064,128]{1,0:T(8,128)(2,1)S(1)}, bf16[2064,128]{1,0:T(8,128)(2,1)S(1)}, u32[]{:S(2)}, u32[]{:S(2)}) collective-permute-start(bf16[2064,128]{1,0:T(8,128)(2,1)S(1)} %get-tuple-element.22.refs_4_.load), channel_id=1, source_target_pairs={{0,4},{4,8},{8,12},{12,0},{1,5},{5,9},{9,13},{13,1},{2,6},{6,10},{... | collective-permute-start | bytes 1585160 | tf_op jit(solution)/shard_map/ppermute | solution.py:454
  11.3 3.3 %collective-permute-start.2 = (bf16[2048,128]{1,0:T(8,128)(2,1)S(1)}, bf16[2048,128]{1,0:T(8,128)(2,1)S(1)}, u32[]{:S(2)}, u32[]{:S(2)}) collective-permute-start(bf16[2048,128]{1,0:T(8,128)(2,1)S(1)} %get-tuple-element.26), channel_id=1, source_target_pairs={{0,1},{1,0},{2,3},{3,2},{4,5},{5,4},{6,7},{7,6},{8,9},{9,8},{10,11... | collective-permute-start | bytes 1572872 | tf_op jit(solution)/shard_map/ppermute | solution.py:454
  11.5 20.7 %collective-permute-start.7 = (bf16[2048,128]{1,0:T(8,128)(2,1)S(1)}, bf16[2048,128]{1,0:T(8,128)(2,1)S(1)}, u32[]{:S(2)}, u32[]{:S(2)}) collective-permute-start(bf16[2048,128]{1,0:T(8,128)(2,1)S(1)} %get-tuple-element.23), channel_id=1, source_target_pairs={{0,5},{1,4},{4,9},{5,8},{8,13},{9,12},{12,1},{13,0},{2,7},{3,6},{6... | collective-permute-start | bytes 1572872 | tf_op jit(solution)/shard_map/ppermute | solution.py:464
  13.0 25.9 %copy-start.2 = (bf16[2,256,256]{2,1,0:T(8,128)(2,1)S(1)}, bf16[2,256,256]{2,1,0:T(8,128)(2,1)}, u32[]{:S(2)}) copy-start(bf16[2,256,256]{2,1,0:T(8,128)(2,1)} %constant.24.clone.x_inverse) | copy-start | bytes 786436
  13.0 25.9 %copy-start.3 = (bf16[128,128]{1,0:T(8,128)(2,1)S(1)}, bf16[128,128]{1,0:T(8,128)(2,1)}, u32[]{:S(2)}) copy-start(bf16[128,128]{1,0:T(8,128)(2,1)} %constant.25.clone.y_inverse) | copy-start | bytes 98308
  13.0 19.2 %collective-permute-start.4 = (bf16[2048,128]{1,0:T(8,128)(2,1)S(1)}, bf16[2048,128]{1,0:T(8,128)(2,1)S(1)}, u32[]{:S(2)}, u32[]{:S(2)}) collective-permute-start(bf16[2048,128]{1,0:T(8,128)(2,1)S(1)} %get-tuple-element.25.own), channel_id=1, source_target_pairs={{0,2},{2,0},{1,3},{3,1},{4,6},{6,4},{5,7},{7,5},{8,10},{10,8},{9,1... | collective-permute-start | bytes 1572872 | tf_op jit(solution)/shard_map/ppermute | solution.py:454
  14.5 23.0 %collective-permute-start.5 = (bf16[2048,128]{1,0:T(8,128)(2,1)S(1)}, bf16[2048,128]{1,0:T(8,128)(2,1)S(1)}, u32[]{:S(2)}, u32[]{:S(2)}) collective-permute-start(bf16[2048,128]{1,0:T(8,128)(2,1)S(1)} %get-tuple-element.26), channel_id=1, source_target_pairs={{0,3},{1,2},{2,1},{3,0},{4,7},{5,6},{6,5},{7,4},{8,11},{9,10},{10,... | collective-permute-start | bytes 1572872 | tf_op jit(solution)/shard_map/ppermute | solution.py:464
  21.4 27.4 %collective-permute-start.3 = (bf16[2064,128]{1,0:T(8,128)(2,1)S(1)}, bf16[2064,128]{1,0:T(8,128)(2,1)S(1)}, u32[]{:S(2)}, u32[]{:S(2)}) collective-permute-start(bf16[2064,128]{1,0:T(8,128)(2,1)S(1)} %collective-permute-done.refs_4_.load), channel_id=1, source_target_pairs={{0,4},{4,8},{8,12},{12,0},{1,5},{5,9},{9,13},{13,1},{2,6},{6,10},{... | collective-permute-start | bytes 1585160 | tf_op jit(solution)/shard_map/ppermute | solution.py:454
  32.2 22.8 %collective-permute-start.9 = (bf16[2048,128]{1,0:T(8,128)(2,1)S(1)}, bf16[2048,128]{1,0:T(8,128)(2,1)S(1)}, u32[]{:S(2)}, u32[]{:S(2)}) collective-permute-start(bf16[2048,128]{1,0:T(8,128)(2,1)S(1)} %collective-permute-done.7.refs_5_), channel_id=1, source_target_pairs={{0,4},{4,8},{8,12},{12,0},{1,5},{5,9},{9,13},{13,1},{2,6},{6,10},{... | collective-permute-start | bytes 1572872 | tf_op jit(solution)/shard_map/ppermute | solution.py:454
  42.1 4.3 %copy-start.4 = (bf16[2,64,64]{2,1,0:T(8,128)(2,1)S(1)}, bf16[2,64,64]{2,1,0:T(8,128)(2,1)}, u32[]{:S(2)}) copy-start(bf16[2,64,64]{2,1,0:T(8,128)(2,1)} %constant.26.clone.table) | copy-start | bytes 49156
  42.1 4.3 %collective-permute-start.8 = (bf16[1024,128]{1,0:T(8,128)(2,1)S(1)}, bf16[1024,128]{1,0:T(8,128)(2,1)S(1)}, u32[]{:S(2)}, u32[]{:S(2)}) collective-permute-start(bf16[1024,128]{1,0:T(8,128)(2,1)S(1)} %get-tuple-element.35), channel_id=1, source_target_pairs={{0,1},{1,0},{2,3},{3,2},{4,5},{5,4},{6,7},{7,6},{8,9},{9,8},{10,11... | collective-permute-start | bytes 786440 | tf_op jit(solution)/shard_map/ppermute | solution.py:454
  46.3 1.6 %collective-permute-start.6 = (bf16[1024,128]{1,0:T(8,128)(2,1)S(1)}, bf16[1024,128]{1,0:T(8,128)(2,1)S(1)}, u32[]{:S(2)}, u32[]{:S(2)}) collective-permute-start(bf16[1024,128]{1,0:T(8,128)(2,1)S(1)} %get-tuple-element.33), channel_id=1, source_target_pairs={{0,1},{1,0},{2,3},{3,2},{4,5},{5,4},{6,7},{7,6},{8,9},{9,8},{10,11... | collective-permute-start | bytes 786440 | tf_op jit(solution)/shard_map/ppermute | solution.py:454
  58.2 1.6 %collective-permute-start.10 = (bf16[1024,128]{1,0:T(8,128)(2,1)S(1)}, bf16[1024,128]{1,0:T(8,128)(2,1)S(1)}, u32[]{:S(2)}, u32[]{:S(2)}) collective-permute-start(bf16[1024,128]{1,0:T(8,128)(2,1)S(1)} %get-tuple-element.38), channel_id=1, source_target_pairs={{0,1},{1,0},{2,3},{3,2},{4,5},{5,4},{6,7},{7,6},{8,9},{9,8},{10,11... | collective-permute-start | bytes 786440 | tf_op jit(solution)/shard_map/ppermute | solution.py:454

commit v2 on v1

--- a/solution.py
+++ b/solution.py
@@ -149,8 +149,8 @@
         self.fold = self.lanes // self.cells
         self.tiles = plane // self.lanes
         self.own = self.cells // 2 // cores
-        self.halves = (0, self.own)
         self.whole = (0, self.own)
+        self.parts = (0, self.own * 3 // 4, self.own)
         self.size = 2 * self.cells
         self.extra = 16
         self.back = cores * LIG_STEPS * slab
@@ -194,6 +194,8 @@
 
     def lay(table, height, step):
         for tile in range(0, s.tiles, 2):
+            if tile % (s.tiles // pieces) == 0:
+                loads[count + tile * pieces // s.tiles].wait()
             rows = [
                 lines(buffer[:, :, (tile + k) * lanes:(tile + k + 1) * lanes].reshape(lanes, lanes)) for k in range(2)
             ]
@@ -217,8 +219,6 @@
 
     def even():
         step = cells + 8
-        for load in loads[count:]:
-            load.wait()
         lay(tables[0], cells, step)
         for pair in range(0, half, 2):
             rows = [
@@ -230,8 +230,6 @@
 
     def odd():
         step, short = size + 8, cells + 8
-        for load in loads[count:]:
-            load.wait()
         lay(tables[2], size, step)
         for pair in range(0, cells, 2):
             rows = [
@@ -395,6 +393,8 @@
 def cross_back(s, t, own, others, poses, tops, cuts, planes, per=4):
     vmem = pl.BlockSpec(memory_space=pltpu.VMEM)
     shape = jax.ShapeDtypeStruct(((planes[1] - planes[0]) * s.cells, s.back), BF16)
+    used = range(place(cuts, planes[0]), place(cuts, planes[1] - 1) + 1)
+    others, cuts = [others[k] for k in used], tuple(cuts[used[0]:used[-1] + 2])
     operands = [t["x_forward"], t["unpack"], t["x_inverse"], t["y_inverse"], *poses, *tops, own, *others]
     return pl.pallas_call(
         partial(cross_kernel, s, cuts, planes, per),
@@ -474,7 +474,7 @@
     t = tables(s)
     swapped = lambda parts: [passed_along(part, "fft") for part in parts]
 
-    own, *away = sections(s, t, receptor_occupancy, receptor_extent, False, s.halves)
+    own, *away = sections(s, t, receptor_occupancy, receptor_extent, False, s.whole)
     others = swapped(away)
     receptors = [(own, others)]
     receptors.append((passed_along(own, "rec"), [passed_across(part, "rec") for part in away]))
@@ -488,7 +488,8 @@
     own, others = receptors[1]
     own = after(own, spectra[0][0])
     receptors[1] = (own, others)
-    receptors.append((passed_along(own, "rec"), [passed_along(part, "rec") for part in others]))
+    cuts = [others[0][low * s.size:high * s.size] for low, high in zip(s.parts, s.parts[1:])]
+    receptors.append((passed_along(own, "rec"), [passed_along(part, "rec") for part in cuts]))
 
     spectra.append(spectrum(s, t, channel_weight, next_pose, next_others, s.whole))
     poses, tops = [main for main, _ in spectra], [top for _, top in spectra]
@@ -496,10 +497,11 @@
     rows = []
     for step, (own, others) in enumerate(receptors):
         last = step + 1 == REC_STEPS
-        ranges = list(zip(s.halves, s.halves[1:])) if last else [s.whole]
+        cuts = s.parts if last else s.whole
+        ranges = list(zip(cuts, cuts[1:]))
         if last:
             own = after(own, *rows)
-        sides = [cross_back(s, t, own, others, poses, tops, s.halves, planes) for planes in ranges]
+        sides = [cross_back(s, t, own, others, poses, tops, cuts, planes) for planes in ranges]
         parts = [keep for keep, _ in sides] + swapped([send for _, send in sides])
         rows.append(peaks(s, t, own, parts, rows if last else [], last))
     return rows[-1]

time: 61.6 us -> 59.1 us (0.959)
  waiting for transfers between devices: 29.7 us -> 25 us
  starting transfers between devices: 7.56 us -> 9.61 us
    ppermute x9 -> x11, waiting for transfers between devices: 13.6 us -> 9.15 us  [passed_along(): lax.ppermute(value, axis, [(source, (source + steps) % count) for source...]
    ppermute x9 -> x11, starting transfers between devices: 6 us -> 8.95 us  [passed_along(): lax.ppermute(value, axis, [(source, (source + steps) % count) for source...]
    ppermute x2, starting transfers between devices: 1.57 us -> 0.66 us  [passed_across(): return lax.ppermute(value, (axis, 'fft'), pairs)]
    pallas_call x3 -> x4, Pallas kernels: 9.65 us -> 9.98 us  [cross_back(): pl.pallas_call(partial(cross_kernel, s, cuts, planes, per), in_specs=[vme...]
  transfers between devices with their start and end apart: 11 -> 13, of which waited for: 6 -> 5; matrix products, arithmetic and copies ran while one was open for 0% -> 0% of each run, Pallas kernels for 25% -> 32%
where the time goes in v2:
time: 59.1 us; the launch traced here: 59 us
  waiting for transfers between devices  25 us (42%)
  Pallas kernels  22.8 us (39%)
  starting transfers between devices  9.61 us (16%)
  between operations  1.5 us (3%)
    ppermute x2, waiting for transfers between devices, passed_across(): return lax.ppermute(value, (axis, 'fft'), pairs)  15.9 us
    pallas_call x4, Pallas kernels, cross_back(): pl.pallas_call(partial(cross_kernel, s, cuts, planes, per), in_specs=[vme...  9.98 us
    ppermute x11, waiting for transfers between devices, passed_along(): lax.ppermute(value, axis, [(source, (source + steps) % count) for source...  9.15 us
    ppermute x11, starting transfers between devices, passed_along(): lax.ppermute(value, axis, [(source, (source + steps) % count) for source...  8.95 us
    pallas_call x2, Pallas kernels, sections(): pl.pallas_call(partial(section_kernel, s, pieces, rotated, cuts), in_spec...  6.46 us
    pallas_call x3, Pallas kernels, peaks(): pl.pallas_call(partial(peak_kernel, s, len(parts), last), in_specs=[vmem]...  3.54 us
    pallas_call x2, Pallas kernels, spectrum(): pl.pallas_call(partial(spectrum_kernel, s, cuts, per), in_specs=[pl.Block...  2.8 us
  transfers between devices with their start and end apart: 13, of which 5 were waited for; matrix products, arithmetic and copies ran while one was open for 0% of the time, Pallas kernels for 32%

profile of v2, /device:TPU:0, one launch (start us, length us, event | category | flops | bytes accessed | tf_op | source)
XLA Modules:
  0.0 59.0 jit_solution(5524918629508650234)
XLA Ops:
  0.7 2.5 %shard_map.136 = (bf16[2064,128]{1,0:T(8,128)(2,1)S(1)}, bf16[2048,128]{1,0:T(8,128)(2,1)S(1)}) custom-call(s32[1,4,32,4096]{3,2,1,0:T(8,128)} %occ.1, s32[1]{0:T(128)S(6)} %copy.16.scalar, bf16[2,2,128,128]{3,2,1,0:T(8,128)(2,1)} %constant.18.clone.refs_0_, bf16[2,128,128]{2,1,0:T(8,128)(2,1)} %constant.19.clone.refs_1_), custom_call_target="tpu_custom_call" | custom-call | flops 1000 | bytes 1000 | tf_op jit(solution)/shard_map/pallas_call | solution.py:270
  3.2 0.5 collective-permute-start.1
  3.8 2.6 %collective-permute-start = (bf16[2064,128]{1,0:T(8,128)(2,1)S(1)}, bf16[2064,128]{1,0:T(8,128)(2,1)S(1)}, u32[]{:S(2)}, u32[]{:S(2)}) collective-permute-start(bf16[2064,128]{1,0:T(8,128)(2,1)S(1)} %get-tuple-element.24.refs_4_.load), channel_id=1, source_target_pairs={{0,4},{4,8},{8,12},{12,0},{1,5},{5,9},{9,13},{13,1},{2,6},{6,10},{... | collective-permute-start | bytes 1585160 | tf_op jit(solution)/shard_map/ppermute | solution.py:454
  7.1 3.9 %shard_map.137 = (bf16[2048,128]{1,0:T(8,128)(2,1)S(1)}, bf16[2048,128]{1,0:T(8,128)(2,1)S(1)}) custom-call(s32[1,4,32,4096]{3,2,1,0:T(8,128)} %occ.2, s32[1]{0:T(128)S(6)} %copy.15.scalar, bf16[2,2,128,128]{3,2,1,0:T(8,128)(2,1)} %constant.18.clone.refs_0_, bf16[2,128,128]{2,1,0:T(8,128)(2,1)} %constant.19.clone.refs_1_, ...), custom_call_target="tpu_custom_call" | custom-call | flops 1000 | bytes 1000 | tf_op jit(solution)/shard_map/pallas_call | solution.py:270
  11.0 0.2 collective-permute-start.2
  11.2 0.7 %collective-permute-start.7 = (bf16[2048,128]{1,0:T(8,128)(2,1)S(1)}, bf16[2048,128]{1,0:T(8,128)(2,1)S(1)}, u32[]{:S(2)}, u32[]{:S(2)}) collective-permute-start(bf16[2048,128]{1,0:T(8,128)(2,1)S(1)} %get-tuple-element.25), channel_id=1, source_target_pairs={{0,5},{1,4},{4,9},{5,8},{8,13},{9,12},{12,1},{13,0},{2,7},{3,6},{6... | collective-permute-start | bytes 1572872 | tf_op jit(solution)/shard_map/ppermute | solution.py:464
  11.9 2.4 %collective-permute-start.4 = (bf16[2048,128]{1,0:T(8,128)(2,1)S(1)}, bf16[2048,128]{1,0:T(8,128)(2,1)S(1)}, u32[]{:S(2)}, u32[]{:S(2)}) collective-permute-start(bf16[2048,128]{1,0:T(8,128)(2,1)S(1)} %get-tuple-element.27.own), channel_id=1, source_target_pairs={{0,2},{2,0},{1,3},{3,1},{4,6},{6,4},{5,7},{7,5},{8,10},{10,8},{9,1... | collective-permute-start | bytes 1572872 | tf_op jit(solution)/shard_map/ppermute | solution.py:454
  14.3 1.4 %shard_map.138 = (bf16[1024,512]{1,0:T(8,128)(2,1)S(1)}, bf16[64,512]{1,0:T(8,128)(2,1)S(1)}) custom-call(f32[4]{0:T(128)S(1)} %copy-done.5, bf16[2,512,512]{2,1,0:T(8,128)(2,1)S(1)} %copy-done, bf16[2,256,128]{2,1,0:T(8,128)(2,1)S(1)} %copy-done.1, bf16[2048,128]{1,0:T(8,128)(2,1)S(1)} %get-tuple-element.27.own, ...), custom_call_target="tpu_custom_call" | custom-call | flops 1000 | bytes 1000 | tf_op jit(solution)/shard_map/pallas_call | solution.py:325
  15.7 5.6 %collective-permute-done.refs_4_.load = bf16[2064,128]{1,0:T(8,128)(2,1)S(1)} collective-permute-done((bf16[2064,128]{1,0:T(8,128)(2,1)S(1)}, bf16[2064,128]{1,0:T(8,128)(2,1)S(1)}, u32[]{:S(2)}, u32[]{:S(2)}) %collective-permute-start) | collective-permute-done | bytes 528416 | tf_op jit(solution)/shard_map/ppermute | solution.py:454
  21.3 10.7 %collective-permute-done.7.refs_5_ = bf16[2048,128]{1,0:T(8,128)(2,1)S(1)} collective-permute-done((bf16[2048,128]{1,0:T(8,128)(2,1)S(1)}, bf16[2048,128]{1,0:T(8,128)(2,1)S(1)}, u32[]{:S(2)}, u32[]{:S(2)}) %collective-permute-start.7) | collective-permute-done | bytes 524320 | tf_op jit(solution)/shard_map/ppermute | solution.py:464
  32.1 5.1 %collective-permute-done.5.refs_0_ = bf16[2048,128]{1,0:T(8,128)(2,1)S(1)} collective-permute-done((bf16[2048,128]{1,0:T(8,128)(2,1)S(1)}, bf16[2048,128]{1,0:T(8,128)(2,1)S(1)}, u32[]{:S(2)}, u32[]{:S(2)}) %collective-permute-start.5) | collective-permute-done | bytes 524320 | tf_op jit(solution)/shard_map/ppermute | solution.py:464
  37.3 1.4 %shard_map.139 = (bf16[1024,512]{1,0:T(8,128)(2,1)S(1)}, bf16[64,512]{1,0:T(8,128)(2,1)S(1)}) custom-call(f32[4]{0:T(128)S(1)} %copy-done.5, bf16[2,512,512]{2,1,0:T(8,128)(2,1)S(1)} %copy-done, bf16[2,256,128]{2,1,0:T(8,128)(2,1)S(1)} %copy-done.1, bf16[2048,128]{1,0:T(8,128)(2,1)S(1)} %collective-permute-done.4.own, ...), custom_call_target="tpu_custom_call" | custom-call | flops 1000 | bytes 1000 | tf_op jit(solution)/shard_map/pallas_call | solution.py:325
  38.7 3.2 %shard_map.142 = (bf16[1024,128]{1,0:T(8,128)(2,1)S(1)}, bf16[1024,128]{1,0:T(8,128)(2,1)S(1)}) custom-call(bf16[2,512,512]{2,1,0:T(8,128)(2,1)S(1)} %copy-done, bf16[2,256,128]{2,1,0:T(8,128)(2,1)S(1)} %copy-done.1, bf16[2,256,256]{2,1,0:T(8,128)(2,1)S(1)} %copy-done.2, bf16[128,128]{1,0:T(8,128)(2,1)S(1)} %copy-done.3, ...), custom_call_target="tpu_custom_call" | custom-call | flops 1000 | bytes 1000 | tf_op jit(solution)/shard_map/pallas_call | solution.py:399
  41.9 0.6 %collective-permute-start.8 = (bf16[1024,128]{1,0:T(8,128)(2,1)S(1)}, bf16[1024,128]{1,0:T(8,128)(2,1)S(1)}, u32[]{:S(2)}, u32[]{:S(2)}) collective-permute-start(bf16[1024,128]{1,0:T(8,128)(2,1)S(1)} %get-tuple-element.37), channel_id=1, source_target_pairs={{0,1},{1,0},{2,3},{3,2},{4,5},{5,4},{6,7},{7,6},{8,9},{9,8},{10,11... | collective-permute-start | bytes 786440 | tf_op jit(solution)/shard_map/ppermute | solution.py:454
  42.6 3.2 %shard_map.140 = (bf16[1024,128]{1,0:T(8,128)(2,1)S(1)}, bf16[1024,128]{1,0:T(8,128)(2,1)S(1)}) custom-call(bf16[2,512,512]{2,1,0:T(8,128)(2,1)S(1)} %copy-done, bf16[2,256,128]{2,1,0:T(8,128)(2,1)S(1)} %copy-done.1, bf16[2,256,256]{2,1,0:T(8,128)(2,1)S(1)} %copy-done.2, bf16[128,128]{1,0:T(8,128)(2,1)S(1)} %copy-done.3, ...), custom_call_target="tpu_custom_call" | custom-call | flops 1000 | bytes 1000 | tf_op jit(solution)/shard_map/pallas_call | solution.py:399
  45.9 1.8 %collective-permute-start.10 = (bf16[512,128]{1,0:T(8,128)(2,1)S(1)}, bf16[512,128]{1,0:T(8,128)(2,1)S(1)}, u32[]{:S(2)}, u32[]{:S(2)}) collective-permute-start(bf16[512,128]{1,0:T(8,128)(2,1)S(1)} %slice.9), channel_id=1, source_target_pairs={{0,4},{4,8},{8,12},{12,0},{1,5},{5,9},{9,13},{13,1},{2,6},{6,10},{... | collective-permute-start | bytes 393224 | tf_op jit(solution)/shard_map/ppermute | solution.py:454
  47.7 1.0 %shard_map.143.refs_5_ = f32[1,128]{1,0:T(1,128)S(1)} custom-call(bf16[2064,128]{1,0:T(8,128)(2,1)S(1)} %collective-permute-done.refs_4_.load, bf16[2,64,64]{2,1,0:T(8,128)(2,1)S(1)} %copy-done.4, bf16[1024,128]{1,0:T(8,128)(2,1)S(1)} %get-tuple-element.36.refs_0_, bf16[1024,128]{1,0:T(8,128)(2,1)S(1)} %collective-permute-done.8.refs_1_), custom_call_target="tpu_custom_call" | custom-call | flops 1000 | bytes 1000 | tf_op jit(solution)/shard_map/pallas_call | solution.py:441
  48.7 1.0 %shard_map.141.refs_4_ = f32[1,128]{1,0:T(1,128)S(1)} custom-call(bf16[2064,128]{1,0:T(8,128)(2,1)S(1)} %get-tuple-element.24.refs_4_.load, bf16[2,64,64]{2,1,0:T(8,128)(2,1)S(1)} %copy-done.4, bf16[1024,128]{1,0:T(8,128)(2,1)S(1)} %get-tuple-element.34.refs_0_, bf16[1024,128]{1,0:T(8,128)(2,1)S(1)} %collective-permute-done.6.refs_1_), custom_call_target="tpu_custom_call" | custom-call | flops 1000 | bytes 1000 | tf_op jit(solution)/shard_map/pallas_call | solution.py:441
  49.6 2.6 %collective-permute-done.9.refs_5_ = bf16[1536,128]{1,0:T(8,128)(2,1)S(1)} collective-permute-done((bf16[1536,128]{1,0:T(8,128)(2,1)S(1)}, bf16[1536,128]{1,0:T(8,128)(2,1)S(1)}, u32[]{:S(2)}, u32[]{:S(2)}) %collective-permute-start.9) | collective-permute-done | bytes 393248 | tf_op jit(solution)/shard_map/ppermute | solution.py:454
  52.3 2.5 %shard_map.144 = (bf16[768,128]{1,0:T(8,128)(2,1)S(1)}, bf16[768,128]{1,0:T(8,128)(2,1)S(1)}) custom-call(bf16[2,512,512]{2,1,0:T(8,128)(2,1)S(1)} %copy-done, bf16[2,256,128]{2,1,0:T(8,128)(2,1)S(1)} %copy-done.1, bf16[2,256,256]{2,1,0:T(8,128)(2,1)S(1)} %copy-done.2, bf16[128,128]{1,0:T(8,128)(2,1)S(1)} %copy-done.3, ...), custom_call_target="tpu_custom_call" | custom-call | flops 1000 | bytes 1000 | tf_op jit(solution)/shard_map/pallas_call | solution.py:399
  54.9 1.0 %shard_map.145 = (bf16[256,128]{1,0:T(8,128)(2,1)S(1)}, bf16[256,128]{1,0:T(8,128)(2,1)S(1)}) custom-call(bf16[2,512,512]{2,1,0:T(8,128)(2,1)S(1)} %copy-done, bf16[2,256,128]{2,1,0:T(8,128)(2,1)S(1)} %copy-done.1, bf16[2,256,256]{2,1,0:T(8,128)(2,1)S(1)} %copy-done.2, bf16[128,128]{1,0:T(8,128)(2,1)S(1)} %copy-done.3, ...), custom_call_target="tpu_custom_call" | custom-call | flops 1000 | bytes 1000 | tf_op jit(solution)/shard_map/pallas_call | solution.py:399
  55.9 0.5 collective-permute-start.12
  56.5 0.9 %collective-permute-done.12.refs_3_ = bf16[256,128]{1,0:T(8,128)(2,1)S(1)} collective-permute-done((bf16[256,128]{1,0:T(8,128)(2,1)S(1)}, bf16[256,128]{1,0:T(8,128)(2,1)S(1)}, u32[]{:S(2)}, u32[]{:S(2)}) %collective-permute-start.12) | collective-permute-done | bytes 65568 | tf_op jit(solution)/shard_map/ppermute | solution.py:454
  57.4 1.6 %shard_map.146 = f32[1,3,2,32]{3,2,1,0:T(2,128)} custom-call(bf16[2064,128]{1,0:T(8,128)(2,1)S(1)} %collective-permute-done.3.refs_4_.load, bf16[2,64,64]{2,1,0:T(8,128)(2,1)S(1)} %copy-done.4, bf16[768,128]{1,0:T(8,128)(2,1)S(1)} %get-tuple-element.39.refs_0_, bf16[256,128]{1,0:T(8,128)(2,1)S(1)} %get-tuple-element.40.refs_1_, ...), custom_call_target="tpu_custom_call" | custom-call | flops 1000 | bytes 1000 | tf_op jit(solution)/shard_map/pallas_call | solution.py:441
  (27 shorter events, 0.3 us)
Async XLA Ops:
  0.7 13.6 %copy-start = (bf16[2,512,512]{2,1,0:T(8,128)(2,1)S(1)}, bf16[2,512,512]{2,1,0:T(8,128)(2,1)}, u32[]{:S(2)}) copy-start(bf16[2,512,512]{2,1,0:T(8,128)(2,1)} %constant.22.clone.table) | copy-start | bytes 3145732
  0.7 13.6 %copy-start.1 = (bf16[2,256,128]{2,1,0:T(8,128)(2,1)S(1)}, bf16[2,256,128]{2,1,0:T(8,128)(2,1)}, u32[]{:S(2)}) copy-start(bf16[2,256,128]{2,1,0:T(8,128)(2,1)} %constant.23.clone.unpack) | copy-start | bytes 393220
  0.7 13.6 %copy-start.5 = (f32[4]{0:T(128)S(1)}, f32[4]{0:T(128)}, u32[]{:S(2)}) copy-start(f32[4]{0:T(128)} %weight.3) | copy-start | bytes 52
  3.2 3.8 %collective-permute-start.1 = (bf16[2048,128]{1,0:T(8,128)(2,1)S(1)}, bf16[2048,128]{1,0:T(8,128)(2,1)S(1)}, u32[]{:S(2)}, u32[]{:S(2)}) collective-permute-start(bf16[2048,128]{1,0:T(8,128)(2,1)S(1)} %get-tuple-element.25), channel_id=1, source_target_pairs={{0,1},{1,0},{2,3},{3,2},{4,5},{5,4},{6,7},{7,6},{8,9},{9,8},{10,11... | collective-permute-start | bytes 1572872 | tf_op jit(solution)/shard_map/ppermute | solution.py:454
  3.8 17.5 %collective-permute-start = (bf16[2064,128]{1,0:T(8,128)(2,1)S(1)}, bf16[2064,128]{1,0:T(8,128)(2,1)S(1)}, u32[]{:S(2)}, u32[]{:S(2)}) collective-permute-start(bf16[2064,128]{1,0:T(8,128)(2,1)S(1)} %get-tuple-element.24.refs_4_.load), channel_id=1, source_target_pairs={{0,4},{4,8},{8,12},{12,0},{1,5},{5,9},{9,13},{13,1},{2,6},{6,10},{... | collective-permute-start | bytes 1585160 | tf_op jit(solution)/shard_map/ppermute | solution.py:454
  11.0 3.3 %collective-permute-start.2 = (bf16[2048,128]{1,0:T(8,128)(2,1)S(1)}, bf16[2048,128]{1,0:T(8,128)(2,1)S(1)}, u32[]{:S(2)}, u32[]{:S(2)}) collective-permute-start(bf16[2048,128]{1,0:T(8,128)(2,1)S(1)} %get-tuple-element.28), channel_id=1, source_target_pairs={{0,1},{1,0},{2,3},{3,2},{4,5},{5,4},{6,7},{7,6},{8,9},{9,8},{10,11... | collective-permute-start | bytes 1572872 | tf_op jit(solution)/shard_map/ppermute | solution.py:454
  11.2 20.8 %collective-permute-start.7 = (bf16[2048,128]{1,0:T(8,128)(2,1)S(1)}, bf16[2048,128]{1,0:T(8,128)(2,1)S(1)}, u32[]{:S(2)}, u32[]{:S(2)}) collective-permute-start(bf16[2048,128]{1,0:T(8,128)(2,1)S(1)} %get-tuple-element.25), channel_id=1, source_target_pairs={{0,5},{1,4},{4,9},{5,8},{8,13},{9,12},{12,1},{13,0},{2,7},{3,6},{6... | collective-permute-start | bytes 1572872 | tf_op jit(solution)/shard_map/ppermute | solution.py:464
  11.9 26.8 %copy-start.2 = (bf16[2,256,256]{2,1,0:T(8,128)(2,1)S(1)}, bf16[2,256,256]{2,1,0:T(8,128)(2,1)}, u32[]{:S(2)}) copy-start(bf16[2,256,256]{2,1,0:T(8,128)(2,1)} %constant.24.clone.x_inverse) | copy-start | bytes 786436
  11.9 26.8 %copy-start.3 = (bf16[128,128]{1,0:T(8,128)(2,1)S(1)}, bf16[128,128]{1,0:T(8,128)(2,1)}, u32[]{:S(2)}) copy-start(bf16[128,128]{1,0:T(8,128)(2,1)} %constant.25.clone.y_inverse) | copy-start | bytes 98308
  11.9 20.2 %collective-permute-start.4 = (bf16[2048,128]{1,0:T(8,128)(2,1)S(1)}, bf16[2048,128]{1,0:T(8,128)(2,1)S(1)}, u32[]{:S(2)}, u32[]{:S(2)}) collective-permute-start(bf16[2048,128]{1,0:T(8,128)(2,1)S(1)} %get-tuple-element.27.own), channel_id=1, source_target_pairs={{0,2},{2,0},{1,3},{3,1},{4,6},{6,4},{5,7},{7,5},{8,10},{10,8},{9,1... | collective-permute-start | bytes 1572872 | tf_op jit(solution)/shard_map/ppermute | solution.py:454
  14.2 23.0 %collective-permute-start.5 = (bf16[2048,128]{1,0:T(8,128)(2,1)S(1)}, bf16[2048,128]{1,0:T(8,128)(2,1)S(1)}, u32[]{:S(2)}, u32[]{:S(2)}) collective-permute-start(bf16[2048,128]{1,0:T(8,128)(2,1)S(1)} %get-tuple-element.28), channel_id=1, source_target_pairs={{0,3},{1,2},{2,1},{3,0},{4,7},{5,6},{6,5},{7,4},{8,11},{9,10},{10,... | collective-permute-start | bytes 1572872 | tf_op jit(solution)/shard_map/ppermute | solution.py:464
  21.3 28.4 %collective-permute-start.3 = (bf16[2064,128]{1,0:T(8,128)(2,1)S(1)}, bf16[2064,128]{1,0:T(8,128)(2,1)S(1)}, u32[]{:S(2)}, u32[]{:S(2)}) collective-permute-start(bf16[2064,128]{1,0:T(8,128)(2,1)S(1)} %collective-permute-done.refs_4_.load), channel_id=1, source_target_pairs={{0,4},{4,8},{8,12},{12,0},{1,5},{5,9},{9,13},{13,1},{2,6},{6,10},{... | collective-permute-start | bytes 1585160 | tf_op jit(solution)/shard_map/ppermute | solution.py:454
  32.0 20.2 %collective-permute-start.9 = (bf16[1536,128]{1,0:T(8,128)(2,1)S(1)}, bf16[1536,128]{1,0:T(8,128)(2,1)S(1)}, u32[]{:S(2)}, u32[]{:S(2)}) collective-permute-start(bf16[1536,128]{1,0:T(8,128)(2,1)S(1)} %slice.8), channel_id=1, source_target_pairs={{0,4},{4,8},{8,12},{12,0},{1,5},{5,9},{9,13},{13,1},{2,6},{6,10},{... | collective-permute-start | bytes 1179656 | tf_op jit(solution)/shard_map/ppermute | solution.py:454
  41.9 5.8 %copy-start.4 = (bf16[2,64,64]{2,1,0:T(8,128)(2,1)S(1)}, bf16[2,64,64]{2,1,0:T(8,128)(2,1)}, u32[]{:S(2)}) copy-start(bf16[2,64,64]{2,1,0:T(8,128)(2,1)} %constant.26.clone.table) | copy-start | bytes 49156
  41.9 5.8 %collective-permute-start.8 = (bf16[1024,128]{1,0:T(8,128)(2,1)S(1)}, bf16[1024,128]{1,0:T(8,128)(2,1)S(1)}, u32[]{:S(2)}, u32[]{:S(2)}) collective-permute-start(bf16[1024,128]{1,0:T(8,128)(2,1)S(1)} %get-tuple-element.37), channel_id=1, source_target_pairs={{0,1},{1,0},{2,3},{3,2},{4,5},{5,4},{6,7},{7,6},{8,9},{9,8},{10,11... | collective-permute-start | bytes 786440 | tf_op jit(solution)/shard_map/ppermute | solution.py:454
  45.8 2.9 %collective-permute-start.6 = (bf16[1024,128]{1,0:T(8,128)(2,1)S(1)}, bf16[1024,128]{1,0:T(8,128)(2,1)S(1)}, u32[]{:S(2)}, u32[]{:S(2)}) collective-permute-start(bf16[1024,128]{1,0:T(8,128)(2,1)S(1)} %get-tuple-element.35), channel_id=1, source_target_pairs={{0,1},{1,0},{2,3},{3,2},{4,5},{5,4},{6,7},{7,6},{8,9},{9,8},{10,11... | collective-permute-start | bytes 786440 | tf_op jit(solution)/shard_map/ppermute | solution.py:454
  45.9 9.0 %collective-permute-start.10 = (bf16[512,128]{1,0:T(8,128)(2,1)S(1)}, bf16[512,128]{1,0:T(8,128)(2,1)S(1)}, u32[]{:S(2)}, u32[]{:S(2)}) collective-permute-start(bf16[512,128]{1,0:T(8,128)(2,1)S(1)} %slice.9), channel_id=1, source_target_pairs={{0,4},{4,8},{8,12},{12,0},{1,5},{5,9},{9,13},{13,1},{2,6},{6,10},{... | collective-permute-start | bytes 393224 | tf_op jit(solution)/shard_map/ppermute | solution.py:454
  54.8 2.5 %collective-permute-start.11 = (bf16[768,128]{1,0:T(8,128)(2,1)S(1)}, bf16[768,128]{1,0:T(8,128)(2,1)S(1)}, u32[]{:S(2)}, u32[]{:S(2)}) collective-permute-start(bf16[768,128]{1,0:T(8,128)(2,1)S(1)} %get-tuple-element.41), channel_id=1, source_target_pairs={{0,1},{1,0},{2,3},{3,2},{4,5},{5,4},{6,7},{7,6},{8,9},{9,8},{10,11... | collective-permute-start | bytes 589832 | tf_op jit(solution)/shard_map/ppermute | solution.py:454
  55.9 1.4 %collective-permute-start.12 = (bf16[256,128]{1,0:T(8,128)(2,1)S(1)}, bf16[256,128]{1,0:T(8,128)(2,1)S(1)}, u32[]{:S(2)}, u32[]{:S(2)}) collective-permute-start(bf16[256,128]{1,0:T(8,128)(2,1)S(1)} %get-tuple-element.42), channel_id=1, source_target_pairs={{0,1},{1,0},{2,3},{3,2},{4,5},{5,4},{6,7},{7,6},{8,9},{9,8},{10,11... | collective-permute-start | bytes 196616 | tf_op jit(solution)/shard_map/ppermute | solution.py:454

commit v3 on v2

--- a/solution.py
+++ b/solution.py
@@ -68,18 +68,16 @@
     tables["y_odd"] = flips(np.kron(two, full_rows), cells)
     tables["z_odd"] = np.stack([flips(half_mix(core), cells) for core in range(cores)], axis=1)
 
+    group = channels // 2
     spread = []
     for core in range(cores):
-        blocks = []
+        block = np.zeros((cores, 2, group, slab, 2, group, cells), np.float32)
         for turn in range(cores):
             start = (core + turn) % cores * slab
             mix = forward.reshape(2, cells, 2, cells)[:, :, :, start:start + slab]
-            for part in range(2):
-                block = np.zeros((channels, slab, channels, 2, cells), np.float32)
-                for channel in range(channels):
-                    block[channel, :, channel] = mix[:, :, part].transpose(2, 0, 1)
-                blocks.append(block.reshape(channels * slab, channels * 2 * cells))
-        spread.append(np.concatenate(blocks, axis=0))
+            for channel in range(group):
+                block[turn, :, channel, :, :, channel] = mix.transpose(2, 3, 0, 1)
+        spread.append(block.reshape(cores * 2 * group * slab, 2 * group * cells))
     tables["x_forward"] = np.stack(spread)
 
     mirror = np.zeros((cells, cells), np.float32)
@@ -278,24 +276,38 @@
     )(pin(occ), scalar, *[pin(t[name]) for name in names])
 
 
+def regroup(s, parts):
+    half = s.lanes // 2
+    lane = lax.broadcasted_iota(jnp.int32, parts[0].shape, 1)
+    low, high = [], []
+    for one, two in zip(parts[::2], parts[1::2]):
+        low.append(jnp.where(lane < half, one, pltpu.roll(two, half, 1)))
+        high.append(jnp.where(lane < half, pltpu.roll(one, half, 1), two))
+    return [jnp.concatenate(low, axis=1), jnp.concatenate(high, axis=1)]
+
+
 def x_rows(s, cuts, own, others, plane):
     cut = place(cuts, plane)
     parts = []
     for ref, at in ((own, plane * s.size), (others[cut], (plane - cuts[cut]) * s.size)):
         for p in range(2):
             parts.append(ref[at + p * s.cells:at + (p + 1) * s.cells, :])
-    return jnp.concatenate(parts, axis=1)
+    return regroup(s, parts)
 
 
 def unpacked_rows(s, own, others, unpack):
     cells = s.cells
     done = [dot(unpack, ref[:s.size, :]).astype(BF16) for ref in (own, others[0])]
     return [
-        jnp.concatenate(
-            [value[(2 * k + p) * cells:(2 * k + p + 1) * cells] for value in done for p in range(2)], axis=1
-        )
+        regroup(s, [value[(2 * k + p) * cells:(2 * k + p + 1) * cells] for value in done for p in range(2)])
         for k in range(2)
     ]
+
+
+def x_transform(s, rows, table):
+    done = dot(jnp.concatenate([row[k] for k in range(2) for row in rows], axis=0), table)
+    count = len(rows) * s.cells
+    return done[:count], done[count:]
 
 
 def spectrum_kernel(s, cuts, per, weight, table, unpack, own, *refs):
@@ -303,20 +315,30 @@
     volume = 1.0 / float(s.cells) ** 3
     core = lax.axis_index("fft")
 
-    def put(ref, at, value):
-        for channel in range(s.channels):
-            lanes = slice(channel * s.size, (channel + 1) * s.size)
-            ref[at:at + value.shape[0], lanes] = (value[:, lanes] * (weight[channel] * volume)).astype(BF16)
+    lane = lax.broadcasted_iota(jnp.int32, (s.cells, s.size), 1)
+    scales = [
+        jnp.where(lane < s.cells, weight[2 * k], weight[2 * k + 1]) * volume for k in range(2)
+    ]
+
+    def put(ref, at, values):
+        for k, value in enumerate(values):
+            for q in range(2):
+                from_lanes = slice(q * s.size, (q + 1) * s.size)
+                to_lanes = slice((2 * k + q) * s.size, (2 * k + q + 1) * s.size)
+                for row in range(0, value.shape[0], s.cells):
+                    ref[at + row:at + row + s.cells, to_lanes] = (
+                        value[row:row + s.cells, from_lanes] * scales[k]
+                    ).astype(BF16)
 
     for start in range(0, s.own, per):
         rows = [x_rows(s, cuts, own, others, plane) for plane in range(start, start + per)]
         if start == 0:
             rows[0], high = unpacked_rows(s, own, others, unpack[core])
             rows.append(high)
-        done = dot(jnp.concatenate(rows, axis=0), table[core])
-        put(main, start * s.cells, done[:per * s.cells])
+        done = x_transform(s, rows, table[core])
+        put(main, start * s.cells, [value[:per * s.cells] for value in done])
         if start == 0:
-            put(last, 0, done[per * s.cells:])
+            put(last, 0, [value[per * s.cells:] for value in done])
 
 
 def spectrum(s, t, weight, own, others, cuts, per=4):
@@ -332,7 +354,7 @@
     )(weight, t["x_forward"], t["unpack"], own, *others)
 
 
-def cross_kernel(s, cuts, planes, per, table, unpack, x_inverse, y_inverse, *refs):
+def cross_kernel(s, cuts, planes, most, table, unpack, x_inverse, y_inverse, *refs):
     poses, tops = refs[:LIG_STEPS], refs[LIG_STEPS:2 * LIG_STEPS]
     own, others = refs[2 * LIG_STEPS], refs[2 * LIG_STEPS + 1:-2]
     keep, send = refs[-2:]
@@ -343,33 +365,34 @@
     kept = lax.broadcasted_iota(jnp.int32, (cells // 2, lanes), 1) < lanes // 2
 
     def correlate(receptor, pose):
-        straight = None
-        for channel in range(s.channels):
-            here = slice(channel * width, (channel + 1) * width)
-            one = receptor[:, here]
-            two = pose[:, here].astype(F32)
-            terms = (one * two, pltpu.roll(one, cells, 1) * two)
-            straight = terms if straight is None else (straight[0] + terms[0], straight[1] + terms[1])
-        same, turned = straight
-        return jnp.where(is_real, same + pltpu.roll(same, cells, 1), pltpu.roll(turned, cells, 1) - turned)
-
-    for start in range(planes[0], planes[1], per):
+        real = imag = None
+        for k, value in enumerate(receptor):
+            one = [value[:, q * width:(q + 1) * width] for q in range(2)]
+            two = [pose[:, (2 * k + q) * width:(2 * k + q + 1) * width].astype(F32) for q in range(2)]
+            same = one[0] * two[0] + one[1] * two[1]
+            turned = one[1] * two[0] - one[0] * two[1]
+            real = same if real is None else real + same
+            imag = turned if imag is None else imag + turned
+        return jnp.where(is_real, real, imag) + pltpu.roll(jnp.where(is_real, imag, real), cells, 1)
+
+    for start in range(planes[0], planes[1], most):
+        per = min(most, planes[1] - start)
         rows = [x_rows(s, cuts, own, others, plane) for plane in range(start, start + per)]
         if start == 0:
             rows[0], high = unpacked_rows(s, own, others, unpack[core])
             rows.append(high)
-        done = dot(jnp.concatenate(rows, axis=0), table[core])
+        done = x_transform(s, rows, table[core])
         cross = []
         for k in range(per):
             both = []
             for pose in range(LIG_STEPS):
                 at = (start + k) * cells
-                value = correlate(done[k * cells:(k + 1) * cells], poses[pose][at:at + cells, :])
+                value = correlate([half[k * cells:(k + 1) * cells] for half in done], poses[pose][at:at + cells, :])
                 if start + k == 0:
                     row = lax.broadcasted_iota(jnp.int32, (cells, width), 0)
                     at_zero = (row == 0) & ((lane == 0) | (lane == cells)) & (core == 0)
                     value = jnp.where(at_zero, 0.0, value)
-                    top = pltpu.roll(correlate(done[per * cells:], tops[pose][...]), cells, 1)
+                    top = pltpu.roll(correlate([half[per * cells:] for half in done], tops[pose][...]), cells, 1)
                     value = value + jnp.where(is_real, -top, top)
                 both.append(value.astype(BF16))
             cross.append(jnp.concatenate(both, axis=1))
@@ -412,13 +435,15 @@
     cells = s.cells
     low = cells // 2
     core = lax.axis_index("fft")
+    step = low + 8
     at = 0
     for part in parts:
-        held[at:at + part.shape[0], :] = part[...].astype(F32)
-        at += part.shape[0]
+        for row in range(0, part.shape[0], low):
+            held[at:at + low, :] = part[row:row + low, :].astype(F32)
+            at += step
     best = None
     for pair in range(0, low, 2):
-        columns = [held[pl.ds(pair + k, cells, stride=low), :] for k in range(2)]
+        columns = [held[pl.ds(pair + k, cells, stride=step), :] for k in range(2)]
         scores = dot(table[core], jnp.concatenate(columns, axis=1).astype(BF16))
         here = jnp.maximum(scores[:, :s.back], scores[:, s.back:])
         best = here if best is None else jnp.maximum(best, here)
@@ -443,7 +468,7 @@
         in_specs=[vmem] * (2 + len(parts) + len(earlier)),
         out_specs=vmem,
         out_shape=jax.ShapeDtypeStruct(shape, F32),
-        scratch_shapes=[pltpu.VMEM((s.cells * s.cells // 2, s.back), F32)],
+        scratch_shapes=[pltpu.VMEM((s.cells * (s.cells // 2 + 8), s.back), F32)],
         compiler_params=params(),
         cost_estimate=COST,
     )(load, t["z_inverse"], *parts, *earlier)

time: 59.1 us -> 58.2 us (0.985)
  Pallas kernels: 22.8 us -> 17.7 us
  waiting for transfers between devices: 25 us -> 28.4 us
  starting transfers between devices: 9.61 us -> 10.4 us
    ppermute x11, waiting for transfers between devices: 9.15 us -> 13.4 us  [passed_along(): lax.ppermute(value, axis, [(source, (source + steps) % count) for source...]
    pallas_call x4, Pallas kernels: 9.98 us -> 7.62 us  [cross_back(): pl.pallas_call(partial(cross_kernel, s, cuts, planes, per), in_specs=[vme...]
    pallas_call x3, Pallas kernels: 3.54 us -> 2.03 us  [peaks(): pl.pallas_call(partial(peak_kernel, s, len(parts), last), in_specs=[vmem]...]
    ppermute x2, waiting for transfers between devices: 15.9 us -> 15 us  [passed_across(): return lax.ppermute(value, (axis, 'fft'), pairs)]
    pallas_call x2, Pallas kernels: 6.46 us -> 5.54 us  [sections(): pl.pallas_call(partial(section_kernel, s, pieces, rotated, cuts), in_spec...]
    ppermute x2, starting transfers between devices: 0.66 us -> 1.56 us  [passed_across(): return lax.ppermute(value, (axis, 'fft'), pairs)]
  transfers between devices with their start and end apart: 13 -> 13, of which waited for: 5 -> 6; matrix products, arithmetic and copies ran while one was open for 0% -> 0% of each run, Pallas kernels for 32% -> 24%
where the time goes in v3:
time: 58.2 us; the launch traced here: 58 us
  waiting for transfers between devices  28.4 us (49%)
  Pallas kernels  17.7 us (30%)
  starting transfers between devices  10.4 us (18%)
  between operations  1.49 us (3%)
    ppermute x2, waiting for transfers between devices, passed_across(): return lax.ppermute(value, (axis, 'fft'), pairs)  15 us
    ppermute x11, waiting for transfers between devices, passed_along(): lax.ppermute(value, axis, [(source, (source + steps) % count) for source...  13.4 us
    ppermute x11, starting transfers between devices, passed_along(): lax.ppermute(value, axis, [(source, (source + steps) % count) for source...  8.85 us
    pallas_call x4, Pallas kernels, cross_back(): pl.pallas_call(partial(cross_kernel, s, cuts, planes, per), in_specs=[vme...  7.62 us
    pallas_call x2, Pallas kernels, sections(): pl.pallas_call(partial(section_kernel, s, pieces, rotated, cuts), in_spec...  5.54 us
    pallas_call x2, Pallas kernels, spectrum(): pl.pallas_call(partial(spectrum_kernel, s, cuts, per), in_specs=[pl.Block...  2.49 us
    pallas_call x3, Pallas kernels, peaks(): pl.pallas_call(partial(peak_kernel, s, len(parts), last), in_specs=[vmem]...  2.03 us
    ppermute x2, starting transfers between devices, passed_across(): return lax.ppermute(value, (axis, 'fft'), pairs)  1.56 us
  transfers between devices with their start and end apart: 13, of which 6 were waited for; matrix products, arithmetic and copies ran while one was open for 0% of the time, Pallas kernels for 24%

profile of v3, /device:TPU:0, one launch (start us, length us, event | category | flops | bytes accessed | tf_op | source)
XLA Modules:
  0.0 58.0 jit_solution(4286416165008505164)
XLA Ops:
  0.7 2.5 %shard_map.136 = (bf16[2064,128]{1,0:T(8,128)(2,1)S(1)}, bf16[2048,128]{1,0:T(8,128)(2,1)S(1)}) custom-call(s32[1,4,32,4096]{3,2,1,0:T(8,128)} %occ.1, s32[1]{0:T(128)S(6)} %copy.16.scalar, bf16[2,2,128,128]{3,2,1,0:T(8,128)(2,1)} %constant.18.clone.refs_0_, bf16[2,128,128]{2,1,0:T(8,128)(2,1)} %constant.19.clone.refs_1_), custom_call_target="tpu_custom_call" | custom-call | flops 1000 | bytes 1000 | tf_op jit(solution)/shard_map/pallas_call | solution.py:268
  3.2 0.5 collective-permute-start.1
  3.7 2.6 %collective-permute-start = (bf16[2064,128]{1,0:T(8,128)(2,1)S(1)}, bf16[2064,128]{1,0:T(8,128)(2,1)S(1)}, u32[]{:S(2)}, u32[]{:S(2)}) collective-permute-start(bf16[2064,128]{1,0:T(8,128)(2,1)S(1)} %get-tuple-element.24.refs_4_.load), channel_id=1, source_target_pairs={{0,4},{4,8},{8,12},{12,0},{1,5},{5,9},{9,13},{13,1},{2,6},{6,10},{... | collective-permute-start | bytes 1585160 | tf_op jit(solution)/shard_map/ppermute | solution.py:479
  7.0 3.1 %shard_map.137 = (bf16[2048,128]{1,0:T(8,128)(2,1)S(1)}, bf16[2048,128]{1,0:T(8,128)(2,1)S(1)}) custom-call(s32[1,4,32,4096]{3,2,1,0:T(8,128)} %occ.2, s32[1]{0:T(128)S(6)} %copy.15.scalar, bf16[2,2,128,128]{3,2,1,0:T(8,128)(2,1)} %constant.18.clone.refs_0_, bf16[2,128,128]{2,1,0:T(8,128)(2,1)} %constant.19.clone.refs_1_, ...), custom_call_target="tpu_custom_call" | custom-call | flops 1000 | bytes 1000 | tf_op jit(solution)/shard_map/pallas_call | solution.py:268
  10.1 0.2 collective-permute-start.2
  10.3 1.5 %collective-permute-start.7 = (bf16[2048,128]{1,0:T(8,128)(2,1)S(1)}, bf16[2048,128]{1,0:T(8,128)(2,1)S(1)}, u32[]{:S(2)}, u32[]{:S(2)}) collective-permute-start(bf16[2048,128]{1,0:T(8,128)(2,1)S(1)} %get-tuple-element.25), channel_id=1, source_target_pairs={{0,5},{1,4},{4,9},{5,8},{8,13},{9,12},{12,1},{13,0},{2,7},{3,6},{6... | collective-permute-start | bytes 1572872 | tf_op jit(solution)/shard_map/ppermute | solution.py:489
  11.8 1.5 %collective-permute-start.4 = (bf16[2048,128]{1,0:T(8,128)(2,1)S(1)}, bf16[2048,128]{1,0:T(8,128)(2,1)S(1)}, u32[]{:S(2)}, u32[]{:S(2)}) collective-permute-start(bf16[2048,128]{1,0:T(8,128)(2,1)S(1)} %get-tuple-element.27.own), channel_id=1, source_target_pairs={{0,2},{2,0},{1,3},{3,1},{4,6},{6,4},{5,7},{7,5},{8,10},{10,8},{9,1... | collective-permute-start | bytes 1572872 | tf_op jit(solution)/shard_map/ppermute | solution.py:479
  13.4 1.3 %shard_map.138 = (bf16[1024,512]{1,0:T(8,128)(2,1)S(1)}, bf16[64,512]{1,0:T(8,128)(2,1)S(1)}) custom-call(f32[4]{0:T(128)S(1)} %copy-done.5, bf16[2,256,256]{2,1,0:T(8,128)(2,1)S(1)} %copy-done, bf16[2,256,128]{2,1,0:T(8,128)(2,1)S(1)} %copy-done.1, bf16[2048,128]{1,0:T(8,128)(2,1)S(1)} %get-tuple-element.27.own, ...), custom_call_target="tpu_custom_call" | custom-call | flops 1000 | bytes 1000 | tf_op jit(solution)/shard_map/pallas_call | solution.py:347
  14.7 6.6 %collective-permute-done.refs_4_.load = bf16[2064,128]{1,0:T(8,128)(2,1)S(1)} collective-permute-done((bf16[2064,128]{1,0:T(8,128)(2,1)S(1)}, bf16[2064,128]{1,0:T(8,128)(2,1)S(1)}, u32[]{:S(2)}, u32[]{:S(2)}) %collective-permute-start) | collective-permute-done | bytes 528416 | tf_op jit(solution)/shard_map/ppermute | solution.py:479
  21.2 10.7 %collective-permute-done.7.refs_5_ = bf16[2048,128]{1,0:T(8,128)(2,1)S(1)} collective-permute-done((bf16[2048,128]{1,0:T(8,128)(2,1)S(1)}, bf16[2048,128]{1,0:T(8,128)(2,1)S(1)}, u32[]{:S(2)}, u32[]{:S(2)}) %collective-permute-start.7) | collective-permute-done | bytes 524320 | tf_op jit(solution)/shard_map/ppermute | solution.py:489
  32.1 4.2 %collective-permute-done.5.refs_0_ = bf16[2048,128]{1,0:T(8,128)(2,1)S(1)} collective-permute-done((bf16[2048,128]{1,0:T(8,128)(2,1)S(1)}, bf16[2048,128]{1,0:T(8,128)(2,1)S(1)}, u32[]{:S(2)}, u32[]{:S(2)}) %collective-permute-start.5) | collective-permute-done | bytes 524320 | tf_op jit(solution)/shard_map/ppermute | solution.py:489
  36.3 1.2 %shard_map.139 = (bf16[1024,512]{1,0:T(8,128)(2,1)S(1)}, bf16[64,512]{1,0:T(8,128)(2,1)S(1)}) custom-call(f32[4]{0:T(128)S(1)} %copy-done.5, bf16[2,256,256]{2,1,0:T(8,128)(2,1)S(1)} %copy-done, bf16[2,256,128]{2,1,0:T(8,128)(2,1)S(1)} %copy-done.1, bf16[2048,128]{1,0:T(8,128)(2,1)S(1)} %collective-permute-done.4.own, ...), custom_call_target="tpu_custom_call" | custom-call | flops 1000 | bytes 1000 | tf_op jit(solution)/shard_map/pallas_call | solution.py:347
  37.6 2.4 %shard_map.142 = (bf16[1024,128]{1,0:T(8,128)(2,1)S(1)}, bf16[1024,128]{1,0:T(8,128)(2,1)S(1)}) custom-call(bf16[2,256,256]{2,1,0:T(8,128)(2,1)S(1)} %copy-done, bf16[2,256,128]{2,1,0:T(8,128)(2,1)S(1)} %copy-done.1, bf16[2,256,256]{2,1,0:T(8,128)(2,1)S(1)} %copy-done.2, bf16[128,128]{1,0:T(8,128)(2,1)S(1)} %copy-done.3, ...), custom_call_target="tpu_custom_call" | custom-call | flops 1000 | bytes 1000 | tf_op jit(solution)/shard_map/pallas_call | solution.py:422
  40.0 1.0 %collective-permute-start.8 = (bf16[1024,128]{1,0:T(8,128)(2,1)S(1)}, bf16[1024,128]{1,0:T(8,128)(2,1)S(1)}, u32[]{:S(2)}, u32[]{:S(2)}) collective-permute-start(bf16[1024,128]{1,0:T(8,128)(2,1)S(1)} %get-tuple-element.37), channel_id=1, source_target_pairs={{0,1},{1,0},{2,3},{3,2},{4,5},{5,4},{6,7},{7,6},{8,9},{9,8},{10,11... | collective-permute-start | bytes 786440 | tf_op jit(solution)/shard_map/ppermute | solution.py:479
  40.9 2.4 %shard_map.140 = (bf16[1024,128]{1,0:T(8,128)(2,1)S(1)}, bf16[1024,128]{1,0:T(8,128)(2,1)S(1)}) custom-call(bf16[2,256,256]{2,1,0:T(8,128)(2,1)S(1)} %copy-done, bf16[2,256,128]{2,1,0:T(8,128)(2,1)S(1)} %copy-done.1, bf16[2,256,256]{2,1,0:T(8,128)(2,1)S(1)} %copy-done.2, bf16[128,128]{1,0:T(8,128)(2,1)S(1)} %copy-done.3, ...), custom_call_target="tpu_custom_call" | custom-call | flops 1000 | bytes 1000 | tf_op jit(solution)/shard_map/pallas_call | solution.py:422
  43.4 2.7 %collective-permute-start.10 = (bf16[512,128]{1,0:T(8,128)(2,1)S(1)}, bf16[512,128]{1,0:T(8,128)(2,1)S(1)}, u32[]{:S(2)}, u32[]{:S(2)}) collective-permute-start(bf16[512,128]{1,0:T(8,128)(2,1)S(1)} %slice.9), channel_id=1, source_target_pairs={{0,4},{4,8},{8,12},{12,0},{1,5},{5,9},{9,13},{13,1},{2,6},{6,10},{... | collective-permute-start | bytes 393224 | tf_op jit(solution)/shard_map/ppermute | solution.py:479
  46.1 0.5 shard_map.143.refs_5_
  46.6 0.5 shard_map.141.refs_4_
  47.0 5.2 %collective-permute-done.9.refs_5_ = bf16[1536,128]{1,0:T(8,128)(2,1)S(1)} collective-permute-done((bf16[1536,128]{1,0:T(8,128)(2,1)S(1)}, bf16[1536,128]{1,0:T(8,128)(2,1)S(1)}, u32[]{:S(2)}, u32[]{:S(2)}) %collective-permute-start.9) | collective-permute-done | bytes 393248 | tf_op jit(solution)/shard_map/ppermute | solution.py:479
  52.2 2.0 %shard_map.144 = (bf16[768,128]{1,0:T(8,128)(2,1)S(1)}, bf16[768,128]{1,0:T(8,128)(2,1)S(1)}) custom-call(bf16[2,256,256]{2,1,0:T(8,128)(2,1)S(1)} %copy-done, bf16[2,256,128]{2,1,0:T(8,128)(2,1)S(1)} %copy-done.1, bf16[2,256,256]{2,1,0:T(8,128)(2,1)S(1)} %copy-done.2, bf16[128,128]{1,0:T(8,128)(2,1)S(1)} %copy-done.3, ...), custom_call_target="tpu_custom_call" | custom-call | flops 1000 | bytes 1000 | tf_op jit(solution)/shard_map/pallas_call | solution.py:422
  54.3 0.4 collective-permute-done.10.refs_5_
  54.8 0.8 %shard_map.145 = (bf16[256,128]{1,0:T(8,128)(2,1)S(1)}, bf16[256,128]{1,0:T(8,128)(2,1)S(1)}) custom-call(bf16[2,256,256]{2,1,0:T(8,128)(2,1)S(1)} %copy-done, bf16[2,256,128]{2,1,0:T(8,128)(2,1)S(1)} %copy-done.1, bf16[2,256,256]{2,1,0:T(8,128)(2,1)S(1)} %copy-done.2, bf16[128,128]{1,0:T(8,128)(2,1)S(1)} %copy-done.3, ...), custom_call_target="tpu_custom_call" | custom-call | flops 1000 | bytes 1000 | tf_op jit(solution)/shard_map/pallas_call | solution.py:422
  55.7 1.2 %collective-permute-done.12.refs_3_ = bf16[256,128]{1,0:T(8,128)(2,1)S(1)} collective-permute-done((bf16[256,128]{1,0:T(8,128)(2,1)S(1)}, bf16[256,128]{1,0:T(8,128)(2,1)S(1)}, u32[]{:S(2)}, u32[]{:S(2)}) %collective-permute-start.12) | collective-permute-done | bytes 65568 | tf_op jit(solution)/shard_map/ppermute | solution.py:479
  56.9 1.1 %shard_map.146 = f32[1,3,2,32]{3,2,1,0:T(2,128)} custom-call(bf16[2064,128]{1,0:T(8,128)(2,1)S(1)} %collective-permute-done.3.refs_4_.load, bf16[2,64,64]{2,1,0:T(8,128)(2,1)S(1)} %copy-done.4, bf16[768,128]{1,0:T(8,128)(2,1)S(1)} %get-tuple-element.39.refs_0_, bf16[256,128]{1,0:T(8,128)(2,1)S(1)} %get-tuple-element.40.refs_1_, ...), custom_call_target="tpu_custom_call" | custom-call | flops 1000 | bytes 1000 | tf_op jit(solution)/shard_map/pallas_call | solution.py:466
  (27 shorter events, 0.5 us)
Async XLA Ops:
  0.7 12.7 %copy-start = (bf16[2,256,256]{2,1,0:T(8,128)(2,1)S(1)}, bf16[2,256,256]{2,1,0:T(8,128)(2,1)}, u32[]{:S(2)}) copy-start(bf16[2,256,256]{2,1,0:T(8,128)(2,1)} %constant.22.clone.table) | copy-start | bytes 786436
  0.7 12.7 %copy-start.1 = (bf16[2,256,128]{2,1,0:T(8,128)(2,1)S(1)}, bf16[2,256,128]{2,1,0:T(8,128)(2,1)}, u32[]{:S(2)}) copy-start(bf16[2,256,128]{2,1,0:T(8,128)(2,1)} %constant.23.clone.unpack) | copy-start | bytes 393220
  0.7 12.7 %copy-start.5 = (f32[4]{0:T(128)S(1)}, f32[4]{0:T(128)}, u32[]{:S(2)}) copy-start(f32[4]{0:T(128)} %weight.3) | copy-start | bytes 52
  3.2 3.8 %collective-permute-start.1 = (bf16[2048,128]{1,0:T(8,128)(2,1)S(1)}, bf16[2048,128]{1,0:T(8,128)(2,1)S(1)}, u32[]{:S(2)}, u32[]{:S(2)}) collective-permute-start(bf16[2048,128]{1,0:T(8,128)(2,1)S(1)} %get-tuple-element.25), channel_id=1, source_target_pairs={{0,1},{1,0},{2,3},{3,2},{4,5},{5,4},{6,7},{7,6},{8,9},{9,8},{10,11... | collective-permute-start | bytes 1572872 | tf_op jit(solution)/shard_map/ppermute | solution.py:479
  3.7 17.5 %collective-permute-start = (bf16[2064,128]{1,0:T(8,128)(2,1)S(1)}, bf16[2064,128]{1,0:T(8,128)(2,1)S(1)}, u32[]{:S(2)}, u32[]{:S(2)}) collective-permute-start(bf16[2064,128]{1,0:T(8,128)(2,1)S(1)} %get-tuple-element.24.refs_4_.load), channel_id=1, source_target_pairs={{0,4},{4,8},{8,12},{12,0},{1,5},{5,9},{9,13},{13,1},{2,6},{6,10},{... | collective-permute-start | bytes 1585160 | tf_op jit(solution)/shard_map/ppermute | solution.py:479
  10.1 27.5 %copy-start.2 = (bf16[2,256,256]{2,1,0:T(8,128)(2,1)S(1)}, bf16[2,256,256]{2,1,0:T(8,128)(2,1)}, u32[]{:S(2)}) copy-start(bf16[2,256,256]{2,1,0:T(8,128)(2,1)} %constant.24.clone.x_inverse) | copy-start | bytes 786436
  10.1 27.5 %copy-start.3 = (bf16[128,128]{1,0:T(8,128)(2,1)S(1)}, bf16[128,128]{1,0:T(8,128)(2,1)}, u32[]{:S(2)}) copy-start(bf16[128,128]{1,0:T(8,128)(2,1)} %constant.25.clone.y_inverse) | copy-start | bytes 98308
  10.1 3.3 %collective-permute-start.2 = (bf16[2048,128]{1,0:T(8,128)(2,1)S(1)}, bf16[2048,128]{1,0:T(8,128)(2,1)S(1)}, u32[]{:S(2)}, u32[]{:S(2)}) collective-permute-start(bf16[2048,128]{1,0:T(8,128)(2,1)S(1)} %get-tuple-element.28), channel_id=1, source_target_pairs={{0,1},{1,0},{2,3},{3,2},{4,5},{5,4},{6,7},{7,6},{8,9},{9,8},{10,11... | collective-permute-start | bytes 1572872 | tf_op jit(solution)/shard_map/ppermute | solution.py:479
  10.3 21.6 %collective-permute-start.7 = (bf16[2048,128]{1,0:T(8,128)(2,1)S(1)}, bf16[2048,128]{1,0:T(8,128)(2,1)S(1)}, u32[]{:S(2)}, u32[]{:S(2)}) collective-permute-start(bf16[2048,128]{1,0:T(8,128)(2,1)S(1)} %get-tuple-element.25), channel_id=1, source_target_pairs={{0,5},{1,4},{4,9},{5,8},{8,13},{9,12},{12,1},{13,0},{2,7},{3,6},{6... | collective-permute-start | bytes 1572872 | tf_op jit(solution)/shard_map/ppermute | solution.py:489
  11.8 20.2 %collective-permute-start.4 = (bf16[2048,128]{1,0:T(8,128)(2,1)S(1)}, bf16[2048,128]{1,0:T(8,128)(2,1)S(1)}, u32[]{:S(2)}, u32[]{:S(2)}) collective-permute-start(bf16[2048,128]{1,0:T(8,128)(2,1)S(1)} %get-tuple-element.27.own), channel_id=1, source_target_pairs={{0,2},{2,0},{1,3},{3,1},{4,6},{6,4},{5,7},{7,5},{8,10},{10,8},{9,1... | collective-permute-start | bytes 1572872 | tf_op jit(solution)/shard_map/ppermute | solution.py:479
  13.3 23.0 %collective-permute-start.5 = (bf16[2048,128]{1,0:T(8,128)(2,1)S(1)}, bf16[2048,128]{1,0:T(8,128)(2,1)S(1)}, u32[]{:S(2)}, u32[]{:S(2)}) collective-permute-start(bf16[2048,128]{1,0:T(8,128)(2,1)S(1)} %get-tuple-element.28), channel_id=1, source_target_pairs={{0,3},{1,2},{2,1},{3,0},{4,7},{5,6},{6,5},{7,4},{8,11},{9,10},{10,... | collective-permute-start | bytes 1572872 | tf_op jit(solution)/shard_map/ppermute | solution.py:489
  21.2 25.8 %collective-permute-start.3 = (bf16[2064,128]{1,0:T(8,128)(2,1)S(1)}, bf16[2064,128]{1,0:T(8,128)(2,1)S(1)}, u32[]{:S(2)}, u32[]{:S(2)}) collective-permute-start(bf16[2064,128]{1,0:T(8,128)(2,1)S(1)} %collective-permute-done.refs_4_.load), channel_id=1, source_target_pairs={{0,4},{4,8},{8,12},{12,0},{1,5},{5,9},{9,13},{13,1},{2,6},{6,10},{... | collective-permute-start | bytes 1585160 | tf_op jit(solution)/shard_map/ppermute | solution.py:479
  32.0 20.2 %collective-permute-start.9 = (bf16[1536,128]{1,0:T(8,128)(2,1)S(1)}, bf16[1536,128]{1,0:T(8,128)(2,1)S(1)}, u32[]{:S(2)}, u32[]{:S(2)}) collective-permute-start(bf16[1536,128]{1,0:T(8,128)(2,1)S(1)} %slice.8), channel_id=1, source_target_pairs={{0,4},{4,8},{8,12},{12,0},{1,5},{5,9},{9,13},{13,1},{2,6},{6,10},{... | collective-permute-start | bytes 1179656 | tf_op jit(solution)/shard_map/ppermute | solution.py:479
  40.0 6.1 %copy-start.4 = (bf16[2,64,64]{2,1,0:T(8,128)(2,1)S(1)}, bf16[2,64,64]{2,1,0:T(8,128)(2,1)}, u32[]{:S(2)}) copy-start(bf16[2,64,64]{2,1,0:T(8,128)(2,1)} %constant.26.clone.table) | copy-start | bytes 49156
  40.0 6.1 %collective-permute-start.8 = (bf16[1024,128]{1,0:T(8,128)(2,1)S(1)}, bf16[1024,128]{1,0:T(8,128)(2,1)S(1)}, u32[]{:S(2)}, u32[]{:S(2)}) collective-permute-start(bf16[1024,128]{1,0:T(8,128)(2,1)S(1)} %get-tuple-element.37), channel_id=1, source_target_pairs={{0,1},{1,0},{2,3},{3,2},{4,5},{5,4},{6,7},{7,6},{8,9},{9,8},{10,11... | collective-permute-start | bytes 786440 | tf_op jit(solution)/shard_map/ppermute | solution.py:479
  43.3 3.2 %collective-permute-start.6 = (bf16[1024,128]{1,0:T(8,128)(2,1)S(1)}, bf16[1024,128]{1,0:T(8,128)(2,1)S(1)}, u32[]{:S(2)}, u32[]{:S(2)}) collective-permute-start(bf16[1024,128]{1,0:T(8,128)(2,1)S(1)} %get-tuple-element.35), channel_id=1, source_target_pairs={{0,1},{1,0},{2,3},{3,2},{4,5},{5,4},{6,7},{7,6},{8,9},{9,8},{10,11... | collective-permute-start | bytes 786440 | tf_op jit(solution)/shard_map/ppermute | solution.py:479
  43.4 11.4 %collective-permute-start.10 = (bf16[512,128]{1,0:T(8,128)(2,1)S(1)}, bf16[512,128]{1,0:T(8,128)(2,1)S(1)}, u32[]{:S(2)}, u32[]{:S(2)}) collective-permute-start(bf16[512,128]{1,0:T(8,128)(2,1)S(1)} %slice.9), channel_id=1, source_target_pairs={{0,4},{4,8},{8,12},{12,0},{1,5},{5,9},{9,13},{13,1},{2,6},{6,10},{... | collective-permute-start | bytes 393224 | tf_op jit(solution)/shard_map/ppermute | solution.py:479
  54.3 2.7 %collective-permute-start.11 = (bf16[768,128]{1,0:T(8,128)(2,1)S(1)}, bf16[768,128]{1,0:T(8,128)(2,1)S(1)}, u32[]{:S(2)}, u32[]{:S(2)}) collective-permute-start(bf16[768,128]{1,0:T(8,128)(2,1)S(1)} %get-tuple-element.41), channel_id=1, source_target_pairs={{0,1},{1,0},{2,3},{3,2},{4,5},{5,4},{6,7},{7,6},{8,9},{9,8},{10,11... | collective-permute-start | bytes 589832 | tf_op jit(solution)/shard_map/ppermute | solution.py:479
  55.6 1.3 %collective-permute-start.12 = (bf16[256,128]{1,0:T(8,128)(2,1)S(1)}, bf16[256,128]{1,0:T(8,128)(2,1)S(1)}, u32[]{:S(2)}, u32[]{:S(2)}) collective-permute-start(bf16[256,128]{1,0:T(8,128)(2,1)S(1)} %get-tuple-element.42), channel_id=1, source_target_pairs={{0,1},{1,0},{2,3},{3,2},{4,5},{5,4},{6,7},{7,6},{8,9},{9,8},{10,11... | collective-permute-start | bytes 196616 | tf_op jit(solution)/shard_map/ppermute | solution.py:479

commit v4 on v3

--- a/solution.py
+++ b/solution.py
@@ -257,11 +257,11 @@
     scratch = [
         pltpu.SMEM(scalar.shape, jnp.int32),
         pltpu.VMEM(occ.shape[1:], jnp.int32),
-        pltpu.VMEM((cells * ((s.size if rotated else cells) + 8), lanes), F32),
+        pltpu.VMEM(((cells + 1) * ((s.size if rotated else cells) + 8), lanes), F32),
     ]
     scratch += [pltpu.VMEM(t[name].shape[-2:], BF16) for name in names]
     if rotated:
-        scratch.append(pltpu.VMEM((cells * (cells + 8), lanes), F32))
+        scratch.append(pltpu.VMEM(((cells + 1) * (cells + 8), lanes), F32))
     scratch.append(pltpu.SemaphoreType.DMA((1 + len(names) + pieces,)))
     rows = [s.own * s.size + (0 if rotated else s.extra)]
     rows += [(high - low) * s.size for low, high in zip(cuts, cuts[1:])]
@@ -450,7 +450,7 @@
     row = jnp.max(best, axis=0, keepdims=True)
     row = jnp.maximum(row, pltpu.roll(row, s.back // 2, 1)) * (1.0 / (cells * math.sqrt(cells)))
     plane = lax.broadcasted_iota(jnp.int32, row.shape, 1) % s.slab + core * s.slab
-    extent = load[s.own * s.size:s.own * s.size + 1, :].astype(F32)
+    extent = load[s.own * s.size:, :].astype(F32)[:1]
     row = jnp.where(plane.astype(F32) < extent, row, 0.0)
     if not last:
         out[...] = row
@@ -468,7 +468,7 @@
         in_specs=[vmem] * (2 + len(parts) + len(earlier)),
         out_specs=vmem,
         out_shape=jax.ShapeDtypeStruct(shape, F32),
-        scratch_shapes=[pltpu.VMEM((s.cells * (s.cells // 2 + 8), s.back), F32)],
+        scratch_shapes=[pltpu.VMEM(((s.cells + 1) * (s.cells // 2 + 8), s.back), F32)],
         compiler_params=params(),
         cost_estimate=COST,
     )(load, t["z_inverse"], *parts, *earlier)

time: 58.2 us -> 58.2 us (level)
    ppermute x2, waiting for transfers between devices: 15 us -> 15.9 us  [passed_across(): return lax.ppermute(value, (axis, 'fft'), pairs)]
    ppermute x11, waiting for transfers between devices: 13.4 us -> 12.6 us  [passed_along(): lax.ppermute(value, axis, [(source, (source + steps) % count) for source...]
where the time goes in v4:
time: 58.2 us; the launch traced here: 58 us
  waiting for transfers between devices  28.5 us (49%)
  Pallas kernels  17.7 us (30%)
  starting transfers between devices  10.3 us (18%)
  between operations  1.5 us (3%)
    ppermute x2, waiting for transfers between devices, passed_across(): return lax.ppermute(value, (axis, 'fft'), pairs)  15.9 us
    ppermute x11, waiting for transfers between devices, passed_along(): lax.ppermute(value, axis, [(source, (source + steps) % count) for source...  12.6 us
    ppermute x11, starting transfers between devices, passed_along(): lax.ppermute(value, axis, [(source, (source + steps) % count) for source...  8.77 us
    pallas_call x4, Pallas kernels, cross_back(): pl.pallas_call(partial(cross_kernel, s, cuts, planes, per), in_specs=[vme...  7.62 us
    pallas_call x2, Pallas kernels, sections(): pl.pallas_call(partial(section_kernel, s, pieces, rotated, cuts), in_spec...  5.54 us
    pallas_call x2, Pallas kernels, spectrum(): pl.pallas_call(partial(spectrum_kernel, s, cuts, per), in_specs=[pl.Block...  2.49 us
    pallas_call x3, Pallas kernels, peaks(): pl.pallas_call(partial(peak_kernel, s, len(parts), last), in_specs=[vmem]...  2.03 us
    ppermute x2, starting transfers between devices, passed_across(): return lax.ppermute(value, (axis, 'fft'), pairs)  1.52 us
  transfers between devices with their start and end apart: 13, of which 6 were waited for; matrix products, arithmetic and copies ran while one was open for 0% of the time, Pallas kernels for 24%

profile of v4, /device:TPU:0, one launch (start us, length us, event | category | flops | bytes accessed | tf_op | source)
XLA Modules:
  0.0 58.0 jit_solution(4924884613853735894)
XLA Ops:
  0.7 2.5 %shard_map.136 = (bf16[2064,128]{1,0:T(8,128)(2,1)S(1)}, bf16[2048,128]{1,0:T(8,128)(2,1)S(1)}) custom-call(s32[1,4,32,4096]{3,2,1,0:T(8,128)} %occ.1, s32[1]{0:T(128)S(6)} %copy.16.scalar, bf16[2,2,128,128]{3,2,1,0:T(8,128)(2,1)} %constant.18.clone.refs_0_, bf16[2,128,128]{2,1,0:T(8,128)(2,1)} %constant.19.clone.refs_1_), custom_call_target="tpu_custom_call" | custom-call | flops 1000 | bytes 1000 | tf_op jit(solution)/shard_map/pallas_call | solution.py:268
  3.2 0.5 collective-permute-start.1
  3.7 2.6 %collective-permute-start = (bf16[2064,128]{1,0:T(8,128)(2,1)S(1)}, bf16[2064,128]{1,0:T(8,128)(2,1)S(1)}, u32[]{:S(2)}, u32[]{:S(2)}) collective-permute-start(bf16[2064,128]{1,0:T(8,128)(2,1)S(1)} %get-tuple-element.24.refs_4_.load), channel_id=1, source_target_pairs={{0,4},{4,8},{8,12},{12,0},{1,5},{5,9},{9,13},{13,1},{2,6},{6,10},{... | collective-permute-start | bytes 1585160 | tf_op jit(solution)/shard_map/ppermute | solution.py:479
  7.0 3.1 %shard_map.137 = (bf16[2048,128]{1,0:T(8,128)(2,1)S(1)}, bf16[2048,128]{1,0:T(8,128)(2,1)S(1)}) custom-call(s32[1,4,32,4096]{3,2,1,0:T(8,128)} %occ.2, s32[1]{0:T(128)S(6)} %copy.15.scalar, bf16[2,2,128,128]{3,2,1,0:T(8,128)(2,1)} %constant.18.clone.refs_0_, bf16[2,128,128]{2,1,0:T(8,128)(2,1)} %constant.19.clone.refs_1_, ...), custom_call_target="tpu_custom_call" | custom-call | flops 1000 | bytes 1000 | tf_op jit(solution)/shard_map/pallas_call | solution.py:268
  10.1 0.2 collective-permute-start.2
  10.3 1.5 %collective-permute-start.7 = (bf16[2048,128]{1,0:T(8,128)(2,1)S(1)}, bf16[2048,128]{1,0:T(8,128)(2,1)S(1)}, u32[]{:S(2)}, u32[]{:S(2)}) collective-permute-start(bf16[2048,128]{1,0:T(8,128)(2,1)S(1)} %get-tuple-element.25), channel_id=1, source_target_pairs={{0,5},{1,4},{4,9},{5,8},{8,13},{9,12},{12,1},{13,0},{2,7},{3,6},{6... | collective-permute-start | bytes 1572872 | tf_op jit(solution)/shard_map/ppermute | solution.py:489
  11.8 2.4 %collective-permute-start.4 = (bf16[2048,128]{1,0:T(8,128)(2,1)S(1)}, bf16[2048,128]{1,0:T(8,128)(2,1)S(1)}, u32[]{:S(2)}, u32[]{:S(2)}) collective-permute-start(bf16[2048,128]{1,0:T(8,128)(2,1)S(1)} %get-tuple-element.27.own), channel_id=1, source_target_pairs={{0,2},{2,0},{1,3},{3,1},{4,6},{6,4},{5,7},{7,5},{8,10},{10,8},{9,1... | collective-permute-start | bytes 1572872 | tf_op jit(solution)/shard_map/ppermute | solution.py:479
  14.2 1.3 %shard_map.138 = (bf16[1024,512]{1,0:T(8,128)(2,1)S(1)}, bf16[64,512]{1,0:T(8,128)(2,1)S(1)}) custom-call(f32[4]{0:T(128)S(1)} %copy-done.5, bf16[2,256,256]{2,1,0:T(8,128)(2,1)S(1)} %copy-done, bf16[2,256,128]{2,1,0:T(8,128)(2,1)S(1)} %copy-done.1, bf16[2048,128]{1,0:T(8,128)(2,1)S(1)} %get-tuple-element.27.own, ...), custom_call_target="tpu_custom_call" | custom-call | flops 1000 | bytes 1000 | tf_op jit(solution)/shard_map/pallas_call | solution.py:347
  15.5 5.7 %collective-permute-done.refs_4_.load = bf16[2064,128]{1,0:T(8,128)(2,1)S(1)} collective-permute-done((bf16[2064,128]{1,0:T(8,128)(2,1)S(1)}, bf16[2064,128]{1,0:T(8,128)(2,1)S(1)}, u32[]{:S(2)}, u32[]{:S(2)}) %collective-permute-start) | collective-permute-done | bytes 528416 | tf_op jit(solution)/shard_map/ppermute | solution.py:479
  21.2 10.7 %collective-permute-done.7.refs_5_ = bf16[2048,128]{1,0:T(8,128)(2,1)S(1)} collective-permute-done((bf16[2048,128]{1,0:T(8,128)(2,1)S(1)}, bf16[2048,128]{1,0:T(8,128)(2,1)S(1)}, u32[]{:S(2)}, u32[]{:S(2)}) %collective-permute-start.7) | collective-permute-done | bytes 524320 | tf_op jit(solution)/shard_map/ppermute | solution.py:489
  32.1 5.2 %collective-permute-done.5.refs_0_ = bf16[2048,128]{1,0:T(8,128)(2,1)S(1)} collective-permute-done((bf16[2048,128]{1,0:T(8,128)(2,1)S(1)}, bf16[2048,128]{1,0:T(8,128)(2,1)S(1)}, u32[]{:S(2)}, u32[]{:S(2)}) %collective-permute-start.5) | collective-permute-done | bytes 524320 | tf_op jit(solution)/shard_map/ppermute | solution.py:489
  37.2 1.2 %shard_map.139 = (bf16[1024,512]{1,0:T(8,128)(2,1)S(1)}, bf16[64,512]{1,0:T(8,128)(2,1)S(1)}) custom-call(f32[4]{0:T(128)S(1)} %copy-done.5, bf16[2,256,256]{2,1,0:T(8,128)(2,1)S(1)} %copy-done, bf16[2,256,128]{2,1,0:T(8,128)(2,1)S(1)} %copy-done.1, bf16[2048,128]{1,0:T(8,128)(2,1)S(1)} %collective-permute-done.4.own, ...), custom_call_target="tpu_custom_call" | custom-call | flops 1000 | bytes 1000 | tf_op jit(solution)/shard_map/pallas_call | solution.py:347
  38.5 2.4 %shard_map.142 = (bf16[1024,128]{1,0:T(8,128)(2,1)S(1)}, bf16[1024,128]{1,0:T(8,128)(2,1)S(1)}) custom-call(bf16[2,256,256]{2,1,0:T(8,128)(2,1)S(1)} %copy-done, bf16[2,256,128]{2,1,0:T(8,128)(2,1)S(1)} %copy-done.1, bf16[2,256,256]{2,1,0:T(8,128)(2,1)S(1)} %copy-done.2, bf16[128,128]{1,0:T(8,128)(2,1)S(1)} %copy-done.3, ...), custom_call_target="tpu_custom_call" | custom-call | flops 1000 | bytes 1000 | tf_op jit(solution)/shard_map/pallas_call | solution.py:422
  40.9 0.6 %collective-permute-start.8 = (bf16[1024,128]{1,0:T(8,128)(2,1)S(1)}, bf16[1024,128]{1,0:T(8,128)(2,1)S(1)}, u32[]{:S(2)}, u32[]{:S(2)}) collective-permute-start(bf16[1024,128]{1,0:T(8,128)(2,1)S(1)} %get-tuple-element.37), channel_id=1, source_target_pairs={{0,1},{1,0},{2,3},{3,2},{4,5},{5,4},{6,7},{7,6},{8,9},{9,8},{10,11... | collective-permute-start | bytes 786440 | tf_op jit(solution)/shard_map/ppermute | solution.py:479
  41.6 2.4 %shard_map.140 = (bf16[1024,128]{1,0:T(8,128)(2,1)S(1)}, bf16[1024,128]{1,0:T(8,128)(2,1)S(1)}) custom-call(bf16[2,256,256]{2,1,0:T(8,128)(2,1)S(1)} %copy-done, bf16[2,256,128]{2,1,0:T(8,128)(2,1)S(1)} %copy-done.1, bf16[2,256,256]{2,1,0:T(8,128)(2,1)S(1)} %copy-done.2, bf16[128,128]{1,0:T(8,128)(2,1)S(1)} %copy-done.3, ...), custom_call_target="tpu_custom_call" | custom-call | flops 1000 | bytes 1000 | tf_op jit(solution)/shard_map/pallas_call | solution.py:422
  44.0 2.1 %collective-permute-start.10 = (bf16[512,128]{1,0:T(8,128)(2,1)S(1)}, bf16[512,128]{1,0:T(8,128)(2,1)S(1)}, u32[]{:S(2)}, u32[]{:S(2)}) collective-permute-start(bf16[512,128]{1,0:T(8,128)(2,1)S(1)} %slice.9), channel_id=1, source_target_pairs={{0,4},{4,8},{8,12},{12,0},{1,5},{5,9},{9,13},{13,1},{2,6},{6,10},{... | collective-permute-start | bytes 393224 | tf_op jit(solution)/shard_map/ppermute | solution.py:479
  46.1 0.5 shard_map.143.refs_5_
  46.6 0.5 shard_map.141.refs_4_
  47.0 5.2 %collective-permute-done.9.refs_5_ = bf16[1536,128]{1,0:T(8,128)(2,1)S(1)} collective-permute-done((bf16[1536,128]{1,0:T(8,128)(2,1)S(1)}, bf16[1536,128]{1,0:T(8,128)(2,1)S(1)}, u32[]{:S(2)}, u32[]{:S(2)}) %collective-permute-start.9) | collective-permute-done | bytes 393248 | tf_op jit(solution)/shard_map/ppermute | solution.py:479
  52.2 2.0 %shard_map.144 = (bf16[768,128]{1,0:T(8,128)(2,1)S(1)}, bf16[768,128]{1,0:T(8,128)(2,1)S(1)}) custom-call(bf16[2,256,256]{2,1,0:T(8,128)(2,1)S(1)} %copy-done, bf16[2,256,128]{2,1,0:T(8,128)(2,1)S(1)} %copy-done.1, bf16[2,256,256]{2,1,0:T(8,128)(2,1)S(1)} %copy-done.2, bf16[128,128]{1,0:T(8,128)(2,1)S(1)} %copy-done.3, ...), custom_call_target="tpu_custom_call" | custom-call | flops 1000 | bytes 1000 | tf_op jit(solution)/shard_map/pallas_call | solution.py:422
  54.3 0.4 collective-permute-done.10.refs_5_
  54.8 0.8 %shard_map.145 = (bf16[256,128]{1,0:T(8,128)(2,1)S(1)}, bf16[256,128]{1,0:T(8,128)(2,1)S(1)}) custom-call(bf16[2,256,256]{2,1,0:T(8,128)(2,1)S(1)} %copy-done, bf16[2,256,128]{2,1,0:T(8,128)(2,1)S(1)} %copy-done.1, bf16[2,256,256]{2,1,0:T(8,128)(2,1)S(1)} %copy-done.2, bf16[128,128]{1,0:T(8,128)(2,1)S(1)} %copy-done.3, ...), custom_call_target="tpu_custom_call" | custom-call | flops 1000 | bytes 1000 | tf_op jit(solution)/shard_map/pallas_call | solution.py:422
  55.7 1.2 %collective-permute-done.12.refs_3_ = bf16[256,128]{1,0:T(8,128)(2,1)S(1)} collective-permute-done((bf16[256,128]{1,0:T(8,128)(2,1)S(1)}, bf16[256,128]{1,0:T(8,128)(2,1)S(1)}, u32[]{:S(2)}, u32[]{:S(2)}) %collective-permute-start.12) | collective-permute-done | bytes 65568 | tf_op jit(solution)/shard_map/ppermute | solution.py:479
  56.9 1.1 %shard_map.146 = f32[1,3,2,32]{3,2,1,0:T(2,128)} custom-call(bf16[2064,128]{1,0:T(8,128)(2,1)S(1)} %collective-permute-done.3.refs_4_.load, bf16[2,64,64]{2,1,0:T(8,128)(2,1)S(1)} %copy-done.4, bf16[768,128]{1,0:T(8,128)(2,1)S(1)} %get-tuple-element.39.refs_0_, bf16[256,128]{1,0:T(8,128)(2,1)S(1)} %get-tuple-element.40.refs_1_, ...), custom_call_target="tpu_custom_call" | custom-call | flops 1000 | bytes 1000 | tf_op jit(solution)/shard_map/pallas_call | solution.py:466
  (27 shorter events, 0.4 us)
Async XLA Ops:
  0.7 13.6 %copy-start = (bf16[2,256,256]{2,1,0:T(8,128)(2,1)S(1)}, bf16[2,256,256]{2,1,0:T(8,128)(2,1)}, u32[]{:S(2)}) copy-start(bf16[2,256,256]{2,1,0:T(8,128)(2,1)} %constant.22.clone.table) | copy-start | bytes 786436
  0.7 13.6 %copy-start.1 = (bf16[2,256,128]{2,1,0:T(8,128)(2,1)S(1)}, bf16[2,256,128]{2,1,0:T(8,128)(2,1)}, u32[]{:S(2)}) copy-start(bf16[2,256,128]{2,1,0:T(8,128)(2,1)} %constant.23.clone.unpack) | copy-start | bytes 393220
  0.7 13.5 %copy-start.5 = (f32[4]{0:T(128)S(1)}, f32[4]{0:T(128)}, u32[]{:S(2)}) copy-start(f32[4]{0:T(128)} %weight.3) | copy-start | bytes 52
  3.2 3.8 %collective-permute-start.1 = (bf16[2048,128]{1,0:T(8,128)(2,1)S(1)}, bf16[2048,128]{1,0:T(8,128)(2,1)S(1)}, u32[]{:S(2)}, u32[]{:S(2)}) collective-permute-start(bf16[2048,128]{1,0:T(8,128)(2,1)S(1)} %get-tuple-element.25), channel_id=1, source_target_pairs={{0,1},{1,0},{2,3},{3,2},{4,5},{5,4},{6,7},{7,6},{8,9},{9,8},{10,11... | collective-permute-start | bytes 1572872 | tf_op jit(solution)/shard_map/ppermute | solution.py:479
  3.7 17.5 %collective-permute-start = (bf16[2064,128]{1,0:T(8,128)(2,1)S(1)}, bf16[2064,128]{1,0:T(8,128)(2,1)S(1)}, u32[]{:S(2)}, u32[]{:S(2)}) collective-permute-start(bf16[2064,128]{1,0:T(8,128)(2,1)S(1)} %get-tuple-element.24.refs_4_.load), channel_id=1, source_target_pairs={{0,4},{4,8},{8,12},{12,0},{1,5},{5,9},{9,13},{13,1},{2,6},{6,10},{... | collective-permute-start | bytes 1585160 | tf_op jit(solution)/shard_map/ppermute | solution.py:479
  10.1 28.4 %copy-start.2 = (bf16[2,256,256]{2,1,0:T(8,128)(2,1)S(1)}, bf16[2,256,256]{2,1,0:T(8,128)(2,1)}, u32[]{:S(2)}) copy-start(bf16[2,256,256]{2,1,0:T(8,128)(2,1)} %constant.24.clone.x_inverse) | copy-start | bytes 786436
  10.1 28.4 %copy-start.3 = (bf16[128,128]{1,0:T(8,128)(2,1)S(1)}, bf16[128,128]{1,0:T(8,128)(2,1)}, u32[]{:S(2)}) copy-start(bf16[128,128]{1,0:T(8,128)(2,1)} %constant.25.clone.y_inverse) | copy-start | bytes 98308
  10.1 4.1 %collective-permute-start.2 = (bf16[2048,128]{1,0:T(8,128)(2,1)S(1)}, bf16[2048,128]{1,0:T(8,128)(2,1)S(1)}, u32[]{:S(2)}, u32[]{:S(2)}) collective-permute-start(bf16[2048,128]{1,0:T(8,128)(2,1)S(1)} %get-tuple-element.28), channel_id=1, source_target_pairs={{0,1},{1,0},{2,3},{3,2},{4,5},{5,4},{6,7},{7,6},{8,9},{9,8},{10,11... | collective-permute-start | bytes 1572872 | tf_op jit(solution)/shard_map/ppermute | solution.py:479
  10.3 21.6 %collective-permute-start.7 = (bf16[2048,128]{1,0:T(8,128)(2,1)S(1)}, bf16[2048,128]{1,0:T(8,128)(2,1)S(1)}, u32[]{:S(2)}, u32[]{:S(2)}) collective-permute-start(bf16[2048,128]{1,0:T(8,128)(2,1)S(1)} %get-tuple-element.25), channel_id=1, source_target_pairs={{0,5},{1,4},{4,9},{5,8},{8,13},{9,12},{12,1},{13,0},{2,7},{3,6},{6... | collective-permute-start | bytes 1572872 | tf_op jit(solution)/shard_map/ppermute | solution.py:489
  11.8 20.2 %collective-permute-start.4 = (bf16[2048,128]{1,0:T(8,128)(2,1)S(1)}, bf16[2048,128]{1,0:T(8,128)(2,1)S(1)}, u32[]{:S(2)}, u32[]{:S(2)}) collective-permute-start(bf16[2048,128]{1,0:T(8,128)(2,1)S(1)} %get-tuple-element.27.own), channel_id=1, source_target_pairs={{0,2},{2,0},{1,3},{3,1},{4,6},{6,4},{5,7},{7,5},{8,10},{10,8},{9,1... | collective-permute-start | bytes 1572872 | tf_op jit(solution)/shard_map/ppermute | solution.py:479
  14.2 23.0 %collective-permute-start.5 = (bf16[2048,128]{1,0:T(8,128)(2,1)S(1)}, bf16[2048,128]{1,0:T(8,128)(2,1)S(1)}, u32[]{:S(2)}, u32[]{:S(2)}) collective-permute-start(bf16[2048,128]{1,0:T(8,128)(2,1)S(1)} %get-tuple-element.28), channel_id=1, source_target_pairs={{0,3},{1,2},{2,1},{3,0},{4,7},{5,6},{6,5},{7,4},{8,11},{9,10},{10,... | collective-permute-start | bytes 1572872 | tf_op jit(solution)/shard_map/ppermute | solution.py:489
  21.2 25.8 %collective-permute-start.3 = (bf16[2064,128]{1,0:T(8,128)(2,1)S(1)}, bf16[2064,128]{1,0:T(8,128)(2,1)S(1)}, u32[]{:S(2)}, u32[]{:S(2)}) collective-permute-start(bf16[2064,128]{1,0:T(8,128)(2,1)S(1)} %collective-permute-done.refs_4_.load), channel_id=1, source_target_pairs={{0,4},{4,8},{8,12},{12,0},{1,5},{5,9},{9,13},{13,1},{2,6},{6,10},{... | collective-permute-start | bytes 1585160 | tf_op jit(solution)/shard_map/ppermute | solution.py:479
  32.0 20.2 %collective-permute-start.9 = (bf16[1536,128]{1,0:T(8,128)(2,1)S(1)}, bf16[1536,128]{1,0:T(8,128)(2,1)S(1)}, u32[]{:S(2)}, u32[]{:S(2)}) collective-permute-start(bf16[1536,128]{1,0:T(8,128)(2,1)S(1)} %slice.8), channel_id=1, source_target_pairs={{0,4},{4,8},{8,12},{12,0},{1,5},{5,9},{9,13},{13,1},{2,6},{6,10},{... | collective-permute-start | bytes 1179656 | tf_op jit(solution)/shard_map/ppermute | solution.py:479
  40.9 5.2 %copy-start.4 = (bf16[2,64,64]{2,1,0:T(8,128)(2,1)S(1)}, bf16[2,64,64]{2,1,0:T(8,128)(2,1)}, u32[]{:S(2)}) copy-start(bf16[2,64,64]{2,1,0:T(8,128)(2,1)} %constant.26.clone.table) | copy-start | bytes 49156
  40.9 5.2 %collective-permute-start.8 = (bf16[1024,128]{1,0:T(8,128)(2,1)S(1)}, bf16[1024,128]{1,0:T(8,128)(2,1)S(1)}, u32[]{:S(2)}, u32[]{:S(2)}) collective-permute-start(bf16[1024,128]{1,0:T(8,128)(2,1)S(1)} %get-tuple-element.37), channel_id=1, source_target_pairs={{0,1},{1,0},{2,3},{3,2},{4,5},{5,4},{6,7},{7,6},{8,9},{9,8},{10,11... | collective-permute-start | bytes 786440 | tf_op jit(solution)/shard_map/ppermute | solution.py:479
  43.9 2.6 %collective-permute-start.6 = (bf16[1024,128]{1,0:T(8,128)(2,1)S(1)}, bf16[1024,128]{1,0:T(8,128)(2,1)S(1)}, u32[]{:S(2)}, u32[]{:S(2)}) collective-permute-start(bf16[1024,128]{1,0:T(8,128)(2,1)S(1)} %get-tuple-element.35), channel_id=1, source_target_pairs={{0,1},{1,0},{2,3},{3,2},{4,5},{5,4},{6,7},{7,6},{8,9},{9,8},{10,11... | collective-permute-start | bytes 786440 | tf_op jit(solution)/shard_map/ppermute | solution.py:479
  44.0 10.7 %collective-permute-start.10 = (bf16[512,128]{1,0:T(8,128)(2,1)S(1)}, bf16[512,128]{1,0:T(8,128)(2,1)S(1)}, u32[]{:S(2)}, u32[]{:S(2)}) collective-permute-start(bf16[512,128]{1,0:T(8,128)(2,1)S(1)} %slice.9), channel_id=1, source_target_pairs={{0,4},{4,8},{8,12},{12,0},{1,5},{5,9},{9,13},{13,1},{2,6},{6,10},{... | collective-permute-start | bytes 393224 | tf_op jit(solution)/shard_map/ppermute | solution.py:479
  54.3 2.7 %collective-permute-start.11 = (bf16[768,128]{1,0:T(8,128)(2,1)S(1)}, bf16[768,128]{1,0:T(8,128)(2,1)S(1)}, u32[]{:S(2)}, u32[]{:S(2)}) collective-permute-start(bf16[768,128]{1,0:T(8,128)(2,1)S(1)} %get-tuple-element.41), channel_id=1, source_target_pairs={{0,1},{1,0},{2,3},{3,2},{4,5},{5,4},{6,7},{7,6},{8,9},{9,8},{10,11... | collective-permute-start | bytes 589832 | tf_op jit(solution)/shard_map/ppermute | solution.py:479
  55.6 1.3 %collective-permute-start.12 = (bf16[256,128]{1,0:T(8,128)(2,1)S(1)}, bf16[256,128]{1,0:T(8,128)(2,1)S(1)}, u32[]{:S(2)}, u32[]{:S(2)}) collective-permute-start(bf16[256,128]{1,0:T(8,128)(2,1)S(1)} %get-tuple-element.42), channel_id=1, source_target_pairs={{0,1},{1,0},{2,3},{3,2},{4,5},{5,4},{6,7},{7,6},{8,9},{9,8},{10,11... | collective-permute-start | bytes 196616 | tf_op jit(solution)/shard_map/ppermute | solution.py:479

commit v5 on v4

--- a/solution.py
+++ b/solution.py
@@ -500,18 +500,17 @@
     swapped = lambda parts: [passed_along(part, "fft") for part in parts]
 
     own, *away = sections(s, t, receptor_occupancy, receptor_extent, False, s.whole)
-    others = swapped(away)
-    receptors = [(own, others)]
+    receptors = []
     receptors.append((passed_along(own, "rec"), [passed_across(part, "rec") for part in away]))
 
-    ligand_occupancy = after(ligand_occupancy, *others)
+    ligand_occupancy = after(ligand_occupancy, *away)
     pose, *pose_away = sections(s, t, ligand_occupancy, rot_index, True, s.whole)
-    pose_others = swapped(pose_away)
+    pose_others = swapped([after(part, receptors[0][0]) for part in pose_away])
     next_pose, next_others = passed_along(pose, "lig"), [passed_across(part, "lig") for part in pose_away]
+    receptors.insert(0, (own, swapped([after(part, next_pose) for part in away])))
     spectra = [spectrum(s, t, channel_weight, pose, pose_others, s.whole)]
 
     own, others = receptors[1]
-    own = after(own, spectra[0][0])
     receptors[1] = (own, others)
     cuts = [others[0][low * s.size:high * s.size] for low, high in zip(s.parts, s.parts[1:])]
     receptors.append((passed_along(own, "rec"), [passed_along(part, "rec") for part in cuts]))

time: 58.2 us -> 57.7 us (level)
  waiting for transfers between devices: 28.5 us -> 27.4 us
  Pallas kernels: 17.7 us -> 18.5 us
    ppermute x2, waiting for transfers between devices: 15.9 us -> 7.09 us  [passed_across(): return lax.ppermute(value, (axis, 'fft'), pairs)]
    ppermute x11, waiting for transfers between devices: 12.6 us -> 20.3 us  [passed_along(): lax.ppermute(value, axis, [(source, (source + steps) % count) for source...]
    pallas_call x2, Pallas kernels: 5.54 us -> 6.36 us  [sections(): pl.pallas_call(partial(section_kernel, s, pieces, rotated, cuts), in_spec...]
  transfers between devices with their start and end apart: 13 -> 13, of which waited for: 6 -> 6; matrix products, arithmetic and copies ran while one was open for 0% -> 0% of each run, Pallas kernels for 24% -> 26%
where the time goes in v5:
time: 57.7 us; the launch traced here: 57.5 us
  waiting for transfers between devices  27.4 us (47%)
  Pallas kernels  18.5 us (32%)
  starting transfers between devices  10.1 us (18%)
  between operations  1.48 us (3%)
    ppermute x11, waiting for transfers between devices, passed_along(): lax.ppermute(value, axis, [(source, (source + steps) % count) for source...  20.3 us
    ppermute x11, starting transfers between devices, passed_along(): lax.ppermute(value, axis, [(source, (source + steps) % count) for source...  9.11 us
    pallas_call x4, Pallas kernels, cross_back(): pl.pallas_call(partial(cross_kernel, s, cuts, planes, per), in_specs=[vme...  7.62 us
    ppermute x2, waiting for transfers between devices, passed_across(): return lax.ppermute(value, (axis, 'fft'), pairs)  7.09 us
    pallas_call x2, Pallas kernels, sections(): pl.pallas_call(partial(section_kernel, s, pieces, rotated, cuts), in_spec...  6.36 us
    pallas_call x2, Pallas kernels, spectrum(): pl.pallas_call(partial(spectrum_kernel, s, cuts, per), in_specs=[pl.Block...  2.49 us
    pallas_call x3, Pallas kernels, peaks(): pl.pallas_call(partial(peak_kernel, s, len(parts), last), in_specs=[vmem]...  2.04 us
  transfers between devices with their start and end apart: 13, of which 6 were waited for; matrix products, arithmetic and copies ran while one was open for 0% of the time, Pallas kernels for 26%

profile of v5, /device:TPU:0, one launch (start us, length us, event | category | flops | bytes accessed | tf_op | source)
XLA Modules:
  0.0 57.5 jit_solution(6927789230277004078)
XLA Ops:
  0.7 2.4 %shard_map.136 = (bf16[2064,128]{1,0:T(8,128)(2,1)S(1)}, bf16[2048,128]{1,0:T(8,128)(2,1)S(1)}) custom-call(s32[1,4,32,4096]{3,2,1,0:T(8,128)} %occ.1, s32[1]{0:T(128)S(6)} %copy.16.scalar, bf16[2,2,128,128]{3,2,1,0:T(8,128)(2,1)} %constant.18.clone.refs_0_, bf16[2,128,128]{2,1,0:T(8,128)(2,1)} %constant.19.clone.refs_1_), custom_call_target="tpu_custom_call" | custom-call | flops 1000 | bytes 1000 | tf_op jit(solution)/shard_map/pallas_call | solution.py:268
  3.1 3.1 %collective-permute-start = (bf16[2064,128]{1,0:T(8,128)(2,1)S(1)}, bf16[2064,128]{1,0:T(8,128)(2,1)S(1)}, u32[]{:S(2)}, u32[]{:S(2)}) collective-permute-start(bf16[2064,128]{1,0:T(8,128)(2,1)S(1)} %get-tuple-element.25.refs_4_.load), channel_id=1, source_target_pairs={{0,4},{4,8},{8,12},{12,0},{1,5},{5,9},{9,13},{13,1},{2,6},{6,10},{... | collective-permute-start | bytes 1585160 | tf_op jit(solution)/shard_map/ppermute | solution.py:479
  6.9 3.9 %shard_map.137 = (bf16[2048,128]{1,0:T(8,128)(2,1)S(1)}, bf16[2048,128]{1,0:T(8,128)(2,1)S(1)}) custom-call(s32[1,4,32,4096]{3,2,1,0:T(8,128)} %occ.2, s32[1]{0:T(128)S(6)} %copy.15.scalar, bf16[2,2,128,128]{3,2,1,0:T(8,128)(2,1)} %constant.18.clone.refs_0_, bf16[2,128,128]{2,1,0:T(8,128)(2,1)} %constant.19.clone.refs_1_, ...), custom_call_target="tpu_custom_call" | custom-call | flops 1000 | bytes 1000 | tf_op jit(solution)/shard_map/pallas_call | solution.py:268
  10.8 1.6 %collective-permute-start.3 = (bf16[2048,128]{1,0:T(8,128)(2,1)S(1)}, bf16[2048,128]{1,0:T(8,128)(2,1)S(1)}, u32[]{:S(2)}, u32[]{:S(2)}) collective-permute-start(bf16[2048,128]{1,0:T(8,128)(2,1)S(1)} %get-tuple-element.28.own), channel_id=1, source_target_pairs={{0,2},{2,0},{1,3},{3,1},{4,6},{6,4},{5,7},{7,5},{8,10},{10,8},{9,1... | collective-permute-start | bytes 1572872 | tf_op jit(solution)/shard_map/ppermute | solution.py:479
  12.4 1.0 %collective-permute-start.4 = (bf16[2048,128]{1,0:T(8,128)(2,1)S(1)}, bf16[2048,128]{1,0:T(8,128)(2,1)S(1)}, u32[]{:S(2)}, u32[]{:S(2)}) collective-permute-start(bf16[2048,128]{1,0:T(8,128)(2,1)S(1)} %get-tuple-element.30), channel_id=1, source_target_pairs={{0,3},{1,2},{2,1},{3,0},{4,7},{5,6},{6,5},{7,4},{8,11},{9,10},{10,... | collective-permute-start | bytes 1572872 | tf_op jit(solution)/shard_map/ppermute | solution.py:489
  13.3 12.4 %collective-permute-done.3.own = bf16[2048,128]{1,0:T(8,128)(2,1)S(1)} collective-permute-done((bf16[2048,128]{1,0:T(8,128)(2,1)S(1)}, bf16[2048,128]{1,0:T(8,128)(2,1)S(1)}, u32[]{:S(2)}, u32[]{:S(2)}) %collective-permute-start.3) | collective-permute-done | bytes 524320 | tf_op jit(solution)/shard_map/ppermute | solution.py:479
  25.7 0.5 collective-permute-start.5
  26.3 0.7 %collective-permute-start.1 = (bf16[2064,128]{1,0:T(8,128)(2,1)S(1)}, bf16[2064,128]{1,0:T(8,128)(2,1)S(1)}, u32[]{:S(2)}, u32[]{:S(2)}) collective-permute-start(bf16[2064,128]{1,0:T(8,128)(2,1)S(1)} %collective-permute-done.refs_4_.load), channel_id=1, source_target_pairs={{0,4},{4,8},{8,12},{12,0},{1,5},{5,9},{9,13},{13,1},{2,6},{6,10},{... | collective-permute-start | bytes 1585160 | tf_op jit(solution)/shard_map/ppermute | solution.py:479
  27.0 3.7 %collective-permute-done.7.refs_5_ = bf16[2048,128]{1,0:T(8,128)(2,1)S(1)} collective-permute-done((bf16[2048,128]{1,0:T(8,128)(2,1)S(1)}, bf16[2048,128]{1,0:T(8,128)(2,1)S(1)}, u32[]{:S(2)}, u32[]{:S(2)}) %collective-permute-start.7) | collective-permute-done | bytes 524320 | tf_op jit(solution)/shard_map/ppermute | solution.py:489
  31.1 3.4 %collective-permute-done.4.refs_0_ = bf16[2048,128]{1,0:T(8,128)(2,1)S(1)} collective-permute-done((bf16[2048,128]{1,0:T(8,128)(2,1)S(1)}, bf16[2048,128]{1,0:T(8,128)(2,1)S(1)}, u32[]{:S(2)}, u32[]{:S(2)}) %collective-permute-start.4) | collective-permute-done | bytes 524320 | tf_op jit(solution)/shard_map/ppermute | solution.py:489
  34.5 1.2 %shard_map.139 = (bf16[1024,512]{1,0:T(8,128)(2,1)S(1)}, bf16[64,512]{1,0:T(8,128)(2,1)S(1)}) custom-call(f32[4]{0:T(128)S(1)} %copy-done.5, bf16[2,256,256]{2,1,0:T(8,128)(2,1)S(1)} %copy-done, bf16[2,256,128]{2,1,0:T(8,128)(2,1)S(1)} %copy-done.1, bf16[2048,128]{1,0:T(8,128)(2,1)S(1)} %collective-permute-done.3.own, ...), custom_call_target="tpu_custom_call" | custom-call | flops 1000 | bytes 1000 | tf_op jit(solution)/shard_map/pallas_call | solution.py:347
  35.8 1.3 %shard_map.138 = (bf16[1024,512]{1,0:T(8,128)(2,1)S(1)}, bf16[64,512]{1,0:T(8,128)(2,1)S(1)}) custom-call(f32[4]{0:T(128)S(1)} %copy-done.5, bf16[2,256,256]{2,1,0:T(8,128)(2,1)S(1)} %copy-done, bf16[2,256,128]{2,1,0:T(8,128)(2,1)S(1)} %copy-done.1, bf16[2048,128]{1,0:T(8,128)(2,1)S(1)} %get-tuple-element.28.own, ...), custom_call_target="tpu_custom_call" | custom-call | flops 1000 | bytes 1000 | tf_op jit(solution)/shard_map/pallas_call | solution.py:347
  37.1 2.4 %shard_map.140 = (bf16[1024,128]{1,0:T(8,128)(2,1)S(1)}, bf16[1024,128]{1,0:T(8,128)(2,1)S(1)}) custom-call(bf16[2,256,256]{2,1,0:T(8,128)(2,1)S(1)} %copy-done, bf16[2,256,128]{2,1,0:T(8,128)(2,1)S(1)} %copy-done.1, bf16[2,256,256]{2,1,0:T(8,128)(2,1)S(1)} %copy-done.2, bf16[128,128]{1,0:T(8,128)(2,1)S(1)} %copy-done.3, ...), custom_call_target="tpu_custom_call" | custom-call | flops 1000 | bytes 1000 | tf_op jit(solution)/shard_map/pallas_call | solution.py:422
  39.5 1.2 %collective-permute-start.6 = (bf16[1024,128]{1,0:T(8,128)(2,1)S(1)}, bf16[1024,128]{1,0:T(8,128)(2,1)S(1)}, u32[]{:S(2)}, u32[]{:S(2)}) collective-permute-start(bf16[1024,128]{1,0:T(8,128)(2,1)S(1)} %get-tuple-element.37), channel_id=1, source_target_pairs={{0,1},{1,0},{2,3},{3,2},{4,5},{5,4},{6,7},{7,6},{8,9},{9,8},{10,11... | collective-permute-start | bytes 786440 | tf_op jit(solution)/shard_map/ppermute | solution.py:479
  40.7 2.4 %shard_map.142 = (bf16[1024,128]{1,0:T(8,128)(2,1)S(1)}, bf16[1024,128]{1,0:T(8,128)(2,1)S(1)}) custom-call(bf16[2,256,256]{2,1,0:T(8,128)(2,1)S(1)} %copy-done, bf16[2,256,128]{2,1,0:T(8,128)(2,1)S(1)} %copy-done.1, bf16[2,256,256]{2,1,0:T(8,128)(2,1)S(1)} %copy-done.2, bf16[128,128]{1,0:T(8,128)(2,1)S(1)} %copy-done.3, ...), custom_call_target="tpu_custom_call" | custom-call | flops 1000 | bytes 1000 | tf_op jit(solution)/shard_map/pallas_call | solution.py:422
  43.1 1.0 %collective-permute-start.10 = (bf16[512,128]{1,0:T(8,128)(2,1)S(1)}, bf16[512,128]{1,0:T(8,128)(2,1)S(1)}, u32[]{:S(2)}, u32[]{:S(2)}) collective-permute-start(bf16[512,128]{1,0:T(8,128)(2,1)S(1)} %slice.9), channel_id=1, source_target_pairs={{0,4},{4,8},{8,12},{12,0},{1,5},{5,9},{9,13},{13,1},{2,6},{6,10},{... | collective-permute-start | bytes 393224 | tf_op jit(solution)/shard_map/ppermute | solution.py:479
  44.1 0.5 shard_map.141.refs_4_
  44.7 0.5 shard_map.143.refs_5_
  45.1 6.9 %collective-permute-done.9.refs_5_ = bf16[1536,128]{1,0:T(8,128)(2,1)S(1)} collective-permute-done((bf16[1536,128]{1,0:T(8,128)(2,1)S(1)}, bf16[1536,128]{1,0:T(8,128)(2,1)S(1)}, u32[]{:S(2)}, u32[]{:S(2)}) %collective-permute-start.9) | collective-permute-done | bytes 393248 | tf_op jit(solution)/shard_map/ppermute | solution.py:479
  52.0 2.0 %shard_map.144 = (bf16[768,128]{1,0:T(8,128)(2,1)S(1)}, bf16[768,128]{1,0:T(8,128)(2,1)S(1)}) custom-call(bf16[2,256,256]{2,1,0:T(8,128)(2,1)S(1)} %copy-done, bf16[2,256,128]{2,1,0:T(8,128)(2,1)S(1)} %copy-done.1, bf16[2,256,256]{2,1,0:T(8,128)(2,1)S(1)} %copy-done.2, bf16[128,128]{1,0:T(8,128)(2,1)S(1)} %copy-done.3, ...), custom_call_target="tpu_custom_call" | custom-call | flops 1000 | bytes 1000 | tf_op jit(solution)/shard_map/pallas_call | solution.py:422
  54.1 0.8 %shard_map.145 = (bf16[256,128]{1,0:T(8,128)(2,1)S(1)}, bf16[256,128]{1,0:T(8,128)(2,1)S(1)}) custom-call(bf16[2,256,256]{2,1,0:T(8,128)(2,1)S(1)} %copy-done, bf16[2,256,128]{2,1,0:T(8,128)(2,1)S(1)} %copy-done.1, bf16[2,256,256]{2,1,0:T(8,128)(2,1)S(1)} %copy-done.2, bf16[128,128]{1,0:T(8,128)(2,1)S(1)} %copy-done.3, ...), custom_call_target="tpu_custom_call" | custom-call | flops 1000 | bytes 1000 | tf_op jit(solution)/shard_map/pallas_call | solution.py:422
  55.0 0.6 collective-permute-start.12
  55.5 0.9 %collective-permute-done.12.refs_3_ = bf16[256,128]{1,0:T(8,128)(2,1)S(1)} collective-permute-done((bf16[256,128]{1,0:T(8,128)(2,1)S(1)}, bf16[256,128]{1,0:T(8,128)(2,1)S(1)}, u32[]{:S(2)}, u32[]{:S(2)}) %collective-permute-start.12) | collective-permute-done | bytes 65568 | tf_op jit(solution)/shard_map/ppermute | solution.py:479
  56.4 1.1 %shard_map.146 = f32[1,3,2,32]{3,2,1,0:T(2,128)} custom-call(bf16[2064,128]{1,0:T(8,128)(2,1)S(1)} %collective-permute-done.1.refs_4_.load, bf16[2,64,64]{2,1,0:T(8,128)(2,1)S(1)} %copy-done.4, bf16[768,128]{1,0:T(8,128)(2,1)S(1)} %get-tuple-element.41.refs_0_, bf16[256,128]{1,0:T(8,128)(2,1)S(1)} %get-tuple-element.42.refs_1_, ...), custom_call_target="tpu_custom_call" | custom-call | flops 1000 | bytes 1000 | tf_op jit(solution)/shard_map/pallas_call | solution.py:466
  (27 shorter events, 0.8 us)
Async XLA Ops:
  3.1 31.4 %copy-start = (bf16[2,256,256]{2,1,0:T(8,128)(2,1)S(1)}, bf16[2,256,256]{2,1,0:T(8,128)(2,1)}, u32[]{:S(2)}) copy-start(bf16[2,256,256]{2,1,0:T(8,128)(2,1)} %constant.22.clone.table) | copy-start | bytes 786436
  3.1 31.4 %copy-start.1 = (bf16[2,256,128]{2,1,0:T(8,128)(2,1)S(1)}, bf16[2,256,128]{2,1,0:T(8,128)(2,1)}, u32[]{:S(2)}) copy-start(bf16[2,256,128]{2,1,0:T(8,128)(2,1)} %constant.23.clone.unpack) | copy-start | bytes 393220
  3.1 31.4 %copy-start.5 = (f32[4]{0:T(128)S(1)}, f32[4]{0:T(128)}, u32[]{:S(2)}) copy-start(f32[4]{0:T(128)} %weight.3) | copy-start | bytes 52
  3.1 22.6 %collective-permute-start = (bf16[2064,128]{1,0:T(8,128)(2,1)S(1)}, bf16[2064,128]{1,0:T(8,128)(2,1)S(1)}, u32[]{:S(2)}, u32[]{:S(2)}) collective-permute-start(bf16[2064,128]{1,0:T(8,128)(2,1)S(1)} %get-tuple-element.25.refs_4_.load), channel_id=1, source_target_pairs={{0,4},{4,8},{8,12},{12,0},{1,5},{5,9},{9,13},{13,1},{2,6},{6,10},{... | collective-permute-start | bytes 1585160 | tf_op jit(solution)/shard_map/ppermute | solution.py:479
  10.8 26.3 %copy-start.2 = (bf16[2,256,256]{2,1,0:T(8,128)(2,1)S(1)}, bf16[2,256,256]{2,1,0:T(8,128)(2,1)}, u32[]{:S(2)}) copy-start(bf16[2,256,256]{2,1,0:T(8,128)(2,1)} %constant.24.clone.x_inverse) | copy-start | bytes 786436
  10.8 26.3 %copy-start.3 = (bf16[128,128]{1,0:T(8,128)(2,1)S(1)}, bf16[128,128]{1,0:T(8,128)(2,1)}, u32[]{:S(2)}) copy-start(bf16[128,128]{1,0:T(8,128)(2,1)} %constant.25.clone.y_inverse) | copy-start | bytes 98308
  10.8 14.9 %collective-permute-start.3 = (bf16[2048,128]{1,0:T(8,128)(2,1)S(1)}, bf16[2048,128]{1,0:T(8,128)(2,1)S(1)}, u32[]{:S(2)}, u32[]{:S(2)}) collective-permute-start(bf16[2048,128]{1,0:T(8,128)(2,1)S(1)} %get-tuple-element.28.own), channel_id=1, source_target_pairs={{0,2},{2,0},{1,3},{3,1},{4,6},{6,4},{5,7},{7,5},{8,10},{10,8},{9,1... | collective-permute-start | bytes 1572872 | tf_op jit(solution)/shard_map/ppermute | solution.py:479
  12.4 18.3 %collective-permute-start.7 = (bf16[2048,128]{1,0:T(8,128)(2,1)S(1)}, bf16[2048,128]{1,0:T(8,128)(2,1)S(1)}, u32[]{:S(2)}, u32[]{:S(2)}) collective-permute-start(bf16[2048,128]{1,0:T(8,128)(2,1)S(1)} %get-tuple-element.35), channel_id=1, source_target_pairs={{0,5},{1,4},{4,9},{5,8},{8,13},{9,12},{12,1},{13,0},{2,7},{3,6},{6... | collective-permute-start | bytes 1572872 | tf_op jit(solution)/shard_map/ppermute | solution.py:489
  12.4 22.1 %collective-permute-start.4 = (bf16[2048,128]{1,0:T(8,128)(2,1)S(1)}, bf16[2048,128]{1,0:T(8,128)(2,1)S(1)}, u32[]{:S(2)}, u32[]{:S(2)}) collective-permute-start(bf16[2048,128]{1,0:T(8,128)(2,1)S(1)} %get-tuple-element.30), channel_id=1, source_target_pairs={{0,3},{1,2},{2,1},{3,0},{4,7},{5,6},{6,5},{7,4},{8,11},{9,10},{10,... | collective-permute-start | bytes 1572872 | tf_op jit(solution)/shard_map/ppermute | solution.py:489
  25.7 10.0 %collective-permute-start.2 = (bf16[2048,128]{1,0:T(8,128)(2,1)S(1)}, bf16[2048,128]{1,0:T(8,128)(2,1)S(1)}, u32[]{:S(2)}, u32[]{:S(2)}) collective-permute-start(bf16[2048,128]{1,0:T(8,128)(2,1)S(1)} %get-tuple-element.30), channel_id=1, source_target_pairs={{0,1},{1,0},{2,3},{3,2},{4,5},{5,4},{6,7},{7,6},{8,9},{9,8},{10,11... | collective-permute-start | bytes 1572872 | tf_op jit(solution)/shard_map/ppermute | solution.py:479
  25.7 11.3 %collective-permute-start.5 = (bf16[2048,128]{1,0:T(8,128)(2,1)S(1)}, bf16[2048,128]{1,0:T(8,128)(2,1)S(1)}, u32[]{:S(2)}, u32[]{:S(2)}) collective-permute-start(bf16[2048,128]{1,0:T(8,128)(2,1)S(1)} %get-tuple-element.35), channel_id=1, source_target_pairs={{0,1},{1,0},{2,3},{3,2},{4,5},{5,4},{6,7},{7,6},{8,9},{9,8},{10,11... | collective-permute-start | bytes 1572872 | tf_op jit(solution)/shard_map/ppermute | solution.py:479
  26.3 18.9 %collective-permute-start.1 = (bf16[2064,128]{1,0:T(8,128)(2,1)S(1)}, bf16[2064,128]{1,0:T(8,128)(2,1)S(1)}, u32[]{:S(2)}, u32[]{:S(2)}) collective-permute-start(bf16[2064,128]{1,0:T(8,128)(2,1)S(1)} %collective-permute-done.refs_4_.load), channel_id=1, source_target_pairs={{0,4},{4,8},{8,12},{12,0},{1,5},{5,9},{9,13},{13,1},{2,6},{6,10},{... | collective-permute-start | bytes 1585160 | tf_op jit(solution)/shard_map/ppermute | solution.py:479
  30.7 21.3 %collective-permute-start.9 = (bf16[1536,128]{1,0:T(8,128)(2,1)S(1)}, bf16[1536,128]{1,0:T(8,128)(2,1)S(1)}, u32[]{:S(2)}, u32[]{:S(2)}) collective-permute-start(bf16[1536,128]{1,0:T(8,128)(2,1)S(1)} %slice.8), channel_id=1, source_target_pairs={{0,4},{4,8},{8,12},{12,0},{1,5},{5,9},{9,13},{13,1},{2,6},{6,10},{... | collective-permute-start | bytes 1179656 | tf_op jit(solution)/shard_map/ppermute | solution.py:479
  39.5 4.6 %copy-start.4 = (bf16[2,64,64]{2,1,0:T(8,128)(2,1)S(1)}, bf16[2,64,64]{2,1,0:T(8,128)(2,1)}, u32[]{:S(2)}) copy-start(bf16[2,64,64]{2,1,0:T(8,128)(2,1)} %constant.26.clone.table) | copy-start | bytes 49156
  39.5 4.6 %collective-permute-start.6 = (bf16[1024,128]{1,0:T(8,128)(2,1)S(1)}, bf16[1024,128]{1,0:T(8,128)(2,1)S(1)}, u32[]{:S(2)}, u32[]{:S(2)}) collective-permute-start(bf16[1024,128]{1,0:T(8,128)(2,1)S(1)} %get-tuple-element.37), channel_id=1, source_target_pairs={{0,1},{1,0},{2,3},{3,2},{4,5},{5,4},{6,7},{7,6},{8,9},{9,8},{10,11... | collective-permute-start | bytes 786440 | tf_op jit(solution)/shard_map/ppermute | solution.py:479
  43.0 1.6 %collective-permute-start.8 = (bf16[1024,128]{1,0:T(8,128)(2,1)S(1)}, bf16[1024,128]{1,0:T(8,128)(2,1)S(1)}, u32[]{:S(2)}, u32[]{:S(2)}) collective-permute-start(bf16[1024,128]{1,0:T(8,128)(2,1)S(1)} %get-tuple-element.39), channel_id=1, source_target_pairs={{0,1},{1,0},{2,3},{3,2},{4,5},{5,4},{6,7},{7,6},{8,9},{9,8},{10,11... | collective-permute-start | bytes 786440 | tf_op jit(solution)/shard_map/ppermute | solution.py:479
  43.1 11.0 %collective-permute-start.10 = (bf16[512,128]{1,0:T(8,128)(2,1)S(1)}, bf16[512,128]{1,0:T(8,128)(2,1)S(1)}, u32[]{:S(2)}, u32[]{:S(2)}) collective-permute-start(bf16[512,128]{1,0:T(8,128)(2,1)S(1)} %slice.9), channel_id=1, source_target_pairs={{0,4},{4,8},{8,12},{12,0},{1,5},{5,9},{9,13},{13,1},{2,6},{6,10},{... | collective-permute-start | bytes 393224 | tf_op jit(solution)/shard_map/ppermute | solution.py:479
  54.0 2.4 %collective-permute-start.11 = (bf16[768,128]{1,0:T(8,128)(2,1)S(1)}, bf16[768,128]{1,0:T(8,128)(2,1)S(1)}, u32[]{:S(2)}, u32[]{:S(2)}) collective-permute-start(bf16[768,128]{1,0:T(8,128)(2,1)S(1)} %get-tuple-element.43), channel_id=1, source_target_pairs={{0,1},{1,0},{2,3},{3,2},{4,5},{5,4},{6,7},{7,6},{8,9},{9,8},{10,11... | collective-permute-start | bytes 589832 | tf_op jit(solution)/shard_map/ppermute | solution.py:479
  55.0 1.5 %collective-permute-start.12 = (bf16[256,128]{1,0:T(8,128)(2,1)S(1)}, bf16[256,128]{1,0:T(8,128)(2,1)S(1)}, u32[]{:S(2)}, u32[]{:S(2)}) collective-permute-start(bf16[256,128]{1,0:T(8,128)(2,1)S(1)} %get-tuple-element.44), channel_id=1, source_target_pairs={{0,1},{1,0},{2,3},{3,2},{4,5},{5,4},{6,7},{7,6},{8,9},{9,8},{10,11... | collective-permute-start | bytes 196616 | tf_op jit(solution)/shard_map/ppermute | solution.py:479

commit v6 on v5

--- a/solution.py
+++ b/solution.py
@@ -154,21 +154,56 @@
         self.back = cores * LIG_STEPS * slab
 
 
-def section_kernel(s, pieces, rotated, cuts, occ, scalar, *refs):
+def y_planes(s, table, held, pair):
+    half, step = s.cells // 2, s.cells + 8
+    rows = [
+        jnp.concatenate([held[pl.ds(q * half + pair + k, s.cells, stride=step), :] for q in range(2)], axis=0)
+        for k in range(2)
+    ]
+    done = dot(table[...], jnp.concatenate(rows, axis=1).astype(BF16)).astype(BF16)
+    return [done[:, k * s.lanes:(k + 1) * s.lanes] for k in range(2)]
+
+
+def away_kernel(s, extent, held, table, out):
+    for pair in range(0, s.own, 2):
+        for k, plane in enumerate(y_planes(s, table.at[0], held, s.own + pair)):
+            out[(pair + k) * s.size:(pair + k + 1) * s.size, :] = plane
+    out[s.own * s.size:, :] = jnp.full((s.extra, s.lanes), extent[0].astype(F32)).astype(BF16)
+
+
+def away_planes(s, t, extent, held):
+    vmem = pl.BlockSpec(memory_space=pltpu.VMEM)
+    return pl.pallas_call(
+        partial(away_kernel, s),
+        in_specs=[pl.BlockSpec(memory_space=pltpu.SMEM)] + [vmem] * 2,
+        out_specs=vmem,
+        out_shape=jax.ShapeDtypeStruct((s.own * s.size + s.extra, s.lanes), BF16),
+        compiler_params=params(),
+        cost_estimate=COST,
+    )(extent, held, t["y_even"])
+
+
+def section_kernel(s, pieces, rotated, cuts, occ, *refs):
     cells, lanes = s.cells, s.lanes
     half, size = cells // 2, s.size
     count = 4 if rotated else 2
+    if rotated:
+        scalar, refs = refs[0], refs[1:]
     hbm, refs = refs[:count], refs[count:]
     outs, refs = refs[:len(cuts)], refs[len(cuts):]
-    small, buffer, held = refs[:3]
+    if rotated:
+        small, buffer, held = refs[:3]
+    else:
+        small, buffer, held = None, refs[0], outs[1]
+        refs = (None, None, *refs)
     tables = refs[3:3 + count]
     turned = refs[-2] if rotated else None
     sems = refs[-1]
     core = lax.axis_index("fft")
 
-    first = pltpu.make_async_copy(scalar, small, sems.at[0])
-    first.start()
     if rotated:
+        first = pltpu.make_async_copy(scalar, small, sems.at[0])
+        first.start()
         first.wait()
         turns = small[0]
         is_odd = turns % 2 == 1
@@ -218,13 +253,9 @@
     def even():
         step = cells + 8
         lay(tables[0], cells, step)
-        for pair in range(0, half, 2):
-            rows = [
-                jnp.concatenate([column(held, q * half + pair + k, step) for q in range(2)], axis=0) for k in range(2)
-            ]
-            done = dot(tables[1][...], jnp.concatenate(rows, axis=1).astype(BF16)).astype(BF16)
-            for k in range(2):
-                put(pair + k, done[:, k * lanes:(k + 1) * lanes])
+        for pair in range(0, half if rotated else s.own, 2):
+            for k, plane in enumerate(y_planes(s, tables[1], held, pair)):
+                put(pair + k, plane)
 
     def odd():
         step, short = size + 8, cells + 8
@@ -241,12 +272,13 @@
             put(plane, jnp.concatenate(both, axis=0).astype(BF16))
 
     if rotated:
+        for out in outs:
+            out[out.shape[0] - s.extra:, :] = jnp.zeros((s.extra, lanes), BF16)
         pl.when(jnp.logical_not(is_odd))(even)
         pl.when(is_odd)(odd)
     else:
         even()
-        first.wait()
-        outs[0][s.own * size:, :] = jnp.full((s.extra, lanes), small[0].astype(F32)).astype(BF16)
+        outs[0][s.own * size:, :] = jnp.zeros((2 * s.extra, lanes), BF16)
 
 
 def sections(s, t, occ, scalar, rotated, cuts, pieces=2):
@@ -254,26 +286,28 @@
     names = ["z_even", "y_even"] + (["y_odd", "z_odd"] if rotated else [])
     hbm = pl.BlockSpec(memory_space=pltpu.HBM)
     pin = lambda value: pltpu.with_memory_space_constraint(value, pltpu.HBM)
-    scratch = [
-        pltpu.SMEM(scalar.shape, jnp.int32),
-        pltpu.VMEM(occ.shape[1:], jnp.int32),
-        pltpu.VMEM(((cells + 1) * ((s.size if rotated else cells) + 8), lanes), F32),
-    ]
+    scratch = [pltpu.VMEM(occ.shape[1:], jnp.int32)]
+    if rotated:
+        scratch.insert(0, pltpu.SMEM(scalar.shape, jnp.int32))
+        scratch.append(pltpu.VMEM(((cells + 1) * (s.size + 8), lanes), F32))
     scratch += [pltpu.VMEM(t[name].shape[-2:], BF16) for name in names]
     if rotated:
         scratch.append(pltpu.VMEM(((cells + 1) * (cells + 8), lanes), F32))
     scratch.append(pltpu.SemaphoreType.DMA((1 + len(names) + pieces,)))
-    rows = [s.own * s.size + (0 if rotated else s.extra)]
-    rows += [(high - low) * s.size for low, high in zip(cuts, cuts[1:])]
+    rows = [s.own * s.size + (1 if rotated else 2) * s.extra]
+    rows += [(high - low) * s.size + s.extra for low, high in zip(cuts, cuts[1:])]
+    shapes = [jax.ShapeDtypeStruct((count, lanes), BF16) for count in rows]
+    if not rotated:
+        shapes[1:] = [jax.ShapeDtypeStruct(((cells + 1) * (cells + 8), lanes), F32)]
     return pl.pallas_call(
         partial(section_kernel, s, pieces, rotated, cuts),
-        in_specs=[hbm, pl.BlockSpec(memory_space=pl.ANY)] + [hbm] * len(names),
-        out_specs=[pl.BlockSpec(memory_space=pltpu.VMEM)] * len(rows),
-        out_shape=[jax.ShapeDtypeStruct((count, lanes), BF16) for count in rows],
+        in_specs=[hbm] + [pl.BlockSpec(memory_space=pl.ANY)] * rotated + [hbm] * len(names),
+        out_specs=[pl.BlockSpec(memory_space=pltpu.VMEM)] * len(shapes),
+        out_shape=shapes,
         scratch_shapes=scratch,
         compiler_params=params(),
         cost_estimate=COST,
-    )(pin(occ), scalar, *[pin(t[name]) for name in names])
+    )(pin(occ), *([scalar] if rotated else []), *[pin(t[name]) for name in names])
 
 
 def regroup(s, parts):
@@ -450,7 +484,7 @@
     row = jnp.max(best, axis=0, keepdims=True)
     row = jnp.maximum(row, pltpu.roll(row, s.back // 2, 1)) * (1.0 / (cells * math.sqrt(cells)))
     plane = lax.broadcasted_iota(jnp.int32, row.shape, 1) % s.slab + core * s.slab
-    extent = load[s.own * s.size:, :].astype(F32)[:1]
+    extent = load[load.shape[0] - s.extra:, :].astype(F32)[:1]
     row = jnp.where(plane.astype(F32) < extent, row, 0.0)
     if not last:
         out[...] = row
@@ -499,7 +533,8 @@
     t = tables(s)
     swapped = lambda parts: [passed_along(part, "fft") for part in parts]
 
-    own, *away = sections(s, t, receptor_occupancy, receptor_extent, False, s.whole)
+    own, held = sections(s, t, receptor_occupancy, None, False, s.whole)
+    away = [away_planes(s, t, after(receptor_extent, own), held)]
     receptors = []
     receptors.append((passed_along(own, "rec"), [passed_across(part, "rec") for part in away]))
 
@@ -512,7 +547,8 @@
 
     own, others = receptors[1]
     receptors[1] = (own, others)
-    cuts = [others[0][low * s.size:high * s.size] for low, high in zip(s.parts, s.parts[1:])]
+    ends = [part * s.size for part in s.parts[:-1]] + [None]
+    cuts = [others[0][low:high] for low, high in zip(ends, ends[1:])]
     receptors.append((passed_along(own, "rec"), [passed_along(part, "rec") for part in cuts]))
 
     spectra.append(spectrum(s, t, channel_weight, next_pose, next_others, s.whole))
@@ -527,7 +563,7 @@
             own = after(own, *rows)
         sides = [cross_back(s, t, own, others, poses, tops, cuts, planes) for planes in ranges]
         parts = [keep for keep, _ in sides] + swapped([send for _, send in sides])
-        rows.append(peaks(s, t, own, parts, rows if last else [], last))
+        rows.append(peaks(s, t, others[-1], parts, rows if last else [], last))
     return rows[-1]
 
 

time: 57.7 us -> 57.2 us (level)
  waiting for transfers between devices: 27.4 us -> 24.7 us
  starting transfers between devices: 10.1 us -> 12.3 us
    ppermute x11, waiting for transfers between devices: 20.3 us -> 18 us  [passed_along(): lax.ppermute(value, axis, [(source, (source + steps) % count) for source...]
    ppermute x11, starting transfers between devices: 9.11 us -> 10.5 us  [passed_along(): lax.ppermute(value, axis, [(source, (source + steps) % count) for source...]
    ppermute x2, starting transfers between devices: 0.97 us -> 1.84 us  [passed_across(): return lax.ppermute(value, (axis, 'fft'), pairs)]
  transfers between devices with their start and end apart: 13 -> 13, of which waited for: 6 -> 5; matrix products, arithmetic and copies ran while one was open for 0% -> 0% of each run, Pallas kernels for 26% -> 27%
where the time goes in v6:
time: 57.2 us; the launch traced here: 57.3 us
  waiting for transfers between devices  24.7 us (43%)
  Pallas kernels  18.7 us (33%)
  starting transfers between devices  12.3 us (22%)
  between operations  1.55 us (3%)
    ppermute x11, waiting for transfers between devices, passed_along(): lax.ppermute(value, axis, [(source, (source + steps) % count) for source...  18 us
    ppermute x11, starting transfers between devices, passed_along(): lax.ppermute(value, axis, [(source, (source + steps) % count) for source...  10.5 us
    pallas_call x4, Pallas kernels, cross_back(): pl.pallas_call(partial(cross_kernel, s, cuts, planes, per), in_specs=[vme...  7.64 us
    ppermute x2, waiting for transfers between devices, passed_across(): return lax.ppermute(value, (axis, 'fft'), pairs)  6.68 us
    pallas_call x2, Pallas kernels, sections(): pl.pallas_call(partial(section_kernel, s, pieces, rotated, cuts), in_spec...  6.19 us
    pallas_call x2, Pallas kernels, spectrum(): pl.pallas_call(partial(spectrum_kernel, s, cuts, per), in_specs=[pl.Block...  2.48 us
    pallas_call x3, Pallas kernels, peaks(): pl.pallas_call(partial(peak_kernel, s, len(parts), last), in_specs=[vmem]...  2.04 us
    ppermute x2, starting transfers between devices, passed_across(): return lax.ppermute(value, (axis, 'fft'), pairs)  1.84 us
  transfers between devices with their start and end apart: 13, of which 5 were waited for; matrix products, arithmetic and copies ran while one was open for 0% of the time, Pallas kernels for 27%

profile of v6, /device:TPU:0, one launch (start us, length us, event | category | flops | bytes accessed | tf_op | source)
XLA Modules:
  0.0 57.3 jit_solution(5305090723682095959)
XLA Ops:
  0.0 2.3 %shard_map.136 = (bf16[2080,128]{1,0:T(8,128)(2,1)S(1)}, f32[4680,128]{1,0:T(8,128)S(1)}) custom-call(s32[1,4,32,4096]{3,2,1,0:T(8,128)} %occ.1, bf16[2,2,128,128]{3,2,1,0:T(8,128)(2,1)} %constant.18.clone.refs_0_.refs_1_, bf16[2,128,128]{2,1,0:T(8,128)(2,1)} %constant.19.clone.refs_1_.table.refs_2_), custom_call_target="tpu_custom_call" | custom-call | flops 1000 | bytes 1000 | tf_op jit(solution)/shard_map/pallas_call | solution.py:302
  2.3 3.1 %collective-permute-start.2 = (bf16[2080,128]{1,0:T(8,128)(2,1)S(1)}, bf16[2080,128]{1,0:T(8,128)(2,1)S(1)}, u32[]{:S(2)}, u32[]{:S(2)}) collective-permute-start(bf16[2080,128]{1,0:T(8,128)(2,1)S(1)} %get-tuple-element.26.refs_4_), channel_id=1, source_target_pairs={{0,4},{4,8},{8,12},{12,0},{1,5},{5,9},{9,13},{13,1},{2,6},{6,10},{... | collective-permute-start | bytes 1597448 | tf_op jit(solution)/shard_map/ppermute | solution.py:513
  7.1 3.9 %shard_map.138 = (bf16[2064,128]{1,0:T(8,128)(2,1)S(1)}, bf16[2064,128]{1,0:T(8,128)(2,1)S(1)}) custom-call(s32[1,4,32,4096]{3,2,1,0:T(8,128)} %occ.2, s32[1]{0:T(128)S(6)} %copy.15.refs_0_, bf16[2,2,128,128]{3,2,1,0:T(8,128)(2,1)} %constant.18.clone.refs_0_.refs_1_, bf16[2,128,128]{2,1,0:T(8,128)(2,1)} %constant.19.clone.refs_1_.table.refs_2_, ...), custom_call_target="tpu_custom_call" | custom-call | flops 1000 | bytes 1000 | tf_op jit(solution)/shard_map/pallas_call | solution.py:302
  11.1 1.5 %collective-permute-start.4 = (bf16[2064,128]{1,0:T(8,128)(2,1)S(1)}, bf16[2064,128]{1,0:T(8,128)(2,1)S(1)}, u32[]{:S(2)}, u32[]{:S(2)}) collective-permute-start(bf16[2064,128]{1,0:T(8,128)(2,1)S(1)} %get-tuple-element.30.own), channel_id=1, source_target_pairs={{0,2},{2,0},{1,3},{3,1},{4,6},{6,4},{5,7},{7,5},{8,10},{10,8},{9,1... | collective-permute-start | bytes 1585160 | tf_op jit(solution)/shard_map/ppermute | solution.py:513
  12.6 1.8 %collective-permute-start.5 = (bf16[2064,128]{1,0:T(8,128)(2,1)S(1)}, bf16[2064,128]{1,0:T(8,128)(2,1)S(1)}, u32[]{:S(2)}, u32[]{:S(2)}) collective-permute-start(bf16[2064,128]{1,0:T(8,128)(2,1)S(1)} %get-tuple-element.32), channel_id=1, source_target_pairs={{0,3},{1,2},{2,1},{3,0},{4,7},{5,6},{6,5},{7,4},{8,11},{9,10},{10,... | collective-permute-start | bytes 1585160 | tf_op jit(solution)/shard_map/ppermute | solution.py:523
  14.4 11.6 %collective-permute-done.4.own = bf16[2064,128]{1,0:T(8,128)(2,1)S(1)} collective-permute-done((bf16[2064,128]{1,0:T(8,128)(2,1)S(1)}, bf16[2064,128]{1,0:T(8,128)(2,1)S(1)}, u32[]{:S(2)}, u32[]{:S(2)}) %collective-permute-start.4) | collective-permute-done | bytes 528416 | tf_op jit(solution)/shard_map/ppermute | solution.py:513
  26.1 0.5 collective-permute-start.7
  26.6 1.6 %collective-permute-start.6 = (bf16[2080,128]{1,0:T(8,128)(2,1)S(1)}, bf16[2080,128]{1,0:T(8,128)(2,1)S(1)}, u32[]{:S(2)}, u32[]{:S(2)}) collective-permute-start(bf16[2080,128]{1,0:T(8,128)(2,1)S(1)} %collective-permute-done.2.refs_4_), channel_id=1, source_target_pairs={{0,4},{4,8},{8,12},{12,0},{1,5},{5,9},{9,13},{13,1},{2,6},{6,10},{... | collective-permute-start | bytes 1597448 | tf_op jit(solution)/shard_map/ppermute | solution.py:513
  28.1 1.8 %collective-permute-done.refs_5_.load = bf16[2064,128]{1,0:T(8,128)(2,1)S(1)} collective-permute-done((bf16[2064,128]{1,0:T(8,128)(2,1)S(1)}, bf16[2064,128]{1,0:T(8,128)(2,1)S(1)}, u32[]{:S(2)}, u32[]{:S(2)}) %collective-permute-start) | collective-permute-done | bytes 528416 | tf_op jit(solution)/shard_map/ppermute | solution.py:523
  30.1 4.9 %collective-permute-done.5.refs_0_ = bf16[2064,128]{1,0:T(8,128)(2,1)S(1)} collective-permute-done((bf16[2064,128]{1,0:T(8,128)(2,1)S(1)}, bf16[2064,128]{1,0:T(8,128)(2,1)S(1)}, u32[]{:S(2)}, u32[]{:S(2)}) %collective-permute-start.5) | collective-permute-done | bytes 528416 | tf_op jit(solution)/shard_map/ppermute | solution.py:523
  34.9 1.2 %shard_map.140 = (bf16[1024,512]{1,0:T(8,128)(2,1)S(1)}, bf16[64,512]{1,0:T(8,128)(2,1)S(1)}) custom-call(f32[4]{0:T(128)S(1)} %copy-done.6, bf16[2,256,256]{2,1,0:T(8,128)(2,1)S(1)} %copy-done, bf16[2,256,128]{2,1,0:T(8,128)(2,1)S(1)} %copy-done.1, bf16[2064,128]{1,0:T(8,128)(2,1)S(1)} %collective-permute-done.4.own, ...), custom_call_target="tpu_custom_call" | custom-call | flops 1000 | bytes 1000 | tf_op jit(solution)/shard_map/pallas_call | solution.py:381
  36.2 1.2 %shard_map.139 = (bf16[1024,512]{1,0:T(8,128)(2,1)S(1)}, bf16[64,512]{1,0:T(8,128)(2,1)S(1)}) custom-call(f32[4]{0:T(128)S(1)} %copy-done.6, bf16[2,256,256]{2,1,0:T(8,128)(2,1)S(1)} %copy-done, bf16[2,256,128]{2,1,0:T(8,128)(2,1)S(1)} %copy-done.1, bf16[2064,128]{1,0:T(8,128)(2,1)S(1)} %get-tuple-element.30.own, ...), custom_call_target="tpu_custom_call" | custom-call | flops 1000 | bytes 1000 | tf_op jit(solution)/shard_map/pallas_call | solution.py:381
  37.5 2.4 %shard_map.141 = (bf16[1024,128]{1,0:T(8,128)(2,1)S(1)}, bf16[1024,128]{1,0:T(8,128)(2,1)S(1)}) custom-call(bf16[2,256,256]{2,1,0:T(8,128)(2,1)S(1)} %copy-done, bf16[2,256,128]{2,1,0:T(8,128)(2,1)S(1)} %copy-done.1, bf16[2,256,256]{2,1,0:T(8,128)(2,1)S(1)} %copy-done.2, bf16[128,128]{1,0:T(8,128)(2,1)S(1)} %copy-done.4, ...), custom_call_target="tpu_custom_call" | custom-call | flops 1000 | bytes 1000 | tf_op jit(solution)/shard_map/pallas_call | solution.py:456
  39.9 1.2 %collective-permute-start.8 = (bf16[1024,128]{1,0:T(8,128)(2,1)S(1)}, bf16[1024,128]{1,0:T(8,128)(2,1)S(1)}, u32[]{:S(2)}, u32[]{:S(2)}) collective-permute-start(bf16[1024,128]{1,0:T(8,128)(2,1)S(1)} %get-tuple-element.39), channel_id=1, source_target_pairs={{0,1},{1,0},{2,3},{3,2},{4,5},{5,4},{6,7},{7,6},{8,9},{9,8},{10,11... | collective-permute-start | bytes 786440 | tf_op jit(solution)/shard_map/ppermute | solution.py:513
  41.1 2.4 %shard_map.143 = (bf16[1024,128]{1,0:T(8,128)(2,1)S(1)}, bf16[1024,128]{1,0:T(8,128)(2,1)S(1)}) custom-call(bf16[2,256,256]{2,1,0:T(8,128)(2,1)S(1)} %copy-done, bf16[2,256,128]{2,1,0:T(8,128)(2,1)S(1)} %copy-done.1, bf16[2,256,256]{2,1,0:T(8,128)(2,1)S(1)} %copy-done.2, bf16[128,128]{1,0:T(8,128)(2,1)S(1)} %copy-done.4, ...), custom_call_target="tpu_custom_call" | custom-call | flops 1000 | bytes 1000 | tf_op jit(solution)/shard_map/pallas_call | solution.py:456
  43.5 1.8 %collective-permute-start.1 = (bf16[528,128]{1,0:T(8,128)(2,1)S(1)}, bf16[528,128]{1,0:T(8,128)(2,1)S(1)}, u32[]{:S(2)}, u32[]{:S(2)}) collective-permute-start(bf16[528,128]{1,0:T(8,128)(2,1)S(1)} %slice.8), channel_id=1, source_target_pairs={{0,4},{4,8},{8,12},{12,0},{1,5},{5,9},{9,13},{13,1},{2,6},{6,10},{... | collective-permute-start | bytes 405512 | tf_op jit(solution)/shard_map/ppermute | solution.py:513
  45.4 0.5 shard_map.142.refs_4_
  45.8 0.5 shard_map.144.refs_5_
  46.3 5.5 %collective-permute-done.10.refs_5_ = bf16[1536,128]{1,0:T(8,128)(2,1)S(1)} collective-permute-done((bf16[1536,128]{1,0:T(8,128)(2,1)S(1)}, bf16[1536,128]{1,0:T(8,128)(2,1)S(1)}, u32[]{:S(2)}, u32[]{:S(2)}) %collective-permute-start.10) | collective-permute-done | bytes 393248 | tf_op jit(solution)/shard_map/ppermute | solution.py:513
  51.8 2.0 %shard_map.145 = (bf16[768,128]{1,0:T(8,128)(2,1)S(1)}, bf16[768,128]{1,0:T(8,128)(2,1)S(1)}) custom-call(bf16[2,256,256]{2,1,0:T(8,128)(2,1)S(1)} %copy-done, bf16[2,256,128]{2,1,0:T(8,128)(2,1)S(1)} %copy-done.1, bf16[2,256,256]{2,1,0:T(8,128)(2,1)S(1)} %copy-done.2, bf16[128,128]{1,0:T(8,128)(2,1)S(1)} %copy-done.4, ...), custom_call_target="tpu_custom_call" | custom-call | flops 1000 | bytes 1000 | tf_op jit(solution)/shard_map/pallas_call | solution.py:456
  53.9 0.8 %shard_map.146 = (bf16[256,128]{1,0:T(8,128)(2,1)S(1)}, bf16[256,128]{1,0:T(8,128)(2,1)S(1)}) custom-call(bf16[2,256,256]{2,1,0:T(8,128)(2,1)S(1)} %copy-done, bf16[2,256,128]{2,1,0:T(8,128)(2,1)S(1)} %copy-done.1, bf16[2,256,256]{2,1,0:T(8,128)(2,1)S(1)} %copy-done.2, bf16[128,128]{1,0:T(8,128)(2,1)S(1)} %copy-done.4, ...), custom_call_target="tpu_custom_call" | custom-call | flops 1000 | bytes 1000 | tf_op jit(solution)/shard_map/pallas_call | solution.py:456
  54.7 0.6 collective-permute-start.12
  55.3 0.9 %collective-permute-done.12.refs_3_ = bf16[256,128]{1,0:T(8,128)(2,1)S(1)} collective-permute-done((bf16[256,128]{1,0:T(8,128)(2,1)S(1)}, bf16[256,128]{1,0:T(8,128)(2,1)S(1)}, u32[]{:S(2)}, u32[]{:S(2)}) %collective-permute-start.12) | collective-permute-done | bytes 65568 | tf_op jit(solution)/shard_map/ppermute | solution.py:513
  56.2 1.1 %shard_map.147 = f32[1,3,2,32]{3,2,1,0:T(2,128)} custom-call(bf16[528,128]{1,0:T(8,128)(2,1)S(1)} %collective-permute-done.1.refs_5_.load, bf16[2,64,64]{2,1,0:T(8,128)(2,1)S(1)} %copy-done.5, bf16[768,128]{1,0:T(8,128)(2,1)S(1)} %get-tuple-element.43.refs_0_, bf16[256,128]{1,0:T(8,128)(2,1)S(1)} %get-tuple-element.44.refs_1_, ...), custom_call_target="tpu_custom_call" | custom-call | flops 1000 | bytes 1000 | tf_op jit(solution)/shard_map/pallas_call | solution.py:500
  (30 shorter events, 0.6 us)
Async XLA Ops:
  0.0 6.0 %copy-start.3 = (bf16[2,128,128]{2,1,0:T(8,128)(2,1)S(1)}, bf16[2,128,128]{2,1,0:T(8,128)(2,1)}, u32[]{:S(2)}) copy-start(bf16[2,128,128]{2,1,0:T(8,128)(2,1)} %constant.19.clone.refs_1_.table.refs_2_) | copy-start | bytes 196612
  2.3 23.8 %collective-permute-start.2 = (bf16[2080,128]{1,0:T(8,128)(2,1)S(1)}, bf16[2080,128]{1,0:T(8,128)(2,1)S(1)}, u32[]{:S(2)}, u32[]{:S(2)}) collective-permute-start(bf16[2080,128]{1,0:T(8,128)(2,1)S(1)} %get-tuple-element.26.refs_4_), channel_id=1, source_target_pairs={{0,4},{4,8},{8,12},{12,0},{1,5},{5,9},{9,13},{13,1},{2,6},{6,10},{... | collective-permute-start | bytes 1597448 | tf_op jit(solution)/shard_map/ppermute | solution.py:513
  6.4 28.5 %copy-start = (bf16[2,256,256]{2,1,0:T(8,128)(2,1)S(1)}, bf16[2,256,256]{2,1,0:T(8,128)(2,1)}, u32[]{:S(2)}) copy-start(bf16[2,256,256]{2,1,0:T(8,128)(2,1)} %constant.22.clone.table) | copy-start | bytes 786436
  6.4 28.5 %copy-start.1 = (bf16[2,256,128]{2,1,0:T(8,128)(2,1)S(1)}, bf16[2,256,128]{2,1,0:T(8,128)(2,1)}, u32[]{:S(2)}) copy-start(bf16[2,256,128]{2,1,0:T(8,128)(2,1)} %constant.23.clone.unpack) | copy-start | bytes 393220
  6.4 28.5 %copy-start.6 = (f32[4]{0:T(128)S(1)}, f32[4]{0:T(128)}, u32[]{:S(2)}) copy-start(f32[4]{0:T(128)} %weight.3) | copy-start | bytes 52
  11.0 26.4 %copy-start.2 = (bf16[2,256,256]{2,1,0:T(8,128)(2,1)S(1)}, bf16[2,256,256]{2,1,0:T(8,128)(2,1)}, u32[]{:S(2)}) copy-start(bf16[2,256,256]{2,1,0:T(8,128)(2,1)} %constant.24.clone.x_inverse) | copy-start | bytes 786436
  11.0 26.4 %copy-start.4 = (bf16[128,128]{1,0:T(8,128)(2,1)S(1)}, bf16[128,128]{1,0:T(8,128)(2,1)}, u32[]{:S(2)}) copy-start(bf16[128,128]{1,0:T(8,128)(2,1)} %constant.25.clone.y_inverse) | copy-start | bytes 98308
  11.1 15.0 %collective-permute-start.4 = (bf16[2064,128]{1,0:T(8,128)(2,1)S(1)}, bf16[2064,128]{1,0:T(8,128)(2,1)S(1)}, u32[]{:S(2)}, u32[]{:S(2)}) collective-permute-start(bf16[2064,128]{1,0:T(8,128)(2,1)S(1)} %get-tuple-element.30.own), channel_id=1, source_target_pairs={{0,2},{2,0},{1,3},{3,1},{4,6},{6,4},{5,7},{7,5},{8,10},{10,8},{9,1... | collective-permute-start | bytes 1585160 | tf_op jit(solution)/shard_map/ppermute | solution.py:513
  12.6 17.4 %collective-permute-start = (bf16[2064,128]{1,0:T(8,128)(2,1)S(1)}, bf16[2064,128]{1,0:T(8,128)(2,1)S(1)}, u32[]{:S(2)}, u32[]{:S(2)}) collective-permute-start(bf16[2064,128]{1,0:T(8,128)(2,1)S(1)} %shard_map.137), channel_id=1, source_target_pairs={{0,5},{1,4},{4,9},{5,8},{8,13},{9,12},{12,1},{13,0},{2,7},{3,6},{6... | collective-permute-start | bytes 1585160 | tf_op jit(solution)/shard_map/ppermute | solution.py:523
  12.6 22.3 %collective-permute-start.5 = (bf16[2064,128]{1,0:T(8,128)(2,1)S(1)}, bf16[2064,128]{1,0:T(8,128)(2,1)S(1)}, u32[]{:S(2)}, u32[]{:S(2)}) collective-permute-start(bf16[2064,128]{1,0:T(8,128)(2,1)S(1)} %get-tuple-element.32), channel_id=1, source_target_pairs={{0,3},{1,2},{2,1},{3,0},{4,7},{5,6},{6,5},{7,4},{8,11},{9,10},{10,... | collective-permute-start | bytes 1585160 | tf_op jit(solution)/shard_map/ppermute | solution.py:523
  26.1 10.1 %collective-permute-start.3 = (bf16[2064,128]{1,0:T(8,128)(2,1)S(1)}, bf16[2064,128]{1,0:T(8,128)(2,1)S(1)}, u32[]{:S(2)}, u32[]{:S(2)}) collective-permute-start(bf16[2064,128]{1,0:T(8,128)(2,1)S(1)} %get-tuple-element.32), channel_id=1, source_target_pairs={{0,1},{1,0},{2,3},{3,2},{4,5},{5,4},{6,7},{7,6},{8,9},{9,8},{10,11... | collective-permute-start | bytes 1585160 | tf_op jit(solution)/shard_map/ppermute | solution.py:513
  26.1 11.4 %collective-permute-start.7 = (bf16[2064,128]{1,0:T(8,128)(2,1)S(1)}, bf16[2064,128]{1,0:T(8,128)(2,1)S(1)}, u32[]{:S(2)}, u32[]{:S(2)}) collective-permute-start(bf16[2064,128]{1,0:T(8,128)(2,1)S(1)} %shard_map.137), channel_id=1, source_target_pairs={{0,1},{1,0},{2,3},{3,2},{4,5},{5,4},{6,7},{7,6},{8,9},{9,8},{10,11... | collective-permute-start | bytes 1585160 | tf_op jit(solution)/shard_map/ppermute | solution.py:513
  26.6 19.7 %collective-permute-start.6 = (bf16[2080,128]{1,0:T(8,128)(2,1)S(1)}, bf16[2080,128]{1,0:T(8,128)(2,1)S(1)}, u32[]{:S(2)}, u32[]{:S(2)}) collective-permute-start(bf16[2080,128]{1,0:T(8,128)(2,1)S(1)} %collective-permute-done.2.refs_4_), channel_id=1, source_target_pairs={{0,4},{4,8},{8,12},{12,0},{1,5},{5,9},{9,13},{13,1},{2,6},{6,10},{... | collective-permute-start | bytes 1597448 | tf_op jit(solution)/shard_map/ppermute | solution.py:513
  30.0 21.8 %collective-permute-start.10 = (bf16[1536,128]{1,0:T(8,128)(2,1)S(1)}, bf16[1536,128]{1,0:T(8,128)(2,1)S(1)}, u32[]{:S(2)}, u32[]{:S(2)}) collective-permute-start(bf16[1536,128]{1,0:T(8,128)(2,1)S(1)} %slice.9), channel_id=1, source_target_pairs={{0,4},{4,8},{8,12},{12,0},{1,5},{5,9},{9,13},{13,1},{2,6},{6,10},{... | collective-permute-start | bytes 1179656 | tf_op jit(solution)/shard_map/ppermute | solution.py:513
  39.9 5.5 %copy-start.5 = (bf16[2,64,64]{2,1,0:T(8,128)(2,1)S(1)}, bf16[2,64,64]{2,1,0:T(8,128)(2,1)}, u32[]{:S(2)}) copy-start(bf16[2,64,64]{2,1,0:T(8,128)(2,1)} %constant.26.clone.table) | copy-start | bytes 49156
  39.9 5.5 %collective-permute-start.8 = (bf16[1024,128]{1,0:T(8,128)(2,1)S(1)}, bf16[1024,128]{1,0:T(8,128)(2,1)S(1)}, u32[]{:S(2)}, u32[]{:S(2)}) collective-permute-start(bf16[1024,128]{1,0:T(8,128)(2,1)S(1)} %get-tuple-element.39), channel_id=1, source_target_pairs={{0,1},{1,0},{2,3},{3,2},{4,5},{5,4},{6,7},{7,6},{8,9},{9,8},{10,11... | collective-permute-start | bytes 786440 | tf_op jit(solution)/shard_map/ppermute | solution.py:513
  43.4 2.4 %collective-permute-start.9 = (bf16[1024,128]{1,0:T(8,128)(2,1)S(1)}, bf16[1024,128]{1,0:T(8,128)(2,1)S(1)}, u32[]{:S(2)}, u32[]{:S(2)}) collective-permute-start(bf16[1024,128]{1,0:T(8,128)(2,1)S(1)} %get-tuple-element.41), channel_id=1, source_target_pairs={{0,1},{1,0},{2,3},{3,2},{4,5},{5,4},{6,7},{7,6},{8,9},{9,8},{10,11... | collective-permute-start | bytes 786440 | tf_op jit(solution)/shard_map/ppermute | solution.py:513
  43.5 10.3 %collective-permute-start.1 = (bf16[528,128]{1,0:T(8,128)(2,1)S(1)}, bf16[528,128]{1,0:T(8,128)(2,1)S(1)}, u32[]{:S(2)}, u32[]{:S(2)}) collective-permute-start(bf16[528,128]{1,0:T(8,128)(2,1)S(1)} %slice.8), channel_id=1, source_target_pairs={{0,4},{4,8},{8,12},{12,0},{1,5},{5,9},{9,13},{13,1},{2,6},{6,10},{... | collective-permute-start | bytes 405512 | tf_op jit(solution)/shard_map/ppermute | solution.py:513
  53.8 2.4 %collective-permute-start.11 = (bf16[768,128]{1,0:T(8,128)(2,1)S(1)}, bf16[768,128]{1,0:T(8,128)(2,1)S(1)}, u32[]{:S(2)}, u32[]{:S(2)}) collective-permute-start(bf16[768,128]{1,0:T(8,128)(2,1)S(1)} %get-tuple-element.45), channel_id=1, source_target_pairs={{0,1},{1,0},{2,3},{3,2},{4,5},{5,4},{6,7},{7,6},{8,9},{9,8},{10,11... | collective-permute-start | bytes 589832 | tf_op jit(solution)/shard_map/ppermute | solution.py:513
  54.7 1.5 %collective-permute-start.12 = (bf16[256,128]{1,0:T(8,128)(2,1)S(1)}, bf16[256,128]{1,0:T(8,128)(2,1)S(1)}, u32[]{:S(2)}, u32[]{:S(2)}) collective-permute-start(bf16[256,128]{1,0:T(8,128)(2,1)S(1)} %get-tuple-element.46), channel_id=1, source_target_pairs={{0,1},{1,0},{2,3},{3,2},{4,5},{5,4},{6,7},{7,6},{8,9},{9,8},{10,11... | collective-permute-start | bytes 196616 | tf_op jit(solution)/shard_map/ppermute | solution.py:513

commit v7 on v6

--- a/solution.py
+++ b/solution.py
@@ -278,7 +278,7 @@
         pl.when(is_odd)(odd)
     else:
         even()
-        outs[0][s.own * size:, :] = jnp.zeros((2 * s.extra, lanes), BF16)
+        outs[0][s.own * size:, :] = jnp.zeros((s.extra, lanes), BF16)
 
 
 def sections(s, t, occ, scalar, rotated, cuts, pieces=2):
@@ -294,7 +294,7 @@
     if rotated:
         scratch.append(pltpu.VMEM(((cells + 1) * (cells + 8), lanes), F32))
     scratch.append(pltpu.SemaphoreType.DMA((1 + len(names) + pieces,)))
-    rows = [s.own * s.size + (1 if rotated else 2) * s.extra]
+    rows = [s.own * s.size + s.extra]
     rows += [(high - low) * s.size + s.extra for low, high in zip(cuts, cuts[1:])]
     shapes = [jax.ShapeDtypeStruct((count, lanes), BF16) for count in rows]
     if not rotated:

time: 57.2 us -> 57.1 us (level)
  starting transfers between devices: 12.3 us -> 9.34 us
  waiting for transfers between devices: 24.7 us -> 27.2 us
    ppermute x11, starting transfers between devices: 10.5 us -> 7.5 us  [passed_along(): lax.ppermute(value, axis, [(source, (source + steps) % count) for source...]
    ppermute x11, waiting for transfers between devices: 18 us -> 19.6 us  [passed_along(): lax.ppermute(value, axis, [(source, (source + steps) % count) for source...]
    ppermute x2, waiting for transfers between devices: 6.68 us -> 7.55 us  [passed_across(): return lax.ppermute(value, (axis, 'fft'), pairs)]
  transfers between devices with their start and end apart: 13 -> 13, of which waited for: 5 -> 8; matrix products, arithmetic and copies ran while one was open for 0% -> 0% of each run, Pallas kernels for 27% -> 27%
where the time goes in v7:
time: 57.1 us; the launch traced here: 56.9 us
  waiting for transfers between devices  27.2 us (48%)
  Pallas kernels  18.7 us (33%)
  starting transfers between devices  9.34 us (16%)
  between operations  1.54 us (3%)
    ppermute x11, waiting for transfers between devices, passed_along(): lax.ppermute(value, axis, [(source, (source + steps) % count) for source...  19.6 us
    pallas_call x4, Pallas kernels, cross_back(): pl.pallas_call(partial(cross_kernel, s, cuts, planes, per), in_specs=[vme...  7.67 us
    ppermute x2, waiting for transfers between devices, passed_across(): return lax.ppermute(value, (axis, 'fft'), pairs)  7.55 us
    ppermute x11, starting transfers between devices, passed_along(): lax.ppermute(value, axis, [(source, (source + steps) % count) for source...  7.5 us
    pallas_call x2, Pallas kernels, sections(): pl.pallas_call(partial(section_kernel, s, pieces, rotated, cuts), in_spec...  6.19 us
    pallas_call x2, Pallas kernels, spectrum(): pl.pallas_call(partial(spectrum_kernel, s, cuts, per), in_specs=[pl.Block...  2.48 us
    pallas_call x3, Pallas kernels, peaks(): pl.pallas_call(partial(peak_kernel, s, len(parts), last), in_specs=[vmem]...  2.04 us
    ppermute x2, starting transfers between devices, passed_across(): return lax.ppermute(value, (axis, 'fft'), pairs)  1.84 us
  transfers between devices with their start and end apart: 13, of which 8 were waited for; matrix products, arithmetic and copies ran while one was open for 0% of the time, Pallas kernels for 27%

profile of v7, /device:TPU:0, one launch (start us, length us, event | category | flops | bytes accessed | tf_op | source)
XLA Modules:
  0.0 56.9 jit_solution(15227567679124481606)
XLA Ops:
  0.0 2.3 %shard_map.136 = (bf16[2064,128]{1,0:T(8,128)(2,1)S(1)}, f32[4680,128]{1,0:T(8,128)S(1)}) custom-call(s32[1,4,32,4096]{3,2,1,0:T(8,128)} %occ.1, bf16[2,2,128,128]{3,2,1,0:T(8,128)(2,1)} %constant.18.clone.refs_0_.refs_1_, bf16[2,128,128]{2,1,0:T(8,128)(2,1)} %constant.19.clone.refs_1_.table.refs_2_), custom_call_target="tpu_custom_call" | custom-call | flops 1000 | bytes 1000 | tf_op jit(solution)/shard_map/pallas_call | solution.py:302
  2.3 3.1 %collective-permute-start.2 = (bf16[2064,128]{1,0:T(8,128)(2,1)S(1)}, bf16[2064,128]{1,0:T(8,128)(2,1)S(1)}, u32[]{:S(2)}, u32[]{:S(2)}) collective-permute-start(bf16[2064,128]{1,0:T(8,128)(2,1)S(1)} %get-tuple-element.26.refs_4_), channel_id=1, source_target_pairs={{0,4},{4,8},{8,12},{12,0},{1,5},{5,9},{9,13},{13,1},{2,6},{6,10},{... | collective-permute-start | bytes 1585160 | tf_op jit(solution)/shard_map/ppermute | solution.py:513
  7.1 3.9 %shard_map.138 = (bf16[2064,128]{1,0:T(8,128)(2,1)S(1)}, bf16[2064,128]{1,0:T(8,128)(2,1)S(1)}) custom-call(s32[1,4,32,4096]{3,2,1,0:T(8,128)} %occ.2, s32[1]{0:T(128)S(6)} %copy.15.refs_0_, bf16[2,2,128,128]{3,2,1,0:T(8,128)(2,1)} %constant.18.clone.refs_0_.refs_1_, bf16[2,128,128]{2,1,0:T(8,128)(2,1)} %constant.19.clone.refs_1_.table.refs_2_, ...), custom_call_target="tpu_custom_call" | custom-call | flops 1000 | bytes 1000 | tf_op jit(solution)/shard_map/pallas_call | solution.py:302
  11.0 0.7 %collective-permute-start.4 = (bf16[2064,128]{1,0:T(8,128)(2,1)S(1)}, bf16[2064,128]{1,0:T(8,128)(2,1)S(1)}, u32[]{:S(2)}, u32[]{:S(2)}) collective-permute-start(bf16[2064,128]{1,0:T(8,128)(2,1)S(1)} %get-tuple-element.30.own), channel_id=1, source_target_pairs={{0,2},{2,0},{1,3},{3,1},{4,6},{6,4},{5,7},{7,5},{8,10},{10,8},{9,1... | collective-permute-start | bytes 1585160 | tf_op jit(solution)/shard_map/ppermute | solution.py:513
  11.7 0.5 collective-permute-start
  12.2 1.4 %collective-permute-start.5 = (bf16[2064,128]{1,0:T(8,128)(2,1)S(1)}, bf16[2064,128]{1,0:T(8,128)(2,1)S(1)}, u32[]{:S(2)}, u32[]{:S(2)}) collective-permute-start(bf16[2064,128]{1,0:T(8,128)(2,1)S(1)} %get-tuple-element.32), channel_id=1, source_target_pairs={{0,3},{1,2},{2,1},{3,0},{4,7},{5,6},{6,5},{7,4},{8,11},{9,10},{10,... | collective-permute-start | bytes 1585160 | tf_op jit(solution)/shard_map/ppermute | solution.py:523
  13.6 6.7 %collective-permute-done.2.refs_4_ = bf16[2064,128]{1,0:T(8,128)(2,1)S(1)} collective-permute-done((bf16[2064,128]{1,0:T(8,128)(2,1)S(1)}, bf16[2064,128]{1,0:T(8,128)(2,1)S(1)}, u32[]{:S(2)}, u32[]{:S(2)}) %collective-permute-start.2) | collective-permute-done | bytes 528416 | tf_op jit(solution)/shard_map/ppermute | solution.py:513
  20.2 5.8 %collective-permute-done.4.own = bf16[2064,128]{1,0:T(8,128)(2,1)S(1)} collective-permute-done((bf16[2064,128]{1,0:T(8,128)(2,1)S(1)}, bf16[2064,128]{1,0:T(8,128)(2,1)S(1)}, u32[]{:S(2)}, u32[]{:S(2)}) %collective-permute-start.4) | collective-permute-done | bytes 528416 | tf_op jit(solution)/shard_map/ppermute | solution.py:513
  26.1 0.7 %collective-permute-start.6 = (bf16[2064,128]{1,0:T(8,128)(2,1)S(1)}, bf16[2064,128]{1,0:T(8,128)(2,1)S(1)}, u32[]{:S(2)}, u32[]{:S(2)}) collective-permute-start(bf16[2064,128]{1,0:T(8,128)(2,1)S(1)} %collective-permute-done.2.refs_4_), channel_id=1, source_target_pairs={{0,4},{4,8},{8,12},{12,0},{1,5},{5,9},{9,13},{13,1},{2,6},{6,10},{... | collective-permute-start | bytes 1585160 | tf_op jit(solution)/shard_map/ppermute | solution.py:513
  26.8 3.1 %collective-permute-done.refs_5_.load = bf16[2064,128]{1,0:T(8,128)(2,1)S(1)} collective-permute-done((bf16[2064,128]{1,0:T(8,128)(2,1)S(1)}, bf16[2064,128]{1,0:T(8,128)(2,1)S(1)}, u32[]{:S(2)}, u32[]{:S(2)}) %collective-permute-start) | collective-permute-done | bytes 528416 | tf_op jit(solution)/shard_map/ppermute | solution.py:523
  30.0 4.4 %collective-permute-done.5.refs_0_ = bf16[2064,128]{1,0:T(8,128)(2,1)S(1)} collective-permute-done((bf16[2064,128]{1,0:T(8,128)(2,1)S(1)}, bf16[2064,128]{1,0:T(8,128)(2,1)S(1)}, u32[]{:S(2)}, u32[]{:S(2)}) %collective-permute-start.5) | collective-permute-done | bytes 528416 | tf_op jit(solution)/shard_map/ppermute | solution.py:523
  34.4 1.2 %shard_map.140 = (bf16[1024,512]{1,0:T(8,128)(2,1)S(1)}, bf16[64,512]{1,0:T(8,128)(2,1)S(1)}) custom-call(f32[4]{0:T(128)S(1)} %copy-done.6, bf16[2,256,256]{2,1,0:T(8,128)(2,1)S(1)} %copy-done, bf16[2,256,128]{2,1,0:T(8,128)(2,1)S(1)} %copy-done.1, bf16[2064,128]{1,0:T(8,128)(2,1)S(1)} %collective-permute-done.4.own, ...), custom_call_target="tpu_custom_call" | custom-call | flops 1000 | bytes 1000 | tf_op jit(solution)/shard_map/pallas_call | solution.py:381
  35.7 1.2 %shard_map.139 = (bf16[1024,512]{1,0:T(8,128)(2,1)S(1)}, bf16[64,512]{1,0:T(8,128)(2,1)S(1)}) custom-call(f32[4]{0:T(128)S(1)} %copy-done.6, bf16[2,256,256]{2,1,0:T(8,128)(2,1)S(1)} %copy-done, bf16[2,256,128]{2,1,0:T(8,128)(2,1)S(1)} %copy-done.1, bf16[2064,128]{1,0:T(8,128)(2,1)S(1)} %get-tuple-element.30.own, ...), custom_call_target="tpu_custom_call" | custom-call | flops 1000 | bytes 1000 | tf_op jit(solution)/shard_map/pallas_call | solution.py:381
  37.0 2.4 %shard_map.141 = (bf16[1024,128]{1,0:T(8,128)(2,1)S(1)}, bf16[1024,128]{1,0:T(8,128)(2,1)S(1)}) custom-call(bf16[2,256,256]{2,1,0:T(8,128)(2,1)S(1)} %copy-done, bf16[2,256,128]{2,1,0:T(8,128)(2,1)S(1)} %copy-done.1, bf16[2,256,256]{2,1,0:T(8,128)(2,1)S(1)} %copy-done.2, bf16[128,128]{1,0:T(8,128)(2,1)S(1)} %copy-done.4, ...), custom_call_target="tpu_custom_call" | custom-call | flops 1000 | bytes 1000 | tf_op jit(solution)/shard_map/pallas_call | solution.py:456
  39.4 1.7 %collective-permute-start.8 = (bf16[1024,128]{1,0:T(8,128)(2,1)S(1)}, bf16[1024,128]{1,0:T(8,128)(2,1)S(1)}, u32[]{:S(2)}, u32[]{:S(2)}) collective-permute-start(bf16[1024,128]{1,0:T(8,128)(2,1)S(1)} %get-tuple-element.39), channel_id=1, source_target_pairs={{0,1},{1,0},{2,3},{3,2},{4,5},{5,4},{6,7},{7,6},{8,9},{9,8},{10,11... | collective-permute-start | bytes 786440 | tf_op jit(solution)/shard_map/ppermute | solution.py:513
  41.0 2.4 %shard_map.143 = (bf16[1024,128]{1,0:T(8,128)(2,1)S(1)}, bf16[1024,128]{1,0:T(8,128)(2,1)S(1)}) custom-call(bf16[2,256,256]{2,1,0:T(8,128)(2,1)S(1)} %copy-done, bf16[2,256,128]{2,1,0:T(8,128)(2,1)S(1)} %copy-done.1, bf16[2,256,256]{2,1,0:T(8,128)(2,1)S(1)} %copy-done.2, bf16[128,128]{1,0:T(8,128)(2,1)S(1)} %copy-done.4, ...), custom_call_target="tpu_custom_call" | custom-call | flops 1000 | bytes 1000 | tf_op jit(solution)/shard_map/pallas_call | solution.py:456
  43.6 1.0 %collective-permute-start.1 = (bf16[528,128]{1,0:T(8,128)(2,1)S(1)}, bf16[528,128]{1,0:T(8,128)(2,1)S(1)}, u32[]{:S(2)}, u32[]{:S(2)}) collective-permute-start(bf16[528,128]{1,0:T(8,128)(2,1)S(1)} %slice.8), channel_id=1, source_target_pairs={{0,4},{4,8},{8,12},{12,0},{1,5},{5,9},{9,13},{13,1},{2,6},{6,10},{... | collective-permute-start | bytes 405512 | tf_op jit(solution)/shard_map/ppermute | solution.py:513
  44.5 0.5 shard_map.142.refs_4_
  45.1 0.5 shard_map.144.refs_5_
  45.5 5.6 %collective-permute-done.10.refs_5_ = bf16[1536,128]{1,0:T(8,128)(2,1)S(1)} collective-permute-done((bf16[1536,128]{1,0:T(8,128)(2,1)S(1)}, bf16[1536,128]{1,0:T(8,128)(2,1)S(1)}, u32[]{:S(2)}, u32[]{:S(2)}) %collective-permute-start.10) | collective-permute-done | bytes 393248 | tf_op jit(solution)/shard_map/ppermute | solution.py:513
  51.1 2.0 %shard_map.145 = (bf16[768,128]{1,0:T(8,128)(2,1)S(1)}, bf16[768,128]{1,0:T(8,128)(2,1)S(1)}) custom-call(bf16[2,256,256]{2,1,0:T(8,128)(2,1)S(1)} %copy-done, bf16[2,256,128]{2,1,0:T(8,128)(2,1)S(1)} %copy-done.1, bf16[2,256,256]{2,1,0:T(8,128)(2,1)S(1)} %copy-done.2, bf16[128,128]{1,0:T(8,128)(2,1)S(1)} %copy-done.4, ...), custom_call_target="tpu_custom_call" | custom-call | flops 1000 | bytes 1000 | tf_op jit(solution)/shard_map/pallas_call | solution.py:456
  53.6 0.8 %shard_map.146 = (bf16[256,128]{1,0:T(8,128)(2,1)S(1)}, bf16[256,128]{1,0:T(8,128)(2,1)S(1)}) custom-call(bf16[2,256,256]{2,1,0:T(8,128)(2,1)S(1)} %copy-done, bf16[2,256,128]{2,1,0:T(8,128)(2,1)S(1)} %copy-done.1, bf16[2,256,256]{2,1,0:T(8,128)(2,1)S(1)} %copy-done.2, bf16[128,128]{1,0:T(8,128)(2,1)S(1)} %copy-done.4, ...), custom_call_target="tpu_custom_call" | custom-call | flops 1000 | bytes 1000 | tf_op jit(solution)/shard_map/pallas_call | solution.py:456
  54.6 1.1 %collective-permute-done.12.refs_3_ = bf16[256,128]{1,0:T(8,128)(2,1)S(1)} collective-permute-done((bf16[256,128]{1,0:T(8,128)(2,1)S(1)}, bf16[256,128]{1,0:T(8,128)(2,1)S(1)}, u32[]{:S(2)}, u32[]{:S(2)}) %collective-permute-start.12) | collective-permute-done | bytes 65568 | tf_op jit(solution)/shard_map/ppermute | solution.py:513
  55.8 1.1 %shard_map.147 = f32[1,3,2,32]{3,2,1,0:T(2,128)} custom-call(bf16[528,128]{1,0:T(8,128)(2,1)S(1)} %collective-permute-done.1.refs_5_.load, bf16[2,64,64]{2,1,0:T(8,128)(2,1)S(1)} %copy-done.5, bf16[768,128]{1,0:T(8,128)(2,1)S(1)} %get-tuple-element.43.refs_0_, bf16[256,128]{1,0:T(8,128)(2,1)S(1)} %get-tuple-element.44.refs_1_, ...), custom_call_target="tpu_custom_call" | custom-call | flops 1000 | bytes 1000 | tf_op jit(solution)/shard_map/pallas_call | solution.py:500
  (30 shorter events, 1.3 us)
Async XLA Ops:
  0.0 6.0 %copy-start.3 = (bf16[2,128,128]{2,1,0:T(8,128)(2,1)S(1)}, bf16[2,128,128]{2,1,0:T(8,128)(2,1)}, u32[]{:S(2)}) copy-start(bf16[2,128,128]{2,1,0:T(8,128)(2,1)} %constant.19.clone.refs_1_.table.refs_2_) | copy-start | bytes 196612
  2.3 17.9 %collective-permute-start.2 = (bf16[2064,128]{1,0:T(8,128)(2,1)S(1)}, bf16[2064,128]{1,0:T(8,128)(2,1)S(1)}, u32[]{:S(2)}, u32[]{:S(2)}) collective-permute-start(bf16[2064,128]{1,0:T(8,128)(2,1)S(1)} %get-tuple-element.26.refs_4_), channel_id=1, source_target_pairs={{0,4},{4,8},{8,12},{12,0},{1,5},{5,9},{9,13},{13,1},{2,6},{6,10},{... | collective-permute-start | bytes 1585160 | tf_op jit(solution)/shard_map/ppermute | solution.py:513
  6.4 28.0 %copy-start = (bf16[2,256,256]{2,1,0:T(8,128)(2,1)S(1)}, bf16[2,256,256]{2,1,0:T(8,128)(2,1)}, u32[]{:S(2)}) copy-start(bf16[2,256,256]{2,1,0:T(8,128)(2,1)} %constant.22.clone.table) | copy-start | bytes 786436
  6.4 28.0 %copy-start.1 = (bf16[2,256,128]{2,1,0:T(8,128)(2,1)S(1)}, bf16[2,256,128]{2,1,0:T(8,128)(2,1)}, u32[]{:S(2)}) copy-start(bf16[2,256,128]{2,1,0:T(8,128)(2,1)} %constant.23.clone.unpack) | copy-start | bytes 393220
  6.4 28.0 %copy-start.6 = (f32[4]{0:T(128)S(1)}, f32[4]{0:T(128)}, u32[]{:S(2)}) copy-start(f32[4]{0:T(128)} %weight.3) | copy-start | bytes 52
  11.0 25.9 %copy-start.2 = (bf16[2,256,256]{2,1,0:T(8,128)(2,1)S(1)}, bf16[2,256,256]{2,1,0:T(8,128)(2,1)}, u32[]{:S(2)}) copy-start(bf16[2,256,256]{2,1,0:T(8,128)(2,1)} %constant.24.clone.x_inverse) | copy-start | bytes 786436
  11.0 25.9 %copy-start.4 = (bf16[128,128]{1,0:T(8,128)(2,1)S(1)}, bf16[128,128]{1,0:T(8,128)(2,1)}, u32[]{:S(2)}) copy-start(bf16[128,128]{1,0:T(8,128)(2,1)} %constant.25.clone.y_inverse) | copy-start | bytes 98308
  11.0 15.0 %collective-permute-start.4 = (bf16[2064,128]{1,0:T(8,128)(2,1)S(1)}, bf16[2064,128]{1,0:T(8,128)(2,1)S(1)}, u32[]{:S(2)}, u32[]{:S(2)}) collective-permute-start(bf16[2064,128]{1,0:T(8,128)(2,1)S(1)} %get-tuple-element.30.own), channel_id=1, source_target_pairs={{0,2},{2,0},{1,3},{3,1},{4,6},{6,4},{5,7},{7,5},{8,10},{10,8},{9,1... | collective-permute-start | bytes 1585160 | tf_op jit(solution)/shard_map/ppermute | solution.py:513
  11.7 18.1 %collective-permute-start = (bf16[2064,128]{1,0:T(8,128)(2,1)S(1)}, bf16[2064,128]{1,0:T(8,128)(2,1)S(1)}, u32[]{:S(2)}, u32[]{:S(2)}) collective-permute-start(bf16[2064,128]{1,0:T(8,128)(2,1)S(1)} %shard_map.137), channel_id=1, source_target_pairs={{0,5},{1,4},{4,9},{5,8},{8,13},{9,12},{12,1},{13,0},{2,7},{3,6},{6... | collective-permute-start | bytes 1585160 | tf_op jit(solution)/shard_map/ppermute | solution.py:523
  12.2 22.2 %collective-permute-start.5 = (bf16[2064,128]{1,0:T(8,128)(2,1)S(1)}, bf16[2064,128]{1,0:T(8,128)(2,1)S(1)}, u32[]{:S(2)}, u32[]{:S(2)}) collective-permute-start(bf16[2064,128]{1,0:T(8,128)(2,1)S(1)} %get-tuple-element.32), channel_id=1, source_target_pairs={{0,3},{1,2},{2,1},{3,0},{4,7},{5,6},{6,5},{7,4},{8,11},{9,10},{10,... | collective-permute-start | bytes 1585160 | tf_op jit(solution)/shard_map/ppermute | solution.py:523
  20.2 15.4 %collective-permute-start.3 = (bf16[2064,128]{1,0:T(8,128)(2,1)S(1)}, bf16[2064,128]{1,0:T(8,128)(2,1)S(1)}, u32[]{:S(2)}, u32[]{:S(2)}) collective-permute-start(bf16[2064,128]{1,0:T(8,128)(2,1)S(1)} %get-tuple-element.32), channel_id=1, source_target_pairs={{0,1},{1,0},{2,3},{3,2},{4,5},{5,4},{6,7},{7,6},{8,9},{9,8},{10,11... | collective-permute-start | bytes 1585160 | tf_op jit(solution)/shard_map/ppermute | solution.py:513
  26.1 10.9 %collective-permute-start.7 = (bf16[2064,128]{1,0:T(8,128)(2,1)S(1)}, bf16[2064,128]{1,0:T(8,128)(2,1)S(1)}, u32[]{:S(2)}, u32[]{:S(2)}) collective-permute-start(bf16[2064,128]{1,0:T(8,128)(2,1)S(1)} %shard_map.137), channel_id=1, source_target_pairs={{0,1},{1,0},{2,3},{3,2},{4,5},{5,4},{6,7},{7,6},{8,9},{9,8},{10,11... | collective-permute-start | bytes 1585160 | tf_op jit(solution)/shard_map/ppermute | solution.py:513
  26.1 19.5 %collective-permute-start.6 = (bf16[2064,128]{1,0:T(8,128)(2,1)S(1)}, bf16[2064,128]{1,0:T(8,128)(2,1)S(1)}, u32[]{:S(2)}, u32[]{:S(2)}) collective-permute-start(bf16[2064,128]{1,0:T(8,128)(2,1)S(1)} %collective-permute-done.2.refs_4_), channel_id=1, source_target_pairs={{0,4},{4,8},{8,12},{12,0},{1,5},{5,9},{9,13},{13,1},{2,6},{6,10},{... | collective-permute-start | bytes 1585160 | tf_op jit(solution)/shard_map/ppermute | solution.py:513
  29.9 21.2 %collective-permute-start.10 = (bf16[1536,128]{1,0:T(8,128)(2,1)S(1)}, bf16[1536,128]{1,0:T(8,128)(2,1)S(1)}, u32[]{:S(2)}, u32[]{:S(2)}) collective-permute-start(bf16[1536,128]{1,0:T(8,128)(2,1)S(1)} %slice.9), channel_id=1, source_target_pairs={{0,4},{4,8},{8,12},{12,0},{1,5},{5,9},{9,13},{13,1},{2,6},{6,10},{... | collective-permute-start | bytes 1179656 | tf_op jit(solution)/shard_map/ppermute | solution.py:513
  39.4 5.1 %copy-start.5 = (bf16[2,64,64]{2,1,0:T(8,128)(2,1)S(1)}, bf16[2,64,64]{2,1,0:T(8,128)(2,1)}, u32[]{:S(2)}) copy-start(bf16[2,64,64]{2,1,0:T(8,128)(2,1)} %constant.26.clone.table) | copy-start | bytes 49156
  39.4 5.1 %collective-permute-start.8 = (bf16[1024,128]{1,0:T(8,128)(2,1)S(1)}, bf16[1024,128]{1,0:T(8,128)(2,1)S(1)}, u32[]{:S(2)}, u32[]{:S(2)}) collective-permute-start(bf16[1024,128]{1,0:T(8,128)(2,1)S(1)} %get-tuple-element.39), channel_id=1, source_target_pairs={{0,1},{1,0},{2,3},{3,2},{4,5},{5,4},{6,7},{7,6},{8,9},{9,8},{10,11... | collective-permute-start | bytes 786440 | tf_op jit(solution)/shard_map/ppermute | solution.py:513
  43.5 1.6 %collective-permute-start.9 = (bf16[1024,128]{1,0:T(8,128)(2,1)S(1)}, bf16[1024,128]{1,0:T(8,128)(2,1)S(1)}, u32[]{:S(2)}, u32[]{:S(2)}) collective-permute-start(bf16[1024,128]{1,0:T(8,128)(2,1)S(1)} %get-tuple-element.41), channel_id=1, source_target_pairs={{0,1},{1,0},{2,3},{3,2},{4,5},{5,4},{6,7},{7,6},{8,9},{9,8},{10,11... | collective-permute-start | bytes 786440 | tf_op jit(solution)/shard_map/ppermute | solution.py:513
  43.6 10.0 %collective-permute-start.1 = (bf16[528,128]{1,0:T(8,128)(2,1)S(1)}, bf16[528,128]{1,0:T(8,128)(2,1)S(1)}, u32[]{:S(2)}, u32[]{:S(2)}) collective-permute-start(bf16[528,128]{1,0:T(8,128)(2,1)S(1)} %slice.8), channel_id=1, source_target_pairs={{0,4},{4,8},{8,12},{12,0},{1,5},{5,9},{9,13},{13,1},{2,6},{6,10},{... | collective-permute-start | bytes 405512 | tf_op jit(solution)/shard_map/ppermute | solution.py:513
  53.1 2.6 %collective-permute-start.11 = (bf16[768,128]{1,0:T(8,128)(2,1)S(1)}, bf16[768,128]{1,0:T(8,128)(2,1)S(1)}, u32[]{:S(2)}, u32[]{:S(2)}) collective-permute-start(bf16[768,128]{1,0:T(8,128)(2,1)S(1)} %get-tuple-element.45), channel_id=1, source_target_pairs={{0,1},{1,0},{2,3},{3,2},{4,5},{5,4},{6,7},{7,6},{8,9},{9,8},{10,11... | collective-permute-start | bytes 589832 | tf_op jit(solution)/shard_map/ppermute | solution.py:513
  54.4 1.3 %collective-permute-start.12 = (bf16[256,128]{1,0:T(8,128)(2,1)S(1)}, bf16[256,128]{1,0:T(8,128)(2,1)S(1)}, u32[]{:S(2)}, u32[]{:S(2)}) collective-permute-start(bf16[256,128]{1,0:T(8,128)(2,1)S(1)} %get-tuple-element.46), channel_id=1, source_target_pairs={{0,1},{1,0},{2,3},{3,2},{4,5},{5,4},{6,7},{7,6},{8,9},{9,8},{10,11... | collective-permute-start | bytes 196616 | tf_op jit(solution)/shard_map/ppermute | solution.py:513

commit v8 on v7

--- a/solution.py
+++ b/solution.py
@@ -409,13 +409,15 @@
             imag = turned if imag is None else imag + turned
         return jnp.where(is_real, real, imag) + pltpu.roll(jnp.where(is_real, imag, real), cells, 1)
 
+    groups = []
     for start in range(planes[0], planes[1], most):
         per = min(most, planes[1] - start)
         rows = [x_rows(s, cuts, own, others, plane) for plane in range(start, start + per)]
         if start == 0:
             rows[0], high = unpacked_rows(s, own, others, unpack[core])
             rows.append(high)
-        done = x_transform(s, rows, table[core])
+        groups.append((start, per, x_transform(s, rows, table[core])))
+    for start, per, done in groups:
         cross = []
         for k in range(per):
             both = []

time: 57.1 us -> 56.8 us (level)
  starting transfers between devices: 9.34 us -> 12.6 us
  Pallas kernels: 18.7 us -> 16.9 us
  waiting for transfers between devices: 27.2 us -> 25.6 us
    ppermute x11, starting transfers between devices: 7.5 us -> 10.4 us  [passed_along(): lax.ppermute(value, axis, [(source, (source + steps) % count) for source...]
    ppermute x11, waiting for transfers between devices: 19.6 us -> 18.7 us  [passed_along(): lax.ppermute(value, axis, [(source, (source + steps) % count) for source...]
    pallas_call x4, Pallas kernels: 7.67 us -> 6.68 us  [cross_back(): pl.pallas_call(partial(cross_kernel, s, cuts, planes, per), in_specs=[vme...]
    pallas_call x2, Pallas kernels: 6.19 us -> 5.32 us  [sections(): pl.pallas_call(partial(section_kernel, s, pieces, rotated, cuts), in_spec...]
    ppermute x2, waiting for transfers between devices: 7.55 us -> 6.9 us  [passed_across(): return lax.ppermute(value, (axis, 'fft'), pairs)]
  transfers between devices with their start and end apart: 13 -> 13, of which waited for: 8 -> 7; matrix products, arithmetic and copies ran while one was open for 0% -> 0% of each run, Pallas kernels for 27% -> 24%
where the time goes in v8:
time: 56.8 us; the launch traced here: 56.6 us
  waiting for transfers between devices  25.6 us (45%)
  Pallas kernels  16.9 us (30%)
  starting transfers between devices  12.6 us (22%)
  between operations  1.55 us (3%)
    ppermute x11, waiting for transfers between devices, passed_along(): lax.ppermute(value, axis, [(source, (source + steps) % count) for source...  18.7 us
    ppermute x11, starting transfers between devices, passed_along(): lax.ppermute(value, axis, [(source, (source + steps) % count) for source...  10.4 us
    ppermute x2, waiting for transfers between devices, passed_across(): return lax.ppermute(value, (axis, 'fft'), pairs)  6.9 us
    pallas_call x4, Pallas kernels, cross_back(): pl.pallas_call(partial(cross_kernel, s, cuts, planes, per), in_specs=[vme...  6.68 us
    pallas_call x2, Pallas kernels, sections(): pl.pallas_call(partial(section_kernel, s, pieces, rotated, cuts), in_spec...  5.32 us
    pallas_call x2, Pallas kernels, spectrum(): pl.pallas_call(partial(spectrum_kernel, s, cuts, per), in_specs=[pl.Block...  2.48 us
    ppermute x2, starting transfers between devices, passed_across(): return lax.ppermute(value, (axis, 'fft'), pairs)  2.23 us
    pallas_call x3, Pallas kernels, peaks(): pl.pallas_call(partial(peak_kernel, s, len(parts), last), in_specs=[vmem]...  2.04 us
  transfers between devices with their start and end apart: 13, of which 7 were waited for; matrix products, arithmetic and copies ran while one was open for 0% of the time, Pallas kernels for 24%

profile of v8, /device:TPU:0, one launch (start us, length us, event | category | flops | bytes accessed | tf_op | source)
XLA Modules:
  0.0 56.6 jit_solution(2468902160874713179)
XLA Ops:
  0.0 2.3 %shard_map.136 = (bf16[2064,128]{1,0:T(8,128)(2,1)S(1)}, f32[4680,128]{1,0:T(8,128)S(1)}) custom-call(s32[1,4,32,4096]{3,2,1,0:T(8,128)} %occ.1, bf16[2,2,128,128]{3,2,1,0:T(8,128)(2,1)} %constant.18.clone.refs_0_.refs_1_, bf16[2,128,128]{2,1,0:T(8,128)(2,1)} %constant.19.clone.refs_1_.table.refs_2_), custom_call_target="tpu_custom_call" | custom-call | flops 1000 | bytes 1000 | tf_op jit(solution)/shard_map/pallas_call | solution.py:302
  2.3 3.1 %collective-permute-start.2 = (bf16[2064,128]{1,0:T(8,128)(2,1)S(1)}, bf16[2064,128]{1,0:T(8,128)(2,1)S(1)}, u32[]{:S(2)}, u32[]{:S(2)}) collective-permute-start(bf16[2064,128]{1,0:T(8,128)(2,1)S(1)} %get-tuple-element.26.refs_4_), channel_id=1, source_target_pairs={{0,4},{4,8},{8,12},{12,0},{1,5},{5,9},{9,13},{13,1},{2,6},{6,10},{... | collective-permute-start | bytes 1585160 | tf_op jit(solution)/shard_map/ppermute | solution.py:515
  7.1 3.0 %shard_map.138 = (bf16[2064,128]{1,0:T(8,128)(2,1)S(1)}, bf16[2064,128]{1,0:T(8,128)(2,1)S(1)}) custom-call(s32[1,4,32,4096]{3,2,1,0:T(8,128)} %occ.2, s32[1]{0:T(128)S(6)} %copy.15.refs_0_, bf16[2,2,128,128]{3,2,1,0:T(8,128)(2,1)} %constant.18.clone.refs_0_.refs_1_, bf16[2,128,128]{2,1,0:T(8,128)(2,1)} %constant.19.clone.refs_1_.table.refs_2_, ...), custom_call_target="tpu_custom_call" | custom-call | flops 1000 | bytes 1000 | tf_op jit(solution)/shard_map/pallas_call | solution.py:302
  10.2 1.5 %collective-permute-start.4 = (bf16[2064,128]{1,0:T(8,128)(2,1)S(1)}, bf16[2064,128]{1,0:T(8,128)(2,1)S(1)}, u32[]{:S(2)}, u32[]{:S(2)}) collective-permute-start(bf16[2064,128]{1,0:T(8,128)(2,1)S(1)} %get-tuple-element.30.own), channel_id=1, source_target_pairs={{0,2},{2,0},{1,3},{3,1},{4,6},{6,4},{5,7},{7,5},{8,10},{10,8},{9,1... | collective-permute-start | bytes 1585160 | tf_op jit(solution)/shard_map/ppermute | solution.py:515
  11.7 1.3 %collective-permute-start = (bf16[2064,128]{1,0:T(8,128)(2,1)S(1)}, bf16[2064,128]{1,0:T(8,128)(2,1)S(1)}, u32[]{:S(2)}, u32[]{:S(2)}) collective-permute-start(bf16[2064,128]{1,0:T(8,128)(2,1)S(1)} %shard_map.137), channel_id=1, source_target_pairs={{0,5},{1,4},{4,9},{5,8},{8,13},{9,12},{12,1},{13,0},{2,7},{3,6},{6... | collective-permute-start | bytes 1585160 | tf_op jit(solution)/shard_map/ppermute | solution.py:525
  13.0 0.9 %collective-permute-start.5 = (bf16[2064,128]{1,0:T(8,128)(2,1)S(1)}, bf16[2064,128]{1,0:T(8,128)(2,1)S(1)}, u32[]{:S(2)}, u32[]{:S(2)}) collective-permute-start(bf16[2064,128]{1,0:T(8,128)(2,1)S(1)} %get-tuple-element.32), channel_id=1, source_target_pairs={{0,3},{1,2},{2,1},{3,0},{4,7},{5,6},{6,5},{7,4},{8,11},{9,10},{10,... | collective-permute-start | bytes 1585160 | tf_op jit(solution)/shard_map/ppermute | solution.py:525
  14.0 6.3 %collective-permute-done.2.refs_4_ = bf16[2064,128]{1,0:T(8,128)(2,1)S(1)} collective-permute-done((bf16[2064,128]{1,0:T(8,128)(2,1)S(1)}, bf16[2064,128]{1,0:T(8,128)(2,1)S(1)}, u32[]{:S(2)}, u32[]{:S(2)}) %collective-permute-start.2) | collective-permute-done | bytes 528416 | tf_op jit(solution)/shard_map/ppermute | solution.py:515
  20.2 5.0 %collective-permute-done.4.own = bf16[2064,128]{1,0:T(8,128)(2,1)S(1)} collective-permute-done((bf16[2064,128]{1,0:T(8,128)(2,1)S(1)}, bf16[2064,128]{1,0:T(8,128)(2,1)S(1)}, u32[]{:S(2)}, u32[]{:S(2)}) %collective-permute-start.4) | collective-permute-done | bytes 528416 | tf_op jit(solution)/shard_map/ppermute | solution.py:515
  25.2 1.9 %collective-permute-start.6 = (bf16[2064,128]{1,0:T(8,128)(2,1)S(1)}, bf16[2064,128]{1,0:T(8,128)(2,1)S(1)}, u32[]{:S(2)}, u32[]{:S(2)}) collective-permute-start(bf16[2064,128]{1,0:T(8,128)(2,1)S(1)} %collective-permute-done.2.refs_4_), channel_id=1, source_target_pairs={{0,4},{4,8},{8,12},{12,0},{1,5},{5,9},{9,13},{13,1},{2,6},{6,10},{... | collective-permute-start | bytes 1585160 | tf_op jit(solution)/shard_map/ppermute | solution.py:515
  27.1 2.8 %collective-permute-done.refs_5_.load = bf16[2064,128]{1,0:T(8,128)(2,1)S(1)} collective-permute-done((bf16[2064,128]{1,0:T(8,128)(2,1)S(1)}, bf16[2064,128]{1,0:T(8,128)(2,1)S(1)}, u32[]{:S(2)}, u32[]{:S(2)}) %collective-permute-start) | collective-permute-done | bytes 528416 | tf_op jit(solution)/shard_map/ppermute | solution.py:525
  30.0 4.1 %collective-permute-done.5.refs_0_ = bf16[2064,128]{1,0:T(8,128)(2,1)S(1)} collective-permute-done((bf16[2064,128]{1,0:T(8,128)(2,1)S(1)}, bf16[2064,128]{1,0:T(8,128)(2,1)S(1)}, u32[]{:S(2)}, u32[]{:S(2)}) %collective-permute-start.5) | collective-permute-done | bytes 528416 | tf_op jit(solution)/shard_map/ppermute | solution.py:525
  34.1 1.2 %shard_map.140 = (bf16[1024,512]{1,0:T(8,128)(2,1)S(1)}, bf16[64,512]{1,0:T(8,128)(2,1)S(1)}) custom-call(f32[4]{0:T(128)S(1)} %copy-done.6, bf16[2,256,256]{2,1,0:T(8,128)(2,1)S(1)} %copy-done, bf16[2,256,128]{2,1,0:T(8,128)(2,1)S(1)} %copy-done.1, bf16[2064,128]{1,0:T(8,128)(2,1)S(1)} %collective-permute-done.4.own, ...), custom_call_target="tpu_custom_call" | custom-call | flops 1000 | bytes 1000 | tf_op jit(solution)/shard_map/pallas_call | solution.py:381
  35.3 1.2 %shard_map.139 = (bf16[1024,512]{1,0:T(8,128)(2,1)S(1)}, bf16[64,512]{1,0:T(8,128)(2,1)S(1)}) custom-call(f32[4]{0:T(128)S(1)} %copy-done.6, bf16[2,256,256]{2,1,0:T(8,128)(2,1)S(1)} %copy-done, bf16[2,256,128]{2,1,0:T(8,128)(2,1)S(1)} %copy-done.1, bf16[2064,128]{1,0:T(8,128)(2,1)S(1)} %get-tuple-element.30.own, ...), custom_call_target="tpu_custom_call" | custom-call | flops 1000 | bytes 1000 | tf_op jit(solution)/shard_map/pallas_call | solution.py:381
  36.6 2.1 %shard_map.141 = (bf16[1024,128]{1,0:T(8,128)(2,1)S(1)}, bf16[1024,128]{1,0:T(8,128)(2,1)S(1)}) custom-call(bf16[2,256,256]{2,1,0:T(8,128)(2,1)S(1)} %copy-done, bf16[2,256,128]{2,1,0:T(8,128)(2,1)S(1)} %copy-done.1, bf16[2,256,256]{2,1,0:T(8,128)(2,1)S(1)} %copy-done.2, bf16[128,128]{1,0:T(8,128)(2,1)S(1)} %copy-done.4, ...), custom_call_target="tpu_custom_call" | custom-call | flops 1000 | bytes 1000 | tf_op jit(solution)/shard_map/pallas_call | solution.py:458
  38.7 1.2 %collective-permute-start.8 = (bf16[1024,128]{1,0:T(8,128)(2,1)S(1)}, bf16[1024,128]{1,0:T(8,128)(2,1)S(1)}, u32[]{:S(2)}, u32[]{:S(2)}) collective-permute-start(bf16[1024,128]{1,0:T(8,128)(2,1)S(1)} %get-tuple-element.39), channel_id=1, source_target_pairs={{0,1},{1,0},{2,3},{3,2},{4,5},{5,4},{6,7},{7,6},{8,9},{9,8},{10,11... | collective-permute-start | bytes 786440 | tf_op jit(solution)/shard_map/ppermute | solution.py:515
  39.8 2.1 %shard_map.143 = (bf16[1024,128]{1,0:T(8,128)(2,1)S(1)}, bf16[1024,128]{1,0:T(8,128)(2,1)S(1)}) custom-call(bf16[2,256,256]{2,1,0:T(8,128)(2,1)S(1)} %copy-done, bf16[2,256,128]{2,1,0:T(8,128)(2,1)S(1)} %copy-done.1, bf16[2,256,256]{2,1,0:T(8,128)(2,1)S(1)} %copy-done.2, bf16[128,128]{1,0:T(8,128)(2,1)S(1)} %copy-done.4, ...), custom_call_target="tpu_custom_call" | custom-call | flops 1000 | bytes 1000 | tf_op jit(solution)/shard_map/pallas_call | solution.py:458
  42.0 2.4 %collective-permute-start.1 = (bf16[528,128]{1,0:T(8,128)(2,1)S(1)}, bf16[528,128]{1,0:T(8,128)(2,1)S(1)}, u32[]{:S(2)}, u32[]{:S(2)}) collective-permute-start(bf16[528,128]{1,0:T(8,128)(2,1)S(1)} %slice.8), channel_id=1, source_target_pairs={{0,4},{4,8},{8,12},{12,0},{1,5},{5,9},{9,13},{13,1},{2,6},{6,10},{... | collective-permute-start | bytes 405512 | tf_op jit(solution)/shard_map/ppermute | solution.py:515
  44.4 0.5 shard_map.142.refs_4_
  45.4 5.6 %collective-permute-done.10.refs_5_ = bf16[1536,128]{1,0:T(8,128)(2,1)S(1)} collective-permute-done((bf16[1536,128]{1,0:T(8,128)(2,1)S(1)}, bf16[1536,128]{1,0:T(8,128)(2,1)S(1)}, u32[]{:S(2)}, u32[]{:S(2)}) %collective-permute-start.10) | collective-permute-done | bytes 393248 | tf_op jit(solution)/shard_map/ppermute | solution.py:515
  51.0 1.7 %shard_map.145 = (bf16[768,128]{1,0:T(8,128)(2,1)S(1)}, bf16[768,128]{1,0:T(8,128)(2,1)S(1)}) custom-call(bf16[2,256,256]{2,1,0:T(8,128)(2,1)S(1)} %copy-done, bf16[2,256,128]{2,1,0:T(8,128)(2,1)S(1)} %copy-done.1, bf16[2,256,256]{2,1,0:T(8,128)(2,1)S(1)} %copy-done.2, bf16[128,128]{1,0:T(8,128)(2,1)S(1)} %copy-done.4, ...), custom_call_target="tpu_custom_call" | custom-call | flops 1000 | bytes 1000 | tf_op jit(solution)/shard_map/pallas_call | solution.py:458
  52.8 0.5 collective-permute-done.1.refs_5_.load
  53.4 0.8 %shard_map.146 = (bf16[256,128]{1,0:T(8,128)(2,1)S(1)}, bf16[256,128]{1,0:T(8,128)(2,1)S(1)}) custom-call(bf16[2,256,256]{2,1,0:T(8,128)(2,1)S(1)} %copy-done, bf16[2,256,128]{2,1,0:T(8,128)(2,1)S(1)} %copy-done.1, bf16[2,256,256]{2,1,0:T(8,128)(2,1)S(1)} %copy-done.2, bf16[128,128]{1,0:T(8,128)(2,1)S(1)} %copy-done.4, ...), custom_call_target="tpu_custom_call" | custom-call | flops 1000 | bytes 1000 | tf_op jit(solution)/shard_map/pallas_call | solution.py:458
  54.3 1.2 %collective-permute-done.12.refs_3_ = bf16[256,128]{1,0:T(8,128)(2,1)S(1)} collective-permute-done((bf16[256,128]{1,0:T(8,128)(2,1)S(1)}, bf16[256,128]{1,0:T(8,128)(2,1)S(1)}, u32[]{:S(2)}, u32[]{:S(2)}) %collective-permute-start.12) | collective-permute-done | bytes 65568 | tf_op jit(solution)/shard_map/ppermute | solution.py:515
  55.5 1.1 %shard_map.147 = f32[1,3,2,32]{3,2,1,0:T(2,128)} custom-call(bf16[528,128]{1,0:T(8,128)(2,1)S(1)} %collective-permute-done.1.refs_5_.load, bf16[2,64,64]{2,1,0:T(8,128)(2,1)S(1)} %copy-done.5, bf16[768,128]{1,0:T(8,128)(2,1)S(1)} %get-tuple-element.43.refs_0_, bf16[256,128]{1,0:T(8,128)(2,1)S(1)} %get-tuple-element.44.refs_1_, ...), custom_call_target="tpu_custom_call" | custom-call | flops 1000 | bytes 1000 | tf_op jit(solution)/shard_map/pallas_call | solution.py:502
  (30 shorter events, 1.2 us)
Async XLA Ops:
  0.0 6.0 %copy-start.3 = (bf16[2,128,128]{2,1,0:T(8,128)(2,1)S(1)}, bf16[2,128,128]{2,1,0:T(8,128)(2,1)}, u32[]{:S(2)}) copy-start(bf16[2,128,128]{2,1,0:T(8,128)(2,1)} %constant.19.clone.refs_1_.table.refs_2_) | copy-start | bytes 196612
  2.3 17.9 %collective-permute-start.2 = (bf16[2064,128]{1,0:T(8,128)(2,1)S(1)}, bf16[2064,128]{1,0:T(8,128)(2,1)S(1)}, u32[]{:S(2)}, u32[]{:S(2)}) collective-permute-start(bf16[2064,128]{1,0:T(8,128)(2,1)S(1)} %get-tuple-element.26.refs_4_), channel_id=1, source_target_pairs={{0,4},{4,8},{8,12},{12,0},{1,5},{5,9},{9,13},{13,1},{2,6},{6,10},{... | collective-permute-start | bytes 1585160 | tf_op jit(solution)/shard_map/ppermute | solution.py:515
  6.4 27.7 %copy-start = (bf16[2,256,256]{2,1,0:T(8,128)(2,1)S(1)}, bf16[2,256,256]{2,1,0:T(8,128)(2,1)}, u32[]{:S(2)}) copy-start(bf16[2,256,256]{2,1,0:T(8,128)(2,1)} %constant.22.clone.table) | copy-start | bytes 786436
  6.4 27.7 %copy-start.1 = (bf16[2,256,128]{2,1,0:T(8,128)(2,1)S(1)}, bf16[2,256,128]{2,1,0:T(8,128)(2,1)}, u32[]{:S(2)}) copy-start(bf16[2,256,128]{2,1,0:T(8,128)(2,1)} %constant.23.clone.unpack) | copy-start | bytes 393220
  6.4 27.7 %copy-start.6 = (f32[4]{0:T(128)S(1)}, f32[4]{0:T(128)}, u32[]{:S(2)}) copy-start(f32[4]{0:T(128)} %weight.3) | copy-start | bytes 52
  10.2 26.4 %copy-start.2 = (bf16[2,256,256]{2,1,0:T(8,128)(2,1)S(1)}, bf16[2,256,256]{2,1,0:T(8,128)(2,1)}, u32[]{:S(2)}) copy-start(bf16[2,256,256]{2,1,0:T(8,128)(2,1)} %constant.24.clone.x_inverse) | copy-start | bytes 786436
  10.2 26.4 %copy-start.4 = (bf16[128,128]{1,0:T(8,128)(2,1)S(1)}, bf16[128,128]{1,0:T(8,128)(2,1)}, u32[]{:S(2)}) copy-start(bf16[128,128]{1,0:T(8,128)(2,1)} %constant.25.clone.y_inverse) | copy-start | bytes 98308
  10.2 15.0 %collective-permute-start.4 = (bf16[2064,128]{1,0:T(8,128)(2,1)S(1)}, bf16[2064,128]{1,0:T(8,128)(2,1)S(1)}, u32[]{:S(2)}, u32[]{:S(2)}) collective-permute-start(bf16[2064,128]{1,0:T(8,128)(2,1)S(1)} %get-tuple-element.30.own), channel_id=1, source_target_pairs={{0,2},{2,0},{1,3},{3,1},{4,6},{6,4},{5,7},{7,5},{8,10},{10,8},{9,1... | collective-permute-start | bytes 1585160 | tf_op jit(solution)/shard_map/ppermute | solution.py:515
  11.7 18.1 %collective-permute-start = (bf16[2064,128]{1,0:T(8,128)(2,1)S(1)}, bf16[2064,128]{1,0:T(8,128)(2,1)S(1)}, u32[]{:S(2)}, u32[]{:S(2)}) collective-permute-start(bf16[2064,128]{1,0:T(8,128)(2,1)S(1)} %shard_map.137), channel_id=1, source_target_pairs={{0,5},{1,4},{4,9},{5,8},{8,13},{9,12},{12,1},{13,0},{2,7},{3,6},{6... | collective-permute-start | bytes 1585160 | tf_op jit(solution)/shard_map/ppermute | solution.py:525
  13.0 21.0 %collective-permute-start.5 = (bf16[2064,128]{1,0:T(8,128)(2,1)S(1)}, bf16[2064,128]{1,0:T(8,128)(2,1)S(1)}, u32[]{:S(2)}, u32[]{:S(2)}) collective-permute-start(bf16[2064,128]{1,0:T(8,128)(2,1)S(1)} %get-tuple-element.32), channel_id=1, source_target_pairs={{0,3},{1,2},{2,1},{3,0},{4,7},{5,6},{6,5},{7,4},{8,11},{9,10},{10,... | collective-permute-start | bytes 1585160 | tf_op jit(solution)/shard_map/ppermute | solution.py:525
  20.2 15.1 %collective-permute-start.3 = (bf16[2064,128]{1,0:T(8,128)(2,1)S(1)}, bf16[2064,128]{1,0:T(8,128)(2,1)S(1)}, u32[]{:S(2)}, u32[]{:S(2)}) collective-permute-start(bf16[2064,128]{1,0:T(8,128)(2,1)S(1)} %get-tuple-element.32), channel_id=1, source_target_pairs={{0,1},{1,0},{2,3},{3,2},{4,5},{5,4},{6,7},{7,6},{8,9},{9,8},{10,11... | collective-permute-start | bytes 1585160 | tf_op jit(solution)/shard_map/ppermute | solution.py:515
  25.2 11.4 %collective-permute-start.7 = (bf16[2064,128]{1,0:T(8,128)(2,1)S(1)}, bf16[2064,128]{1,0:T(8,128)(2,1)S(1)}, u32[]{:S(2)}, u32[]{:S(2)}) collective-permute-start(bf16[2064,128]{1,0:T(8,128)(2,1)S(1)} %shard_map.137), channel_id=1, source_target_pairs={{0,1},{1,0},{2,3},{3,2},{4,5},{5,4},{6,7},{7,6},{8,9},{9,8},{10,11... | collective-permute-start | bytes 1585160 | tf_op jit(solution)/shard_map/ppermute | solution.py:515
  25.2 20.2 %collective-permute-start.6 = (bf16[2064,128]{1,0:T(8,128)(2,1)S(1)}, bf16[2064,128]{1,0:T(8,128)(2,1)S(1)}, u32[]{:S(2)}, u32[]{:S(2)}) collective-permute-start(bf16[2064,128]{1,0:T(8,128)(2,1)S(1)} %collective-permute-done.2.refs_4_), channel_id=1, source_target_pairs={{0,4},{4,8},{8,12},{12,0},{1,5},{5,9},{9,13},{13,1},{2,6},{6,10},{... | collective-permute-start | bytes 1585160 | tf_op jit(solution)/shard_map/ppermute | solution.py:515
  29.9 21.1 %collective-permute-start.10 = (bf16[1536,128]{1,0:T(8,128)(2,1)S(1)}, bf16[1536,128]{1,0:T(8,128)(2,1)S(1)}, u32[]{:S(2)}, u32[]{:S(2)}) collective-permute-start(bf16[1536,128]{1,0:T(8,128)(2,1)S(1)} %slice.9), channel_id=1, source_target_pairs={{0,4},{4,8},{8,12},{12,0},{1,5},{5,9},{9,13},{13,1},{2,6},{6,10},{... | collective-permute-start | bytes 1179656 | tf_op jit(solution)/shard_map/ppermute | solution.py:515
  38.7 5.8 %copy-start.5 = (bf16[2,64,64]{2,1,0:T(8,128)(2,1)S(1)}, bf16[2,64,64]{2,1,0:T(8,128)(2,1)}, u32[]{:S(2)}) copy-start(bf16[2,64,64]{2,1,0:T(8,128)(2,1)} %constant.26.clone.table) | copy-start | bytes 49156
  38.7 5.8 %collective-permute-start.8 = (bf16[1024,128]{1,0:T(8,128)(2,1)S(1)}, bf16[1024,128]{1,0:T(8,128)(2,1)S(1)}, u32[]{:S(2)}, u32[]{:S(2)}) collective-permute-start(bf16[1024,128]{1,0:T(8,128)(2,1)S(1)} %get-tuple-element.39), channel_id=1, source_target_pairs={{0,1},{1,0},{2,3},{3,2},{4,5},{5,4},{6,7},{7,6},{8,9},{9,8},{10,11... | collective-permute-start | bytes 786440 | tf_op jit(solution)/shard_map/ppermute | solution.py:515
  41.9 3.0 %collective-permute-start.9 = (bf16[1024,128]{1,0:T(8,128)(2,1)S(1)}, bf16[1024,128]{1,0:T(8,128)(2,1)S(1)}, u32[]{:S(2)}, u32[]{:S(2)}) collective-permute-start(bf16[1024,128]{1,0:T(8,128)(2,1)S(1)} %get-tuple-element.41), channel_id=1, source_target_pairs={{0,1},{1,0},{2,3},{3,2},{4,5},{5,4},{6,7},{7,6},{8,9},{9,8},{10,11... | collective-permute-start | bytes 786440 | tf_op jit(solution)/shard_map/ppermute | solution.py:515
  42.0 11.3 %collective-permute-start.1 = (bf16[528,128]{1,0:T(8,128)(2,1)S(1)}, bf16[528,128]{1,0:T(8,128)(2,1)S(1)}, u32[]{:S(2)}, u32[]{:S(2)}) collective-permute-start(bf16[528,128]{1,0:T(8,128)(2,1)S(1)} %slice.8), channel_id=1, source_target_pairs={{0,4},{4,8},{8,12},{12,0},{1,5},{5,9},{9,13},{13,1},{2,6},{6,10},{... | collective-permute-start | bytes 405512 | tf_op jit(solution)/shard_map/ppermute | solution.py:515
  52.8 2.8 %collective-permute-start.11 = (bf16[768,128]{1,0:T(8,128)(2,1)S(1)}, bf16[768,128]{1,0:T(8,128)(2,1)S(1)}, u32[]{:S(2)}, u32[]{:S(2)}) collective-permute-start(bf16[768,128]{1,0:T(8,128)(2,1)S(1)} %get-tuple-element.45), channel_id=1, source_target_pairs={{0,1},{1,0},{2,3},{3,2},{4,5},{5,4},{6,7},{7,6},{8,9},{9,8},{10,11... | collective-permute-start | bytes 589832 | tf_op jit(solution)/shard_map/ppermute | solution.py:515
  54.2 1.3 %collective-permute-start.12 = (bf16[256,128]{1,0:T(8,128)(2,1)S(1)}, bf16[256,128]{1,0:T(8,128)(2,1)S(1)}, u32[]{:S(2)}, u32[]{:S(2)}) collective-permute-start(bf16[256,128]{1,0:T(8,128)(2,1)S(1)} %get-tuple-element.46), channel_id=1, source_target_pairs={{0,1},{1,0},{2,3},{3,2},{4,5},{5,4},{6,7},{7,6},{8,9},{9,8},{10,11... | collective-permute-start | bytes 196616 | tf_op jit(solution)/shard_map/ppermute | solution.py:515
